TPU v7x, 32 devices: a whole 2x2x4 slice. The times are simulated.
32 devices in a mesh: dp: 4 (over z), blk: 8 (over y, x, core).
Axes of the slice: x: 2, y: 2, z: 4, core: 2. Of those that a mesh axis runs over, the one named last changes fastest.
Arguments:
- noise: bfloat16 [640, 8192], P('blk', 'dp'), may hold values from -1 to 1
- buffer: bfloat16 [640, 32768], P('blk', 'dp'), may hold values from -6 to 6
- reinit: int32 [128], P('dp'), may hold values 0 or 1
- slots: int32 [128], P('dp'), may hold values from 0 to 127
- kernel_one: bfloat16 [9, 640, 640], P(None, 'blk'), may hold values from -0.078125 to 0.078125
- bias_one: bfloat16 [640], P('blk'), may hold values from -3 to 3
- kernel_two: bfloat16 [9, 640, 640], P(None, 'blk'), may hold values from -0.078125 to 0.078125
- bias_two: bfloat16 [640], P('blk'), may hold values from -3 to 3
- cotangent: bfloat16 [640, 8192], P('blk', 'dp'), may hold values from -6 to 6
Outputs:
- output: bfloat16 [640, 8192], P('blk', 'dp')
- grad_field: float32 [640, 8192], P('blk', 'dp')
- grad_kernel_one: float32 [9, 640, 640], P(None, 'blk')
- grad_bias_one: float32 [640], P('blk')
- grad_kernel_two: float32 [9, 640, 640], P(None, 'blk')
- grad_bias_two: float32 [640], P('blk')
All inputs are finite; a program needn't handle non-finite values. No bound on the sum of `reinit` on one device may be relied on, other than what follows from the above.
Results may differ from a plain program's by a relative error of at most 0.0055.
Values may be sent and summed in bfloat16 or wider, within the bound.
No kernel may reach another device: no remote copies, remote signals or barrier semaphores. Data moves between devices by JAX's collectives and lax.ppermute only.
A program may use at most 192 MiB of HBM per device.

v0:
```python
import jax
import jax.numpy as jnp
from jax import lax
from jax.sharding import PartitionSpec as P

offsets = [(row, col) for row in (-1, 0, 1) for col in (-1, 0, 1)]


def shift_tap(field, row, col):
    depth = field.shape[0]
    grid = field.reshape(depth, -1, 8, 8)
    grid = jnp.pad(grid, ((0, 0), (0, 0), (1, 1), (1, 1)))
    grid = grid[:, :, 1 + row : 9 + row, 1 + col : 9 + col]
    return grid.reshape(depth, -1)


def silu_slope(value):
    sigma = jax.nn.sigmoid(value)
    return sigma * (1.0 + value * (1.0 - sigma))


def add_conv(total, piece, kernel):
    for number, (row, col) in enumerate(offsets):
        total = total + jnp.dot(
            kernel[number], shift_tap(piece, row, col), preferred_element_type=jnp.float32
        )
    return total


def add_grad(piece, upstream):
    parts = [
        lax.dot_general(
            upstream,
            shift_tap(piece, row, col),
            (((1,), (1,)), ((), ())),
            preferred_element_type=jnp.float32,
        )
        for row, col in offsets
    ]
    return jnp.stack(parts, 0)


def back_shifts(upstream):
    return jnp.stack([shift_tap(upstream, -row, -col) for row, col in offsets], 0)


def spread_rows(kernel, shifted):
    return lax.dot_general(
        kernel, shifted, (((0, 1), (0, 1)), ((), ())), preferred_element_type=jnp.float32
    )


def local(noise, buffer, reinit, slots, kernel_one, bias_one, kernel_two, bias_two, cotangent):
    depth = noise.shape[0]
    images = reinit.shape[0]
    pixels = images * 64
    stored = buffer.reshape(depth, -1, 64)[:, slots, :]
    fresh = noise.reshape(depth, images, 64)
    field = (
        jnp.where(reinit[None, :, None] == 1, fresh, stored)
        .reshape(depth, pixels)
        .astype(jnp.float32)
    )
    act_zero = jax.nn.silu(field).astype(jnp.bfloat16)
    empty = jnp.zeros((depth, pixels), jnp.float32)
    whole_zero = lax.all_gather(act_zero, "blk", axis=0, tiled=True)
    pre_one = add_conv(empty, whole_zero, kernel_one)
    pre_one = pre_one + bias_one.astype(jnp.float32)[:, None]
    act_one = jax.nn.silu(pre_one).astype(jnp.bfloat16)
    whole_one = lax.all_gather(act_one, "blk", axis=0, tiled=True)
    pre_two = add_conv(empty, whole_one, kernel_two)
    output = (field + pre_two + bias_two.astype(jnp.float32)[:, None]).astype(jnp.bfloat16)
    bias_grad_two = jnp.sum(cotangent.astype(jnp.float32), axis=1)
    kernel_grad_two = add_grad(whole_one, cotangent)
    shifted_two = back_shifts(cotangent)
    grad_act_one = lax.psum_scatter(
        spread_rows(kernel_two, shifted_two), "blk", scatter_dimension=0, tiled=True
    )
    grad_pre_one = (grad_act_one * silu_slope(pre_one)).astype(jnp.bfloat16)
    bias_grad_one = jnp.sum(grad_pre_one.astype(jnp.float32), axis=1)
    kernel_grad_one = add_grad(whole_zero, grad_pre_one)
    shifted_one = back_shifts(grad_pre_one)
    grad_act_zero = lax.psum_scatter(
        spread_rows(kernel_one, shifted_one).astype(jnp.bfloat16),
        "blk",
        scatter_dimension=0,
        tiled=True,
    ).astype(jnp.float32)
    grad_field = cotangent.astype(jnp.float32) + grad_act_zero * silu_slope(field)
    summed = lax.psum((kernel_grad_one, bias_grad_one, kernel_grad_two, bias_grad_two), "dp")
    return (output, grad_field, summed[0], summed[1], summed[2], summed[3])


def solution(mesh):
    return jax.shard_map(
        local,
        mesh=mesh,
        in_specs=(
            P("blk", "dp"),
            P("blk", "dp"),
            P("dp"),
            P("dp"),
            P(None, "blk", None),
            P("blk"),
            P(None, "blk", None),
            P("blk"),
            P("blk", "dp"),
        ),
        out_specs=(
            P("blk", "dp"),
            P("blk", "dp"),
            P(None, "blk", None),
            P("blk"),
            P(None, "blk", None),
            P("blk"),
        ),
        check_vma=False,
    )
```

profile of v0, /device:TPU:0, one launch (start us, length us, event | category | flops | bytes accessed | tf_op | source)
XLA Modules:
  0.0 355.2 jit_solution(1953250491575184797)
XLA Ops:
  8.7 3.1 copy.43
  14.8 5.5 %pad_slice_fusion.24 = (bf16[80,32,8,8]{0,3,2,1:T(8,128)(2,1)}, bf16[80,32,8,8]{0,3,2,1:T(8,128)(2,1)}, bf16[80,32,8,8]{0,3,2,1:T(8,128)(2,1)S(1)}, bf16[80,32,8...) fusion(bf16[80,32,8,8]{0,3,2,1:T(8,128)(2,1)} %bitcast.320), kind=kLoop, calls=%fused_computation.27 | loop fusion | bytes 2949120 | tf_op jit(solution)/shard_map/slice | solution.py:13
  22.3 2.0 copy.23
  28.5 4.7 %convolution_bitcast_fusion = f32[640,2048]{1,0:T(8,128)} fusion(bf16[9,80,2048]{2,1,0:T(8,128)(2,1)S(1)} %constant_dynamic-update-slice_fusion, bf16[9,80,640]{2,1,0:T(8,128)(2,1)S(1)} %copy-done.39), kind=kOutput, calls=%fused_computation.18 | convolution fusion | flops 1887436800 | bytes 9113600 | tf_op jit(solution)/shard_map/dot_general | solution.py:48
  33.9 12.8 %all-gather.3.cloned.1.call-done = bf16[640,2048]{1,0:T(8,128)(2,1)} async-done(((bf16[80,2048]{1,0:T(8,128)(2,1)}), bf16[640,2048]{1,0:T(8,128)(2,1)}) %all-gather.3.cloned.1.call-update) | async-done | bytes 2621456 | tf_op jit(solution)/shard_map/all_gather | solution.py:66
  46.7 4.4 %copy.19 = bf16[640,2048]{0,1:T(8,128)(2,1)} copy(bf16[640,2048]{1,0:T(8,128)(2,1)} %all-gather.3.cloned.1.call-done) | data formatting | bytes 5242880 | tf_op jit(solution)/shard_map/all_gather | solution.py:66
  51.1 13.6 %pad_slice_fusion.8 = (bf16[640,32,8,8]{0,3,2,1:T(8,128)(2,1)}, bf16[640,32,8,8]{0,3,2,1:T(8,128)(2,1)}, bf16[640,32,8,8]{0,3,2,1:T(8,128)(2,1)}, bf16[640,32,8,...) fusion(bf16[640,32,8,8]{0,3,2,1:T(8,128)(2,1)} %bitcast.300), kind=kLoop, calls=%fused_computation.9 | loop fusion | bytes 23592960 | tf_op jit(solution)/shard_map/slice | solution.py:13
  64.7 2.1 fusion.50
  77.5 29.2 %reduce-scatter.3.cloned.1.call-done = f32[80,2048]{1,0:T(8,128)} async-done(((f32[640,2048]{1,0:T(8,128)}), f32[80,2048]{1,0:T(8,128)}) %reduce-scatter.3.cloned.1.call-update) | async-done | bytes 655376 | tf_op jit(solution)/shard_map/reduce_scatter | solution.py:76
  106.8 3.9 %convert_reduce_fusion.1 = (f32[80]{0:T(128)S(1)}, bf16[80,2048]{1,0:T(8,128)(2,1)S(1)}, bf16[80,2048]{1,0:T(8,128)(2,1)}) fusion(f32[80,2048]{1,0:T(8,128)} %reduce-scatter.3.cloned.1.call-done, f32[80]{0:T(128)S(1)} %convert_element_type.95, f32[2048,80]{0,1:T(8,128)} %convolution_add_fusion.10, bf16[640,2048]{0,1:T(8,128)(2,1)} %bitcast.298, ...), kind=kOutput, calls=%fused_computation.106 | convolution fusion | flops 212172720 | bytes 4690560 | tf_op jit(solution)/shard_map/dot_general | solution.py:24
  112.0 5.8 %pad_slice_fusion.16 = (bf16[80,32,8,8]{0,3,2,1:T(8,128)(2,1)}, bf16[80,32,8,8]{0,3,2,1:T(8,128)(2,1)}, bf16[80,32,8,8]{0,3,2,1:T(8,128)(2,1)}, bf16[80,32,8,8]{...) fusion(bf16[80,32,8,8]{0,3,2,1:T(8,128)(2,1)} %bitcast.321), kind=kLoop, calls=%fused_computation.19 | loop fusion | bytes 2949120 | tf_op jit(solution)/shard_map/slice | solution.py:13
  117.8 2.0 copy.33
  125.2 2.0 copy.39
  131.1 2.0 copy.36
  135.0 2.0 copy.38
  152.6 5.7 %fusion = bf16[640,2048]{1,0:T(8,128)(2,1)} fusion(bf16[9,80,2048]{2,1,0:T(8,128)(2,1)} %constant_dynamic-update-slice_fusion.8, bf16[9,80,640]{2,1,0:T(8,128)(2,1)S(1)} %copy-done.42), kind=kOutput, calls=%fused_computation.35 | convolution fusion | flops 1888747520 | bytes 6492160 | tf_op jit(solution)/shard_map/dot_general | solution.py:48
  163.1 4.6 %copy.20 = bf16[640,2048]{0,1:T(8,128)(2,1)} copy(bf16[640,2048]{1,0:T(8,128)(2,1)} %all-gather.5.cloned.1.call-done) | data formatting | bytes 5242880 | tf_op jit(solution)/shard_map/all_gather | solution.py:70
  167.7 12.7 %pad_slice_fusion = (bf16[640,32,8,8]{0,3,2,1:T(8,128)(2,1)S(1)}, bf16[640,32,8,8]{0,3,2,1:T(8,128)(2,1)}, bf16[640,32,8,8]{0,3,2,1:T(8,128)(2,1)}, bf16[640,32,...) fusion(bf16[640,32,8,8]{0,3,2,1:T(8,128)(2,1)} %bitcast.301), kind=kLoop, calls=%fused_computation.1 | loop fusion | bytes 23592960 | tf_op jit(solution)/shard_map/slice | solution.py:13
  181.7 2.5 copy-done.29
  195.8 6.5 %reduce-scatter.5.cloned.1.call-done = bf16[80,2048]{1,0:T(8,128)(2,1)} async-done(((bf16[640,2048]{1,0:T(8,128)(2,1)}), bf16[80,2048]{1,0:T(8,128)(2,1)}) %reduce-scatter.5.cloned.1.call-update) | async-done | bytes 327696 | tf_op jit(solution)/shard_map/reduce_scatter | solution.py:83
  202.3 2.2 convert_reduce_fusion
  204.5 12.3 %all-reduce.4 = (f32[80]{0:T(128)}, f32[80]{0:T(128)}) all-reduce(f32[80]{0:T(128)S(1)} %get-tuple-element.10, f32[80]{0:T(128)S(1)} %get-tuple-element.47), channel_id=1, replica_groups=mesh['dp'=4,'blk'=8] {'dp'}, use_global_device_ids=true, to_apply=%region_4.5 | all-reduce | flops 160 | bytes 1280 | tf_op jit(solution)/shard_map/psum | solution.py:90
  232.8 111.7 %all-reduce.8.cloned.1.call-done = (f32[9,80,640]{2,1,0:T(8,128)}, f32[9,80,640]{2,1,0:T(8,128)}) async-done(((f32[9,80,640]{2,1,0:T(8,128)}, f32[9,80,640]{2,1,0:T(8,128)}), (f32[9,80,640]{2,1,0:T(8,128)}, f32[9,80,640]{2,1,0:T(8,128)})) %all-reduce.8.cloned.1.call-update) | async-done | bytes 3686416 | tf_op jit(solution)/shard_map/psum | solution.py:90
  344.5 3.0 copy.81
  (178 shorter events, 84.8 us)
Async XLA Ops:
  7.2 39.6 %all-gather.3.cloned.1.call-start = ((), (), s32[]{:S(2)}) async-start(), calls=%async_computation.2 | async-start | bytes 2949120 | tf_op jit(solution)/shard_map/all_gather | solution.py:66
  8.7 4.0 %copy-start.43 = (bf16[80,2048]{1,0:T(8,128)(2,1)S(1)}, bf16[80,2048]{1,0:T(8,128)(2,1)}, u32[]{:S(2)}) copy-start(bf16[80,2048]{1,0:T(8,128)(2,1)} %param.9) | copy-start | bytes 983044
  13.8 93.0 %reduce-scatter.3.cloned.1.call-start = ((), (), s32[]{:S(2)}) async-start(), calls=%async_computation.4 | async-start | bytes 5898240 | tf_op jit(solution)/shard_map/reduce_scatter | solution.py:76
  33.3 129.9 %all-gather.5.cloned.1.call-start = ((), (), s32[]{:S(2)}) async-start(), calls=%async_computation.3 | async-start | bytes 2949120 | tf_op jit(solution)/shard_map/all_gather | solution.py:70
  64.7 9.2 %copy-start.9 = (bf16[640,32,8,8]{0,3,2,1:T(8,128)(2,1)}, bf16[640,32,8,8]{0,3,2,1:T(8,128)(2,1)S(1)}, u32[]{:S(2)}) copy-start(bf16[640,32,8,8]{0,3,2,1:T(8,128)(2,1)S(1)} %get-tuple-element.26) | copy-start | bytes 7864324
  64.7 10.1 %copy-start.7 = (bf16[640,32,8,8]{0,3,2,1:T(8,128)(2,1)}, bf16[640,32,8,8]{0,3,2,1:T(8,128)(2,1)S(1)}, u32[]{:S(2)}) copy-start(bf16[640,32,8,8]{0,3,2,1:T(8,128)(2,1)S(1)} %get-tuple-element.27) | copy-start | bytes 7864324
  64.7 11.0 %copy-start.5 = (bf16[640,32,8,8]{0,3,2,1:T(8,128)(2,1)}, bf16[640,32,8,8]{0,3,2,1:T(8,128)(2,1)S(1)}, u32[]{:S(2)}) copy-start(bf16[640,32,8,8]{0,3,2,1:T(8,128)(2,1)S(1)} %get-tuple-element.28) | copy-start | bytes 7864324
  64.7 3.9 %copy-start.15 = (bf16[640,32,8,8]{0,3,2,1:T(8,128)(2,1)S(1)}, bf16[640,32,8,8]{0,3,2,1:T(8,128)(2,1)}, u32[]{:S(2)}) copy-start(bf16[640,32,8,8]{0,3,2,1:T(8,128)(2,1)} %get-tuple-element.23) | copy-start | bytes 7864324
  64.7 4.8 %copy-start.41 = (bf16[9,80,640]{2,1,0:T(8,128)(2,1)S(1)}, bf16[9,80,640]{2,1,0:T(8,128)(2,1)}, u32[]{:S(2)}) copy-start(bf16[9,80,640]{2,1,0:T(8,128)(2,1)} %param.13) | copy-start | bytes 2764804
  66.8 3.6 %copy-start.13 = (bf16[640,32,8,8]{0,3,2,1:T(8,128)(2,1)S(1)}, bf16[640,32,8,8]{0,3,2,1:T(8,128)(2,1)}, u32[]{:S(2)}) copy-start(bf16[640,32,8,8]{0,3,2,1:T(8,128)(2,1)} %get-tuple-element.24) | copy-start | bytes 7864324
  110.7 91.5 %reduce-scatter.5.cloned.1.call-start = ((), (), s32[]{:S(2)}) async-start(), calls=%async_computation.5 | async-start | bytes 2949120 | tf_op jit(solution)/shard_map/reduce_scatter | solution.py:83
  137.0 6.0 %copy-start.37 = (bf16[1,80,2048]{2,1,0:T(8,128)(2,1)S(1)}, bf16[1,80,2048]{2,1,0:T(8,128)(2,1)}, u32[]{:S(2)}) copy-start(bf16[1,80,2048]{2,1,0:T(8,128)(2,1)} %copy.37) | copy-start | bytes 983044
  137.0 6.7 %copy-start.38 = (bf16[1,80,2048]{2,1,0:T(8,128)(2,1)S(1)}, bf16[1,80,2048]{2,1,0:T(8,128)(2,1)}, u32[]{:S(2)}) copy-start(bf16[1,80,2048]{2,1,0:T(8,128)(2,1)} %copy.38) | copy-start | bytes 983044
  137.0 7.5 %copy-start.36 = (bf16[1,80,2048]{2,1,0:T(8,128)(2,1)S(1)}, bf16[1,80,2048]{2,1,0:T(8,128)(2,1)}, u32[]{:S(2)}) copy-start(bf16[1,80,2048]{2,1,0:T(8,128)(2,1)} %copy.39) | copy-start | bytes 983044
  142.9 2.8 copy-start.16
  158.4 186.1 %all-reduce.8.cloned.1.call-start = ((), (), s32[]{:S(2)}) async-start(), calls=%async_computation.6 | async-start | bytes 7372800 | tf_op jit(solution)/shard_map/psum | solution.py:90
  180.4 11.0 %copy-start.21 = (bf16[640,32,8,8]{0,3,2,1:T(8,128)(2,1)}, bf16[640,32,8,8]{0,3,2,1:T(8,128)(2,1)S(1)}, u32[]{:S(2)}) copy-start(bf16[640,32,8,8]{0,3,2,1:T(8,128)(2,1)S(1)} %get-tuple-element.19) | copy-start | bytes 7864324
  180.4 12.2 %copy-start.19 = (bf16[640,32,8,8]{0,3,2,1:T(8,128)(2,1)}, bf16[640,32,8,8]{0,3,2,1:T(8,128)(2,1)S(1)}, u32[]{:S(2)}) copy-start(bf16[640,32,8,8]{0,3,2,1:T(8,128)(2,1)S(1)} %get-tuple-element.20) | copy-start | bytes 7864324
  180.4 13.5 %copy-start.17 = (bf16[640,32,8,8]{0,3,2,1:T(8,128)(2,1)}, bf16[640,32,8,8]{0,3,2,1:T(8,128)(2,1)S(1)}, u32[]{:S(2)}) copy-start(bf16[640,32,8,8]{0,3,2,1:T(8,128)(2,1)S(1)} %get-tuple-element.14) | copy-start | bytes 7864324
  180.4 3.7 %copy-start.29 = (bf16[640,32,8,8]{0,3,2,1:T(8,128)(2,1)S(1)}, bf16[640,32,8,8]{0,3,2,1:T(8,128)(2,1)}, u32[]{:S(2)}) copy-start(bf16[640,32,8,8]{0,3,2,1:T(8,128)(2,1)} %get-tuple-element.15) | copy-start | bytes 7864324
  180.4 5.5 %copy-start.27 = (bf16[640,32,8,8]{0,3,2,1:T(8,128)(2,1)S(1)}, bf16[640,32,8,8]{0,3,2,1:T(8,128)(2,1)}, u32[]{:S(2)}) copy-start(bf16[640,32,8,8]{0,3,2,1:T(8,128)(2,1)} %get-tuple-element.16) | copy-start | bytes 7864324
  184.1 3.0 copy-start.25
  195.1 7.2 %copy-start.32 = (bf16[80,2048]{1,0:T(8,128)(2,1)S(1)}, bf16[80,2048]{1,0:T(8,128)(2,1)}, u32[]{:S(2)}) copy-start(bf16[80,2048]{1,0:T(8,128)(2,1)} %get-tuple-element.13) | copy-start | bytes 983044
  344.5 3.0 copy-start.34
  (27 other events, 49.4 us)
Sparse Core Ops, SparseCore 0:
  13.9 32.8 all-gather.2
  50.1 56.5 reduce-scatter.2
  110.9 30.0 all-gather.4
  158.5 43.7 reduce-scatter.4
  205.3 139.1 all-reduce.7
where the time goes:
time: 357 us; the launch traced here: 355 us
  waiting for transfers between devices  160 us (45%)
  local copies, waits for them, and re-layouts  111 us (31%)
  matrix products  51.3 us (14%)
  between operations  14.3 us (4%)
  blocking collectives  12.3 us (3%)
  other arithmetic  4.61 us (1%)
    psum x1, waiting for transfers between devices, local(): lax.psum((kernel_grad_one, bias_grad_one, kernel_grad_two, bias_grad_two)...  112 us
    slice x4, local copies, waits for them, and re-layouts, shift_tap(): grid = grid[:, :, 1 + row:9 + row, 1 + col:9 + col]  37.5 us
    unnamed x111, local copies, waits for them, and re-layouts  37.5 us
    reduce_scatter x1, waiting for transfers between devices, local(): lax.psum_scatter(spread_rows(kernel_two, shifted_two), 'blk', scatter_dim...  29.2 us
    dot_general x18, matrix products, add_conv(): jnp.dot(kernel[number], shift_tap(piece, row, col), preferred_element_typ...  22.6 us
    another operation x18, local copies, waits for them, and re-layouts, back_shifts(): jnp.stack([shift_tap(upstream, -row, -col) for row, col in offsets], 0)  22.3 us
    dot_general x18, matrix products, add_grad(): lax.dot_general(upstream, shift_tap(piece, row, col), (((1,), (1,)), ((),...  18.3 us
    all_gather x1, waiting for transfers between devices, local(): whole_zero = lax.all_gather(act_zero, 'blk', axis=0, tiled=True)  12.8 us
  transfers between devices with their start and end apart: 5, of which 4 were waited for; matrix products, arithmetic and copies ran while one was open for 38% of the time, Pallas kernels for 0%

commit v1 on v0

v1 whole, which is shorter than its diff:
```python
import functools

import jax
import jax.numpy as jnp
from jax import lax
from jax.experimental import pallas as pl
from jax.experimental.pallas import tpu as pltpu
from jax.sharding import PartitionSpec as P

bf16 = jnp.bfloat16
f32 = jnp.float32
offsets = [(row, col) for row in (-1, 0, 1) for col in (-1, 0, 1)]
VMEM_LIMIT = 40 << 20
EXTRA = 16
TILE = 256


def silu_slope(value):
    sigma = jax.nn.sigmoid(value)
    return sigma * (1.0 + value * (1.0 - sigma))


def inside(width, row, col):
    pixel = lax.broadcasted_iota(jnp.int32, (1, width), 1)
    r = ((pixel >> 3) & 7) + row
    s = (pixel & 7) + col
    return (r >= 0) & (r < 8) & (s >= 0) & (s < 8)


def shifted(values, row, col):
    step = 8 * row + col
    if step == 0:
        return values
    width = values.shape[1]
    moved = pltpu.roll(values, (-step) % width, 1)
    return jnp.where(inside(width, row, col), moved, jnp.zeros_like(moved))


def field_kernel(core, reinit, slots, noise, buffer, cotangent, bias, field, send, keep):
    half = field.shape[1] // 2
    lane = lax.broadcasted_iota(jnp.int32, (1, 128), 1)
    me = core[0]
    other = 1 - me

    def place(image, block):
        slot = slots[image]
        start = pl.multiple_of((slot >> 1) * 128, 128)
        stored = buffer[:, pl.ds(start, 128)].astype(f32)
        turned = pltpu.roll(stored, 64, 1)
        stored = jnp.where((slot & 1) == (image & 1), stored, turned)
        return jnp.where(reinit[image] == 1, block, stored)

    for pair in range(field.shape[1] // 128):
        here = pl.ds(pair * 128, 128)
        block = noise[:, here].astype(f32)
        left = place(2 * pair, block)
        right = place(2 * pair + 1, block)
        value = jnp.where(lane < 64, left, right)
        field[:, here] = value.astype(bf16)
        act = (value * jax.nn.sigmoid(value)).astype(bf16)
        owner = (pair * 128) // half
        inner = pl.ds(pair * 128 - owner * half, 128)

        @pl.when(me == owner)
        def _():
            keep[:, inner] = act

        @pl.when(me != owner)
        def _():
            send[:, inner] = act

    tail = pl.ds(half, half)
    keep[:, tail] = cotangent[:, pl.ds(pl.multiple_of(me * half, 128), half)]
    send[:, tail] = cotangent[:, pl.ds(pl.multiple_of(other * half, 128), half)]
    column = jnp.broadcast_to(bias[...].astype(f32), (field.shape[0], 128)).astype(bf16)
    keep[:, pl.ds(2 * half, 128)] = column
    send[:, pl.ds(2 * half, 128)] = column


def write_shifts(stack, values):
    depth = values.shape[0]
    for tap, (row, col) in enumerate(offsets):
        stack[pl.ds(tap * depth, depth), :] = shifted(values, -row, -col)


def write_back(order, block, kernels, stacks, send, keep):
    half, pixels = keep.shape[0], keep.shape[2]

    def step(at, _):
        lanes = pl.ds(pl.multiple_of(at * TILE, TILE), TILE)
        total = None
        for kernel, stack in zip(kernels, stacks):
            part = lax.dot_general(
                kernel[...], stack[:, lanes], (((0,), (0,)), ((), ())), preferred_element_type=f32
            )
            total = part if total is None else total + part
        block[...] = total
        depth = keep.shape[1]
        for slot in range(2 * half):
            rows = block[pl.ds(pl.multiple_of(order[slot] * depth, 8), depth), :]
            if slot < half:
                keep[slot, :, lanes] = rows
            else:
                send[slot - half, :, lanes] = rows.astype(bf16)
        return 0

    lax.fori_loop(0, pixels // TILE, step, 0)


def back_two_kernel(order, own, other, kernel_own, kernel_other, stack_own, stack_other, send, keep, block):
    write_shifts(stack_own, own[...])
    write_shifts(stack_other, other[...])
    write_back(order, block, (kernel_own, kernel_other), (stack_own, stack_other), send, keep)


def back_one_kernel(order, kernel_own, kernel_other, stack_own, stack_other, send, keep, block):
    write_back(order, block, (kernel_own, kernel_other), (stack_own, stack_other), send, keep)


def fetch(order, pieces, whole, sem):
    copies, slot = [], 0
    for piece in pieces:
        count, depth = piece.shape[0], piece.shape[1]
        for at in range(count):
            start = pl.multiple_of(order[slot] * depth, 16)
            copies.append(
                pltpu.make_async_copy(piece.at[at], whole.at[pl.ds(start, depth), :], sem.at[slot])
            )
            slot += 1
    for copy in copies:
        copy.start()
    for copy in copies:
        copy.wait()


def conv_tile(kernel, tile):
    depth = kernel.shape[0] // 9
    spread = jnp.dot(kernel[...], tile, preferred_element_type=f32)
    total = spread[4 * depth : 5 * depth]
    for tap, (row, col) in enumerate(offsets):
        if tap != 4:
            total = total + shifted(spread[tap * depth : (tap + 1) * depth], row, col)
    return total


def conv_one_kernel(
    core, order, own, near, far, kernel_own, kernel_other, bias_own, bias_other, whole, pre_own, pre_other, act, sem
):
    fetch(order, (own, near, far), whole, sem)
    depth = pre_own.shape[0]

    def step(at, _):
        lanes = pl.ds(pl.multiple_of(at * TILE, TILE), TILE)
        tile = whole[:, lanes]
        for kernel, bias, pre, place in (
            (kernel_own, bias_own, pre_own, core[0]),
            (kernel_other, bias_other, pre_other, 1 - core[0]),
        ):
            value = conv_tile(kernel, tile) + bias[:, :1].astype(f32)
            pre[:, lanes] = value
            rows = pl.ds(pl.multiple_of(place * depth, 16), depth)
            act[rows, lanes] = (value * jax.nn.sigmoid(value)).astype(bf16)
        return 0

    lax.fori_loop(0, whole.shape[1] // TILE, step, 0)


def conv_two_kernel(whole, kernel_own, kernel_other, out_own, out_other):
    def step(at, _):
        lanes = pl.ds(pl.multiple_of(at * TILE, TILE), TILE)
        tile = whole[:, lanes]
        out_own[:, lanes] = conv_tile(kernel_own, tile)
        out_other[:, lanes] = conv_tile(kernel_other, tile)
        return 0

    lax.fori_loop(0, whole.shape[1] // TILE, step, 0)


def write_kernel_grad(stack, whole, grad):
    rows = stack.shape[0]
    depth = rows // 9
    transposed = (((1,), (1,)), ((), ()))
    grad[:rows, :] = lax.dot_general(
        stack[...], whole[...], transposed, preferred_element_type=f32
    ).astype(grad.dtype)
    ones = jnp.ones((EXTRA, stack.shape[1]), bf16)
    sums = lax.dot_general(
        ones, stack[4 * depth : 5 * depth, :], transposed, preferred_element_type=f32
    )
    grad[rows:, :] = jnp.zeros((EXTRA, grad.shape[1]), grad.dtype)
    grad[rows:, :depth] = sums.astype(grad.dtype)


def grad_one_kernel(
    core, kept, near, far, pre_own, pre_other, whole, stack_own, stack_other, grad_own, grad_other
):
    depth = pre_own.shape[0]
    for pre, place, stack in (
        (pre_own, core[0], stack_own),
        (pre_other, 1 - core[0], stack_other),
    ):
        rows = pl.ds(pl.multiple_of(place * depth, 16), depth)
        upstream = kept[0, rows, :] + near[0, rows, :].astype(f32) + far[0, rows, :].astype(f32)
        write_shifts(stack, (upstream * silu_slope(pre[...])).astype(bf16))
    write_kernel_grad(stack_other, whole, grad_other)
    write_kernel_grad(stack_own, whole, grad_own)


def grad_two_kernel(order, own, near, far, stack_own, stack_other, whole, grad_own, grad_other, sem):
    fetch(order, (own, near, far), whole, sem)
    write_kernel_grad(stack_other, whole, grad_other)
    write_kernel_grad(stack_own, whole, grad_own)


def finish_kernel(places, quarter, near, far, grad, bias, total, sem):
    size = quarter.shape[0]
    for piece, at, place in (
        (quarter, None, places[0]),
        (near, None, places[1]),
        (far, 0, places[2]),
        (far, 1, places[3]),
    ):
        rows = pl.ds(pl.multiple_of(place * size, 8), size)
        total[rows, :] = (piece[...] if at is None else piece[at]).astype(f32)
    copy = pltpu.make_async_copy(total.at[pl.ds(0, grad.shape[0]), :], grad, sem)
    copy.start()
    bias[...] = total[grad.shape[0] :, :]
    copy.wait()


SMEM = pl.BlockSpec(memory_space=pltpu.SMEM)
VMEM = pl.BlockSpec(memory_space=pltpu.VMEM)
ANY = pl.BlockSpec(memory_space=pl.ANY)


def run(body, name, ins, outs, scratch=(), flops=0, out_specs=None):
    specs, args = zip(*ins)
    moved = sum(a.size * a.dtype.itemsize for a in args) + sum(
        o.size * o.dtype.itemsize for o in outs
    )
    return pl.pallas_call(
        body,
        name=name,
        out_shape=outs,
        in_specs=list(specs),
        out_specs=out_specs or [VMEM] * len(outs),
        scratch_shapes=list(scratch),
        cost_estimate=pl.CostEstimate(flops=flops, bytes_accessed=moved, transcendentals=0),
        compiler_params=pltpu.CompilerParams(vmem_limit_bytes=VMEM_LIMIT),
    )(*args)


def split_local(
    groups, width, noise, buffer, reinit, slots, kernel_one, bias_one, kernel_two, bias_two, cotangent
):
    depth, pixels = noise.shape
    channels = kernel_one.shape[2]
    half = pixels // 2
    chips = width // 2
    block = 2 * depth
    rows = 9 * depth
    work = 2 * 2 * rows * channels * half
    index = lax.axis_index("blk")
    core = index % 2
    chip = index // 2
    group = lax.axis_index("dp")
    shape = jax.ShapeDtypeStruct

    first = [2, 4]

    def chip_swap(values, step):
        pairs = [(i, i ^ first[(step + i) % 2]) for i in range(width)]
        return lax.ppermute(values, "blk", pairs)

    def core_swap(values):
        return lax.ppermute(values, "blk", [(i, i ^ 1) for i in range(width)])

    def group_swap(values, bit):
        return lax.ppermute(values, "dp", [(i, i ^ bit) for i in range(groups)])

    masks = jnp.where(core == 0, jnp.array([0, 1, 2, 3]), jnp.array([0, 2, 1, 3]))
    order = jnp.bitwise_xor(chip, masks).astype(jnp.int32)
    core_at = core.reshape(1).astype(jnp.int32)

    def gather(own):
        near = chip_swap(own, 0)
        far = chip_swap(jnp.concatenate([own, near], 0), 1)
        return own, near, far

    def scatter(send, keep):
        near = chip_swap(send, 1)
        far = chip_swap((keep[1:] + near[1:].astype(f32)).astype(bf16), 0)
        return keep, near, far

    own_one = kernel_one.reshape(rows, channels)
    own_two = kernel_two.reshape(rows, channels)
    other_two = core_swap(own_two)
    other_one = core_swap(own_one)

    field, send, keep = run(
        field_kernel,
        "field",
        [
            (SMEM, core_at),
            (SMEM, reinit),
            (SMEM, slots),
            (VMEM, noise),
            (VMEM, buffer),
            (VMEM, cotangent),
            (VMEM, bias_one[:, None]),
        ],
        [
            shape((depth, pixels), bf16),
            shape((depth, pixels + 128), bf16),
            shape((depth, pixels + 128), bf16),
        ],
    )
    came = core_swap(send)

    def paired(ours, theirs):
        return jnp.where(
            core == 0, jnp.concatenate([ours, theirs], 0), jnp.concatenate([theirs, ours], 0)
        )

    act_zero = paired(keep[:, :half], came[:, :half])[None]
    zero = gather(act_zero)

    stack = shape((rows, half), bf16)
    sends = shape((chips // 2, block, half), bf16)
    keeps = shape((chips // 2, block, half), f32)
    wide = pltpu.VMEM((channels, TILE), f32)
    cot_own, cot_other, send_two, keep_two = run(
        back_two_kernel,
        "back_two",
        [
            (SMEM, order),
            (VMEM, keep[:, half : 2 * half]),
            (VMEM, came[:, half : 2 * half]),
            (VMEM, own_two),
            (VMEM, other_two),
        ],
        [stack, stack, sends, keeps],
        [wide],
        work,
    )
    grad_act = scatter(send_two, keep_two)

    whole = shape((channels, half), bf16)
    plane = shape((depth, half), f32)
    whole_zero, pre_own, pre_other, act_one = run(
        conv_one_kernel,
        "conv_one",
        [
            (SMEM, core_at),
            (SMEM, order),
            (ANY, zero[0]),
            (ANY, zero[1]),
            (ANY, zero[2]),
            (VMEM, own_one),
            (VMEM, other_one),
            (VMEM, keep[:, 2 * half :]),
            (VMEM, came[:, 2 * half :]),
        ],
        [whole, plane, plane, shape((block, half), bf16)],
        [pltpu.SemaphoreType.DMA((chips,))],
        work,
    )
    one = gather(act_one[None])

    grad = [shape((rows + EXTRA, channels), f32), shape((rows + EXTRA, channels), bf16)]
    pre_stack_own, pre_stack_other, grad_one, grad_one_other = run(
        grad_one_kernel,
        "grad_one",
        [
            (SMEM, core_at),
            (VMEM, grad_act[0][:1]),
            (VMEM, grad_act[1][:1]),
            (VMEM, grad_act[2]),
            (VMEM, pre_own),
            (VMEM, pre_other),
            (VMEM, whole_zero),
        ],
        [stack, stack] + grad,
        (),
        work,
    )
    came_one = core_swap(grad_one_other)

    send_one, keep_one = run(
        back_one_kernel,
        "back_one",
        [
            (SMEM, order),
            (VMEM, own_one),
            (VMEM, other_one),
            (VMEM, pre_stack_own),
            (VMEM, pre_stack_other),
        ],
        [sends, keeps],
        [wide],
        work,
    )
    grad_zero = scatter(send_one, keep_one)

    whole_one, grad_two, grad_two_other = run(
        grad_two_kernel,
        "grad_two",
        [
            (SMEM, order),
            (ANY, one[0]),
            (ANY, one[1]),
            (ANY, one[2]),
            (VMEM, cot_own),
            (VMEM, cot_other),
        ],
        [whole] + grad,
        [pltpu.SemaphoreType.DMA((chips,))],
        work,
    )
    came_two = core_swap(grad_two_other)

    out_own, out_other = run(
        conv_two_kernel,
        "conv_two",
        [(VMEM, whole_one), (VMEM, own_two), (VMEM, other_two)],
        [plane, plane],
        (),
        work,
    )

    def unsplit(ours, theirs):
        return jnp.where(
            core == 0, jnp.concatenate([ours, theirs], 1), jnp.concatenate([theirs, ours], 1)
        )

    held = field.astype(f32)
    output = held + unsplit(out_own, core_swap(out_other)) + bias_two.astype(f32)[:, None]
    output = output.astype(bf16)

    total = grad_zero[0][0] + grad_zero[1][0].astype(f32) + grad_zero[2][0].astype(f32)
    ours = lax.dynamic_slice_in_dim(total, core * depth, depth, 0)
    theirs = lax.dynamic_slice_in_dim(total, (1 - core) * depth, depth, 0)
    grad_act_zero = unsplit(ours, core_swap(theirs))
    grad_field = cotangent.astype(f32) + grad_act_zero * silu_slope(held)

    low, high = group % 2, group // 2
    size = (rows + EXTRA) // 4
    places = jnp.stack(
        [
            low * 2 + high,
            low * 2 + 1 - high,
            (1 - low) * 2,
            (1 - low) * 2 + 1,
        ]
    ).astype(jnp.int32)

    def reduce(ours, theirs):
        ours = ours.reshape(2, 2, size, channels)
        theirs = theirs.reshape(2, 2, size, channels)

        def part(at):
            return lax.dynamic_index_in_dim(
                ours, at, 0, keepdims=False
            ) + lax.dynamic_index_in_dim(theirs, at, 0, keepdims=False).astype(f32)

        near = group_swap(part(1 - low).astype(bf16), 1)
        mine = part(low)

        def piece(at):
            return lax.dynamic_index_in_dim(
                mine, at, 0, keepdims=False
            ) + lax.dynamic_index_in_dim(near, at, 0, keepdims=False).astype(f32)

        far = group_swap(piece(1 - high).astype(bf16), 2)
        quarter = (piece(high) + far.astype(f32)).astype(bf16)
        beside = group_swap(quarter, 2)
        joined = jnp.where(high == 0, jnp.stack([quarter, beside]), jnp.stack([beside, quarter]))
        rest = group_swap(joined, 1)
        kernel_grad, bias_grad = run(
            finish_kernel,
            "finish",
            [(SMEM, places), (VMEM, quarter), (VMEM, beside), (VMEM, rest)],
            [shape((rows, channels), f32), shape((EXTRA, channels), f32)],
            [pltpu.VMEM((rows + EXTRA, channels), f32), pltpu.SemaphoreType.DMA],
            0,
            [ANY, VMEM],
        )
        return kernel_grad.reshape(9, depth, channels), bias_grad[0, :depth]

    kernel_grad_one, bias_grad_one = reduce(grad_one, came_one)
    kernel_grad_two, bias_grad_two = reduce(grad_two, came_two)
    return output, grad_field, kernel_grad_one, bias_grad_one, kernel_grad_two, bias_grad_two


def shift_tap(field, row, col):
    depth = field.shape[0]
    grid = field.reshape(depth, -1, 8, 8)
    grid = jnp.pad(grid, ((0, 0), (0, 0), (1, 1), (1, 1)))
    grid = grid[:, :, 1 + row : 9 + row, 1 + col : 9 + col]
    return grid.reshape(depth, -1)


def add_conv(total, piece, kernel):
    for number, (row, col) in enumerate(offsets):
        total = total + jnp.dot(
            kernel[number], shift_tap(piece, row, col), preferred_element_type=f32
        )
    return total


def add_grad(piece, upstream):
    parts = [
        lax.dot_general(
            upstream,
            shift_tap(piece, row, col),
            (((1,), (1,)), ((), ())),
            preferred_element_type=f32,
        )
        for row, col in offsets
    ]
    return jnp.stack(parts, 0)


def back_shifts(upstream):
    return jnp.stack([shift_tap(upstream, -row, -col) for row, col in offsets], 0)


def spread_rows(kernel, moved):
    return lax.dot_general(kernel, moved, (((0, 1), (0, 1)), ((), ())), preferred_element_type=f32)


def plain_local(
    noise, buffer, reinit, slots, kernel_one, bias_one, kernel_two, bias_two, cotangent
):
    depth = noise.shape[0]
    images = reinit.shape[0]
    pixels = images * 64
    stored = buffer.reshape(depth, -1, 64)[:, slots, :]
    fresh = noise.reshape(depth, images, 64)
    field = (
        jnp.where(reinit[None, :, None] == 1, fresh, stored).reshape(depth, pixels).astype(f32)
    )
    act_zero = jax.nn.silu(field).astype(bf16)
    empty = jnp.zeros((depth, pixels), f32)
    whole_zero = lax.all_gather(act_zero, "blk", axis=0, tiled=True)
    pre_one = add_conv(empty, whole_zero, kernel_one)
    pre_one = pre_one + bias_one.astype(f32)[:, None]
    act_one = jax.nn.silu(pre_one).astype(bf16)
    whole_one = lax.all_gather(act_one, "blk", axis=0, tiled=True)
    pre_two = add_conv(empty, whole_one, kernel_two)
    output = (field + pre_two + bias_two.astype(f32)[:, None]).astype(bf16)
    bias_grad_two = jnp.sum(cotangent.astype(f32), axis=1)
    kernel_grad_two = add_grad(whole_one, cotangent)
    grad_act_one = lax.psum_scatter(
        spread_rows(kernel_two, back_shifts(cotangent)), "blk", scatter_dimension=0, tiled=True
    )
    grad_pre_one = (grad_act_one * silu_slope(pre_one)).astype(bf16)
    bias_grad_one = jnp.sum(grad_pre_one.astype(f32), axis=1)
    kernel_grad_one = add_grad(whole_zero, grad_pre_one)
    grad_act_zero = lax.psum_scatter(
        spread_rows(kernel_one, back_shifts(grad_pre_one)).astype(bf16),
        "blk",
        scatter_dimension=0,
        tiled=True,
    ).astype(f32)
    grad_field = cotangent.astype(f32) + grad_act_zero * silu_slope(field)
    summed = lax.psum((kernel_grad_one, bias_grad_one, kernel_grad_two, bias_grad_two), "dp")
    return (output, grad_field, summed[0], summed[1], summed[2], summed[3])


def solution(mesh):
    groups, width = mesh.shape["dp"], mesh.shape["blk"]

    def local(noise, *rest):
        if groups == 4 and width == 8 and noise.shape[0] % 16 == 0 and noise.shape[1] % 512 == 0:
            return split_local(groups, width, noise, *rest)
        return plain_local(noise, *rest)

    return jax.shard_map(
        local,
        mesh=mesh,
        in_specs=(
            P("blk", "dp"),
            P("blk", "dp"),
            P("dp"),
            P("dp"),
            P(None, "blk", None),
            P("blk"),
            P(None, "blk", None),
            P("blk"),
            P("blk", "dp"),
        ),
        out_specs=(
            P("blk", "dp"),
            P("blk", "dp"),
            P(None, "blk", None),
            P("blk"),
            P(None, "blk", None),
            P("blk"),
        ),
        check_vma=False,
    )
```

time: 357 us -> 157 us (0.44)
  local copies, waits for them, and re-layouts: 111 us -> 10.6 us
  waiting for transfers between devices: 160 us -> 79.1 us
  matrix products: 51.3 us -> 0 us
  Pallas kernels: 0 us -> 34.5 us
  starting transfers between devices: 0.87 us -> 24.2 us
  between operations: 14.3 us -> 0.94 us
  blocking collectives: 12.3 us -> 0 us
    psum x1 -> x0, waiting for transfers between devices: 112 us -> none  [local(): lax.psum((kernel_grad_one, bias_grad_one, kernel_grad_two, bias_grad_two)...]
    ppermute x0 -> x23, waiting for transfers between devices: none -> 79.1 us  [the longest x8 60.3 us: group_swap(): return lax.ppermute(values, 'dp', [(i, i ^ bit) for i in range(groups)])]
    dot_general x38 -> x0, matrix products: 51.3 us -> none  [the longest x18 22.6 us: add_conv(): jnp.dot(kernel[number], shift_tap(piece, row, col), preferred_element_typ...]
    slice x4 -> x5, local copies, waits for them, and re-layouts: 37.5 us -> 1.79 us  [the longest x1 1.02 us: split_local(): came[:, half:2 * half]]
    reduce_scatter x2 -> x0, waiting for transfers between devices: 35.7 us -> none  [the longest x1 29.2 us: local(): lax.psum_scatter(spread_rows(kernel_two, shifted_two), 'blk', scatter_dim...]
    pallas_call x0 -> x9, Pallas kernels: none -> 34.5 us  [run(): pl.pallas_call(body, name=name, out_shape=outs, in_specs=list(specs), out...]
    unnamed x111 -> x32, local copies, waits for them, and re-layouts: 37.5 us -> 6.94 us
    ppermute x0 -> x23, starting transfers between devices: none -> 24.2 us  [the longest x8 15.3 us: chip_swap(): return lax.ppermute(values, 'blk', pairs)]
  transfers between devices with their start and end apart: 5 -> 23, of which waited for: 4 -> 14; matrix products, arithmetic and copies ran while one was open for 38% -> 6% of each run, Pallas kernels for 0% -> 19%
where the time goes in v1:
time: 157 us
  waiting for transfers between devices  79.1 us (50%)
  Pallas kernels  34.5 us (22%)
  starting transfers between devices  24.2 us (15%)
  local copies, waits for them, and re-layouts  10.6 us (7%)
  other arithmetic  7.38 us (5%)
    ppermute x8, waiting for transfers between devices, group_swap(): return lax.ppermute(values, 'dp', [(i, i ^ bit) for i in range(groups)])  60.3 us
    pallas_call x9, Pallas kernels, run(): pl.pallas_call(body, name=name, out_shape=outs, in_specs=list(specs), out...  34.5 us
    ppermute x8, waiting for transfers between devices, chip_swap(): return lax.ppermute(values, 'blk', pairs)  17.3 us
    ppermute x8, starting transfers between devices, chip_swap(): return lax.ppermute(values, 'blk', pairs)  15.3 us
    ppermute x8, starting transfers between devices, group_swap(): return lax.ppermute(values, 'dp', [(i, i ^ bit) for i in range(groups)])  8.06 us
    unnamed x32, local copies, waits for them, and re-layouts  6.94 us
  transfers between devices with their start and end apart: 23, of which 14 were waited for; matrix products, arithmetic and copies ran while one was open for 6% of the time, Pallas kernels for 19%

profile of v1, /device:TPU:0, one launch (start us, length us, event | category | flops | bytes accessed | tf_op | source)
XLA Modules:
  0.0 156.7 jit_solution(17915058398731207922)
XLA Ops:
  6.0 3.0 %field.1 = (bf16[80,2048]{1,0:T(8,128)(2,1)S(1)}, bf16[80,2176]{1,0:T(8,128)(2,1)}, bf16[80,2176]{1,0:T(8,128)(2,1)S(1)}) custom-call(s32[1]{0:T(128)} %bitcast.core, s32[32]{0:T(128)S(1)} %copy-done.6, s32[32]{0:T(128)S(1)} %copy-done.7, bf16[80,2048]{1,0:T(8,128)(2,1)S(1)} %copy-done.5, bf16[80,8192]{1,0:T(8,128)(2,1)S(1)} %copy-done.2, ...), custom_call_target="tpu_custom_call" | custom-call | bytes 2990500 | tf_op jit(solution)/shard_map/field/pallas_call | solution.py:241
  12.1 2.9 %collective-permute-start.1 = (bf16[1,160,1024]{2,1,0:T(8,128)(2,1)S(1)}, bf16[1,160,1024]{2,1,0:T(8,128)(2,1)S(1)}, u32[]{:S(2)}, u32[]{:S(2)}) collective-permute-start(bf16[1,160,1024]{2,1,0:T(8,128)(2,1)S(1)} %maximum_select_fusion.4.own), channel_id=1, source_target_pairs={{0,2},{1,5},{2,0},{3,7},{4,6},{5,1},{6,4},{7,3},{8,10},{9,13},{10,... | collective-permute-start | bytes 983048 | tf_op jit(solution)/shard_map/ppermute | solution.py:273
  15.1 5.0 %collective-permute-done.1.near = bf16[1,160,1024]{2,1,0:T(8,128)(2,1)S(1)} collective-permute-done((bf16[1,160,1024]{2,1,0:T(8,128)(2,1)S(1)}, bf16[1,160,1024]{2,1,0:T(8,128)(2,1)S(1)}, u32[]{:S(2)}, u32[]{:S(2)}) %collective-permute-start.1) | collective-permute-done | bytes 327712 | tf_op jit(solution)/shard_map/ppermute | solution.py:273
  20.2 2.1 %collective-permute-start.2 = (bf16[2,160,1024]{2,1,0:T(8,128)(2,1)S(1)}, bf16[2,160,1024]{2,1,0:T(8,128)(2,1)S(1)}, u32[]{:S(2)}, u32[]{:S(2)}) collective-permute-start(bf16[2,160,1024]{2,1,0:T(8,128)(2,1)S(1)} %pad_maximum_fusion), channel_id=1, source_target_pairs={{0,4},{1,3},{2,6},{3,1},{4,0},{5,7},{6,2},{7,5},{8,12},{9,11},{10,... | collective-permute-start | bytes 1966088 | tf_op jit(solution)/shard_map/ppermute | solution.py:273
  22.3 5.3 %back_two.1 = (bf16[720,1024]{1,0:T(8,128)(2,1)S(1)}, bf16[720,1024]{1,0:T(8,128)(2,1)S(1)}, bf16[2,160,1024]{2,1,0:T(8,128)(2,1)S(1)}, f32[2,160,1024]{2,1,0:T(8,128)S(1)}) custom-call(s32[4]{0:T(128)S(1)} %fusion.17.order, bf16[80,1024]{1,0:T(8,128)(2,1)S(1)} %get-tuple-element.68.own, bf16[80,1024]{1,0:T(8,128)(2,1)S(1)} %get-tuple-element.66.other, ...), custom_call_target="tpu_custom_call" | custom-call | flops 1887436800 | bytes 7086096 | tf_op jit(solution)/shard_map/back_two/pallas_call | solution.py:241
  28.5 2.4 %collective-permute-done.2.far = bf16[2,160,1024]{2,1,0:T(8,128)(2,1)S(1)} collective-permute-done((bf16[2,160,1024]{2,1,0:T(8,128)(2,1)S(1)}, bf16[2,160,1024]{2,1,0:T(8,128)(2,1)S(1)}, u32[]{:S(2)}, u32[]{:S(2)}) %collective-permute-start.2) | collective-permute-done | bytes 655392 | tf_op jit(solution)/shard_map/ppermute | solution.py:273
  30.9 5.6 %conv_one.1 = (bf16[640,1024]{1,0:T(8,128)(2,1)S(1)}, f32[80,1024]{1,0:T(8,128)S(1)}, f32[80,1024]{1,0:T(8,128)S(1)}, bf16[160,1024]{1,0:T(8,128)(2,1)S(1)}) custom-call(s32[1]{0:T(128)} %bitcast.core, s32[4]{0:T(128)S(1)} %fusion.17.order, bf16[1,160,1024]{2,1,0:T(8,128)(2,1)S(1)} %maximum_select_fusion.4.own, ...), custom_call_target="tpu_custom_call" | custom-call | flops 1887436800 | bytes 5488660 | tf_op jit(solution)/shard_map/conv_one/pallas_call | solution.py:241
  40.3 3.2 %collective-permute-done.4.near = bf16[1,160,1024]{2,1,0:T(8,128)(2,1)S(1)} collective-permute-done((bf16[1,160,1024]{2,1,0:T(8,128)(2,1)S(1)}, bf16[1,160,1024]{2,1,0:T(8,128)(2,1)S(1)}, u32[]{:S(2)}, u32[]{:S(2)}) %collective-permute-start.4) | collective-permute-done | bytes 327712 | tf_op jit(solution)/shard_map/ppermute | solution.py:273
  43.7 2.1 %collective-permute-start.5 = (bf16[2,160,1024]{2,1,0:T(8,128)(2,1)S(1)}, bf16[2,160,1024]{2,1,0:T(8,128)(2,1)S(1)}, u32[]{:S(2)}, u32[]{:S(2)}) collective-permute-start(bf16[2,160,1024]{2,1,0:T(8,128)(2,1)S(1)} %pad_maximum_fusion.1), channel_id=1, source_target_pairs={{0,4},{1,3},{2,6},{3,1},{4,0},{5,7},{6,2},{7,5},{8,12},{9,11},{10,... | collective-permute-start | bytes 1966088 | tf_op jit(solution)/shard_map/ppermute | solution.py:273
  45.8 3.7 %collective-permute-done.9.far = bf16[1,160,1024]{2,1,0:T(8,128)(2,1)S(1)} collective-permute-done((bf16[1,160,1024]{2,1,0:T(8,128)(2,1)S(1)}, bf16[1,160,1024]{2,1,0:T(8,128)(2,1)S(1)}, u32[]{:S(2)}, u32[]{:S(2)}) %collective-permute-start.9) | collective-permute-done | bytes 327712 | tf_op jit(solution)/shard_map/ppermute | solution.py:273
  49.5 2.8 %grad_one.1 = (bf16[720,1024]{1,0:T(8,128)(2,1)S(1)}, bf16[720,1024]{1,0:T(8,128)(2,1)S(1)}, f32[736,640]{1,0:T(8,128)S(1)}, bf16[736,640]{1,0:T(8,128)(2,1)}) custom-call(s32[1]{0:T(128)} %bitcast.core, f32[1,160,1024]{2,1,0:T(8,128)S(1)} %get-tuple-element.63.kept, bf16[1,160,1024]{2,1,0:T(8,128)(2,1)S(1)} %slice.67.near, ...), custom_call_target="tpu_custom_call" | custom-call | flops 1887436800 | bytes 9052164 | tf_op jit(solution)/shard_map/grad_one/pallas_call | solution.py:241
  52.3 5.2 %back_one.1 = (bf16[2,160,1024]{2,1,0:T(8,128)(2,1)}, f32[2,160,1024]{2,1,0:T(8,128)S(1)}) custom-call(s32[4]{0:T(128)S(1)} %fusion.17.order, bf16[720,640]{1,0:T(8,128)(2,1)S(1)} %bitcast.78, bf16[720,640]{1,0:T(8,128)(2,1)} %collective-permute-done.3.kernel_other, bf16[720,1024]{1,0:T(8,128)(2,1)S(1)} %get-tuple-element.46.stack_own, ...), custom_call_target="tpu_custom_call" | custom-call | flops 1887436800 | bytes 6758416 | tf_op jit(solution)/shard_map/back_one/pallas_call | solution.py:241
  57.6 2.5 %collective-permute-start.10 = (bf16[2,160,1024]{2,1,0:T(8,128)(2,1)}, bf16[2,160,1024]{2,1,0:T(8,128)(2,1)}, u32[]{:S(2)}, u32[]{:S(2)}) collective-permute-start(bf16[2,160,1024]{2,1,0:T(8,128)(2,1)} %get-tuple-element.49), channel_id=1, source_target_pairs={{0,4},{1,3},{2,6},{3,1},{4,0},{5,7},{6,2},{7,5},{8,12},{9,11},{10,... | collective-permute-start | bytes 1966088 | tf_op jit(solution)/shard_map/ppermute | solution.py:273
  60.0 3.6 %grad_two.1 = (bf16[640,1024]{1,0:T(8,128)(2,1)S(1)}, f32[736,640]{1,0:T(8,128)S(1)}, bf16[736,640]{1,0:T(8,128)(2,1)}) custom-call(s32[4]{0:T(128)S(1)} %fusion.17.order, bf16[1,160,1024]{2,1,0:T(8,128)(2,1)S(1)} %bitcast.75, bf16[1,160,1024]{2,1,0:T(8,128)(2,1)S(1)} %collective-permute-done.4.near, bf16[2,160,1024]{2,1,0:T(8,128)(2,1)S(1)} %collective-permute-done.5.far, ...), custom_call_target="tpu_custom_call" | custom-call | flops 1887436800 | bytes 8396816 | tf_op jit(solution)/shard_map/grad_two/pallas_call | solution.py:241
  66.2 2.7 %collective-permute-done.10 = bf16[2,160,1024]{2,1,0:T(8,128)(2,1)} collective-permute-done((bf16[2,160,1024]{2,1,0:T(8,128)(2,1)}, bf16[2,160,1024]{2,1,0:T(8,128)(2,1)}, u32[]{:S(2)}, u32[]{:S(2)}) %collective-permute-start.10) | collective-permute-done | bytes 655392 | tf_op jit(solution)/shard_map/ppermute | solution.py:273
  75.2 5.2 %conv_two.1 = (f32[80,1024]{1,0:T(8,128)S(1)}, f32[80,1024]{1,0:T(8,128)S(1)}) custom-call(bf16[640,1024]{1,0:T(8,128)(2,1)S(1)} %copy-done.13, bf16[720,640]{1,0:T(8,128)(2,1)S(1)} %bitcast.81, bf16[720,640]{1,0:T(8,128)(2,1)} %collective-permute-done.6.kernel_other), custom_call_target="tpu_custom_call" | custom-call | flops 1887436800 | bytes 3809280 | tf_op jit(solution)/shard_map/conv_two/pallas_call | solution.py:241
  83.4 3.0 %collective-permute-done.14 = bf16[2,184,640]{2,1,0:T(8,128)(2,1)S(1)} collective-permute-done((bf16[2,184,640]{2,1,0:T(8,128)(2,1)S(1)}, bf16[2,184,640]{2,1,0:T(8,128)(2,1)S(1)}, u32[]{:S(2)}, u32[]{:S(2)}) %collective-permute-start.14) | collective-permute-done | bytes 471072 | tf_op jit(solution)/shard_map/ppermute | solution.py:279
  86.5 2.6 %collective-permute-start.15 = (bf16[184,640]{1,0:T(8,128)(2,1)S(1)}, bf16[184,640]{1,0:T(8,128)(2,1)S(1)}, u32[]{:S(2)}, u32[]{:S(2)}) collective-permute-start(bf16[184,640]{1,0:T(8,128)(2,1)S(1)} %fusion.15), channel_id=1, source_target_pairs={{0,16},{8,24},{16,0},{24,8},{1,17},{9,25},{17,1},{25,9},{2,18},{10... | collective-permute-start | bytes 706568 | tf_op jit(solution)/shard_map/ppermute | solution.py:279
  89.2 11.6 %collective-permute-done.19 = bf16[2,184,640]{2,1,0:T(8,128)(2,1)S(1)} collective-permute-done((bf16[2,184,640]{2,1,0:T(8,128)(2,1)S(1)}, bf16[2,184,640]{2,1,0:T(8,128)(2,1)S(1)}, u32[]{:S(2)}, u32[]{:S(2)}) %collective-permute-start.19) | collective-permute-done | bytes 471072 | tf_op jit(solution)/shard_map/ppermute | solution.py:279
  104.0 15.0 %collective-permute-done.20 = bf16[184,640]{1,0:T(8,128)(2,1)S(1)} collective-permute-done((bf16[184,640]{1,0:T(8,128)(2,1)S(1)}, bf16[184,640]{1,0:T(8,128)(2,1)S(1)}, u32[]{:S(2)}, u32[]{:S(2)}) %collective-permute-start.20) | collective-permute-done | bytes 235552 | tf_op jit(solution)/shard_map/ppermute | solution.py:279
  119.3 9.8 %collective-permute-done.16.near = bf16[184,640]{1,0:T(8,128)(2,1)S(1)} collective-permute-done((bf16[184,640]{1,0:T(8,128)(2,1)S(1)}, bf16[184,640]{1,0:T(8,128)(2,1)S(1)}, u32[]{:S(2)}, u32[]{:S(2)}) %collective-permute-start.16) | collective-permute-done | bytes 235552 | tf_op jit(solution)/shard_map/ppermute | solution.py:279
  129.4 4.8 %collective-permute-done.21.near = bf16[184,640]{1,0:T(8,128)(2,1)S(1)} collective-permute-done((bf16[184,640]{1,0:T(8,128)(2,1)S(1)}, bf16[184,640]{1,0:T(8,128)(2,1)S(1)}, u32[]{:S(2)}, u32[]{:S(2)}) %collective-permute-start.21) | collective-permute-done | bytes 235552 | tf_op jit(solution)/shard_map/ppermute | solution.py:279
  135.8 8.5 %collective-permute-done.17.far = bf16[2,184,640]{2,1,0:T(8,128)(2,1)S(1)} collective-permute-done((bf16[2,184,640]{2,1,0:T(8,128)(2,1)S(1)}, bf16[2,184,640]{2,1,0:T(8,128)(2,1)S(1)}, u32[]{:S(2)}, u32[]{:S(2)}) %collective-permute-start.17) | collective-permute-done | bytes 471072 | tf_op jit(solution)/shard_map/ppermute | solution.py:279
  146.7 7.6 %collective-permute-done.22.far = bf16[2,184,640]{2,1,0:T(8,128)(2,1)S(1)} collective-permute-done((bf16[2,184,640]{2,1,0:T(8,128)(2,1)S(1)}, bf16[2,184,640]{2,1,0:T(8,128)(2,1)S(1)}, u32[]{:S(2)}, u32[]{:S(2)}) %collective-permute-start.22) | collective-permute-done | bytes 471072 | tf_op jit(solution)/shard_map/ppermute | solution.py:279
  (90 shorter events, 35.5 us)
Async XLA Ops:
  9.0 2.1 %collective-permute-start = (bf16[80,2176]{1,0:T(8,128)(2,1)}, bf16[80,2176]{1,0:T(8,128)(2,1)}, u32[]{:S(2)}, u32[]{:S(2)}) collective-permute-start(bf16[80,2176]{1,0:T(8,128)(2,1)} %get-tuple-element.34), channel_id=1, source_target_pairs={{0,1},{1,0},{2,3},{3,2},{4,5},{5,4},{6,7},{7,6},{8,9},{9,8},{10,11... | collective-permute-start | bytes 1044488 | tf_op jit(solution)/shard_map/ppermute | solution.py:276
  9.4 12.9 %collective-permute-start.6 = (bf16[720,640]{1,0:T(8,128)(2,1)S(1)}, bf16[720,640]{1,0:T(8,128)(2,1)}, u32[]{:S(2)}, u32[]{:S(2)}) collective-permute-start(bf16[720,640]{1,0:T(8,128)(2,1)S(1)} %bitcast.79), channel_id=1, source_target_pairs={{0,1},{1,0},{2,3},{3,2},{4,5},{5,4},{6,7},{7,6},{8,9},{9,8},{10,11... | collective-permute-start | bytes 2764808 | tf_op jit(solution)/shard_map/ppermute | solution.py:276
  12.1 8.0 %collective-permute-start.1 = (bf16[1,160,1024]{2,1,0:T(8,128)(2,1)S(1)}, bf16[1,160,1024]{2,1,0:T(8,128)(2,1)S(1)}, u32[]{:S(2)}, u32[]{:S(2)}) collective-permute-start(bf16[1,160,1024]{2,1,0:T(8,128)(2,1)S(1)} %maximum_select_fusion.4.own), channel_id=1, source_target_pairs={{0,2},{1,5},{2,0},{3,7},{4,6},{5,1},{6,4},{7,3},{8,10},{9,13},{10,... | collective-permute-start | bytes 983048 | tf_op jit(solution)/shard_map/ppermute | solution.py:273
  15.1 13.4 %collective-permute-start.3 = (bf16[720,640]{1,0:T(8,128)(2,1)S(1)}, bf16[720,640]{1,0:T(8,128)(2,1)}, u32[]{:S(2)}, u32[]{:S(2)}) collective-permute-start(bf16[720,640]{1,0:T(8,128)(2,1)S(1)} %bitcast.76), channel_id=1, source_target_pairs={{0,1},{1,0},{2,3},{3,2},{4,5},{5,4},{6,7},{7,6},{8,9},{9,8},{10,11... | collective-permute-start | bytes 2764808 | tf_op jit(solution)/shard_map/ppermute | solution.py:276
  20.2 10.7 %collective-permute-start.2 = (bf16[2,160,1024]{2,1,0:T(8,128)(2,1)S(1)}, bf16[2,160,1024]{2,1,0:T(8,128)(2,1)S(1)}, u32[]{:S(2)}, u32[]{:S(2)}) collective-permute-start(bf16[2,160,1024]{2,1,0:T(8,128)(2,1)S(1)} %pad_maximum_fusion), channel_id=1, source_target_pairs={{0,4},{1,3},{2,6},{3,1},{4,0},{5,7},{6,2},{7,5},{8,12},{9,11},{10,... | collective-permute-start | bytes 1966088 | tf_op jit(solution)/shard_map/ppermute | solution.py:273
  27.6 11.1 %collective-permute-start.8 = (bf16[2,160,1024]{2,1,0:T(8,128)(2,1)S(1)}, bf16[2,160,1024]{2,1,0:T(8,128)(2,1)S(1)}, u32[]{:S(2)}, u32[]{:S(2)}) collective-permute-start(bf16[2,160,1024]{2,1,0:T(8,128)(2,1)S(1)} %get-tuple-element.42), channel_id=1, source_target_pairs={{0,4},{1,3},{2,6},{3,1},{4,0},{5,7},{6,2},{7,5},{8,12},{9,11},{10,... | collective-permute-start | bytes 1966088 | tf_op jit(solution)/shard_map/ppermute | solution.py:273
  36.4 7.1 %collective-permute-start.4 = (bf16[1,160,1024]{2,1,0:T(8,128)(2,1)S(1)}, bf16[1,160,1024]{2,1,0:T(8,128)(2,1)S(1)}, u32[]{:S(2)}, u32[]{:S(2)}) collective-permute-start(bf16[1,160,1024]{2,1,0:T(8,128)(2,1)S(1)} %bitcast.73), channel_id=1, source_target_pairs={{0,2},{1,5},{2,0},{3,7},{4,6},{5,1},{6,4},{7,3},{8,10},{9,13},{10,... | collective-permute-start | bytes 983048 | tf_op jit(solution)/shard_map/ppermute | solution.py:273
  38.8 10.7 %collective-permute-start.9 = (bf16[1,160,1024]{2,1,0:T(8,128)(2,1)S(1)}, bf16[1,160,1024]{2,1,0:T(8,128)(2,1)S(1)}, u32[]{:S(2)}, u32[]{:S(2)}) collective-permute-start(bf16[1,160,1024]{2,1,0:T(8,128)(2,1)S(1)} %get-tuple-element.62), channel_id=1, source_target_pairs={{0,2},{1,5},{2,0},{3,7},{4,6},{5,1},{6,4},{7,3},{8,10},{9,13},{10,... | collective-permute-start | bytes 983048 | tf_op jit(solution)/shard_map/ppermute | solution.py:273
  43.7 16.4 %collective-permute-start.5 = (bf16[2,160,1024]{2,1,0:T(8,128)(2,1)S(1)}, bf16[2,160,1024]{2,1,0:T(8,128)(2,1)S(1)}, u32[]{:S(2)}, u32[]{:S(2)}) collective-permute-start(bf16[2,160,1024]{2,1,0:T(8,128)(2,1)S(1)} %pad_maximum_fusion.1), channel_id=1, source_target_pairs={{0,4},{1,3},{2,6},{3,1},{4,0},{5,7},{6,2},{7,5},{8,12},{9,11},{10,... | collective-permute-start | bytes 1966088 | tf_op jit(solution)/shard_map/ppermute | solution.py:273
  52.3 19.7 %collective-permute-start.13 = (bf16[736,640]{1,0:T(8,128)(2,1)}, bf16[736,640]{1,0:T(8,128)(2,1)}, u32[]{:S(2)}, u32[]{:S(2)}) collective-permute-start(bf16[736,640]{1,0:T(8,128)(2,1)} %get-tuple-element.51), channel_id=1, source_target_pairs={{0,1},{1,0},{2,3},{3,2},{4,5},{5,4},{6,7},{7,6},{8,9},{9,8},{10,11... | collective-permute-start | bytes 2826248 | tf_op jit(solution)/shard_map/ppermute | solution.py:276
  57.6 11.3 %collective-permute-start.10 = (bf16[2,160,1024]{2,1,0:T(8,128)(2,1)}, bf16[2,160,1024]{2,1,0:T(8,128)(2,1)}, u32[]{:S(2)}, u32[]{:S(2)}) collective-permute-start(bf16[2,160,1024]{2,1,0:T(8,128)(2,1)} %get-tuple-element.49), channel_id=1, source_target_pairs={{0,4},{1,3},{2,6},{3,1},{4,0},{5,7},{6,2},{7,5},{8,12},{9,11},{10,... | collective-permute-start | bytes 1966088 | tf_op jit(solution)/shard_map/ppermute | solution.py:273
  66.0 14.4 %collective-permute-start.18 = (bf16[736,640]{1,0:T(8,128)(2,1)}, bf16[736,640]{1,0:T(8,128)(2,1)}, u32[]{:S(2)}, u32[]{:S(2)}) collective-permute-start(bf16[736,640]{1,0:T(8,128)(2,1)} %get-tuple-element.55), channel_id=1, source_target_pairs={{0,1},{1,0},{2,3},{3,2},{4,5},{5,4},{6,7},{7,6},{8,9},{9,8},{10,11... | collective-permute-start | bytes 2826248 | tf_op jit(solution)/shard_map/ppermute | solution.py:276
  69.9 12.4 %collective-permute-start.11 = (bf16[1,160,1024]{2,1,0:T(8,128)(2,1)S(1)}, bf16[1,160,1024]{2,1,0:T(8,128)(2,1)S(1)}, u32[]{:S(2)}, u32[]{:S(2)}) collective-permute-start(bf16[1,160,1024]{2,1,0:T(8,128)(2,1)S(1)} %add_convert_fusion.2), channel_id=1, source_target_pairs={{0,2},{1,5},{2,0},{3,7},{4,6},{5,1},{6,4},{7,3},{8,10},{9,13},{10,... | collective-permute-start | bytes 983048 | tf_op jit(solution)/shard_map/ppermute | solution.py:273
  73.5 12.9 %collective-permute-start.14 = (bf16[2,184,640]{2,1,0:T(8,128)(2,1)S(1)}, bf16[2,184,640]{2,1,0:T(8,128)(2,1)S(1)}, u32[]{:S(2)}, u32[]{:S(2)}) collective-permute-start(bf16[2,184,640]{2,1,0:T(8,128)(2,1)S(1)} %get-tuple-element.60), channel_id=1, source_target_pairs={{0,8},{8,0},{16,24},{24,16},{1,9},{9,1},{17,25},{25,17},{2,10},{10... | collective-permute-start | bytes 1413128 | tf_op jit(solution)/shard_map/ppermute | solution.py:279
  80.4 54.1 %collective-permute-start.7 = (f32[80,1024]{1,0:T(8,128)S(1)}, f32[80,1024]{1,0:T(8,128)S(1)}, u32[]{:S(2)}, u32[]{:S(2)}) collective-permute-start(f32[80,1024]{1,0:T(8,128)S(1)} %get-tuple-element.40), channel_id=1, source_target_pairs={{0,1},{1,0},{2,3},{3,2},{4,5},{5,4},{6,7},{7,6},{8,9},{9,8},{10,11... | collective-permute-start | bytes 983048 | tf_op jit(solution)/shard_map/ppermute | solution.py:276
  81.8 19.0 %collective-permute-start.19 = (bf16[2,184,640]{2,1,0:T(8,128)(2,1)S(1)}, bf16[2,184,640]{2,1,0:T(8,128)(2,1)S(1)}, u32[]{:S(2)}, u32[]{:S(2)}) collective-permute-start(bf16[2,184,640]{2,1,0:T(8,128)(2,1)S(1)} %get-tuple-element.58), channel_id=1, source_target_pairs={{0,8},{8,0},{16,24},{24,16},{1,9},{9,1},{17,25},{25,17},{2,10},{10... | collective-permute-start | bytes 1413128 | tf_op jit(solution)/shard_map/ppermute | solution.py:279
  86.5 16.1 %collective-permute-start.15 = (bf16[184,640]{1,0:T(8,128)(2,1)S(1)}, bf16[184,640]{1,0:T(8,128)(2,1)S(1)}, u32[]{:S(2)}, u32[]{:S(2)}) collective-permute-start(bf16[184,640]{1,0:T(8,128)(2,1)S(1)} %fusion.15), channel_id=1, source_target_pairs={{0,16},{8,24},{16,0},{24,8},{1,17},{9,25},{17,1},{25,9},{2,18},{10... | collective-permute-start | bytes 706568 | tf_op jit(solution)/shard_map/ppermute | solution.py:279
  89.1 45.3 %collective-permute-start.12 = (f32[80,1024]{1,0:T(8,128)S(1)}, f32[80,1024]{1,0:T(8,128)S(1)}, u32[]{:S(2)}, u32[]{:S(2)}) collective-permute-start(f32[80,1024]{1,0:T(8,128)S(1)} %get-tuple-element.65), channel_id=1, source_target_pairs={{0,1},{1,0},{2,3},{3,2},{4,5},{5,4},{6,7},{7,6},{8,9},{9,8},{10,11... | collective-permute-start | bytes 983048 | tf_op jit(solution)/shard_map/ppermute | solution.py:276
  100.9 18.2 %collective-permute-start.20 = (bf16[184,640]{1,0:T(8,128)(2,1)S(1)}, bf16[184,640]{1,0:T(8,128)(2,1)S(1)}, u32[]{:S(2)}, u32[]{:S(2)}) collective-permute-start(bf16[184,640]{1,0:T(8,128)(2,1)S(1)} %fusion.16), channel_id=1, source_target_pairs={{0,16},{8,24},{16,0},{24,8},{1,17},{9,25},{17,1},{25,9},{2,18},{10... | collective-permute-start | bytes 706568 | tf_op jit(solution)/shard_map/ppermute | solution.py:279
  102.7 31.8 %copy-start.4 = (bf16[80,2048]{1,0:T(8,128)(2,1)S(1)}, bf16[80,2048]{1,0:T(8,128)(2,1)}, u32[]{:S(2)}) copy-start(bf16[80,2048]{1,0:T(8,128)(2,1)} %cotangent.1) | copy-start | bytes 983044
  102.7 26.5 %collective-permute-start.16 = (bf16[184,640]{1,0:T(8,128)(2,1)S(1)}, bf16[184,640]{1,0:T(8,128)(2,1)S(1)}, u32[]{:S(2)}, u32[]{:S(2)}) collective-permute-start(bf16[184,640]{1,0:T(8,128)(2,1)S(1)} %fusion.14.quarter), channel_id=1, source_target_pairs={{0,16},{8,24},{16,0},{24,8},{1,17},{9,25},{17,1},{25,9},{2,18},{10... | collective-permute-start | bytes 706568 | tf_op jit(solution)/shard_map/ppermute | solution.py:279
  119.2 15.1 %collective-permute-start.21 = (bf16[184,640]{1,0:T(8,128)(2,1)S(1)}, bf16[184,640]{1,0:T(8,128)(2,1)S(1)}, u32[]{:S(2)}, u32[]{:S(2)}) collective-permute-start(bf16[184,640]{1,0:T(8,128)(2,1)S(1)} %fusion.12.quarter), channel_id=1, source_target_pairs={{0,16},{8,24},{16,0},{24,8},{1,17},{9,25},{17,1},{25,9},{2,18},{10... | collective-permute-start | bytes 706568 | tf_op jit(solution)/shard_map/ppermute | solution.py:279
  129.3 15.0 %collective-permute-start.17 = (bf16[2,184,640]{2,1,0:T(8,128)(2,1)S(1)}, bf16[2,184,640]{2,1,0:T(8,128)(2,1)S(1)}, u32[]{:S(2)}, u32[]{:S(2)}) collective-permute-start(bf16[2,184,640]{2,1,0:T(8,128)(2,1)S(1)} %maximum_select_fusion.2), channel_id=1, source_target_pairs={{0,8},{8,0},{16,24},{24,16},{1,9},{9,1},{17,25},{25,17},{2,10},{10... | collective-permute-start | bytes 1413128 | tf_op jit(solution)/shard_map/ppermute | solution.py:279
  134.4 19.9 %collective-permute-start.22 = (bf16[2,184,640]{2,1,0:T(8,128)(2,1)S(1)}, bf16[2,184,640]{2,1,0:T(8,128)(2,1)S(1)}, u32[]{:S(2)}, u32[]{:S(2)}) collective-permute-start(bf16[2,184,640]{2,1,0:T(8,128)(2,1)S(1)} %maximum_select_fusion.3), channel_id=1, source_target_pairs={{0,8},{8,0},{16,24},{24,16},{1,9},{9,1},{17,25},{25,17},{2,10},{10... | collective-permute-start | bytes 1413128 | tf_op jit(solution)/shard_map/ppermute | solution.py:279
  (15 other events, 49.9 us)

commit v2 on v0

v2 whole, which is shorter than its diff:
```python
import functools

import jax
import jax.numpy as jnp
from jax import lax
from jax.experimental import pallas as pl
from jax.experimental.pallas import tpu as pltpu
from jax.sharding import PartitionSpec as P

bf16 = jnp.bfloat16
f32 = jnp.float32
offsets = [(row, col) for row in (-1, 0, 1) for col in (-1, 0, 1)]
VMEM_LIMIT = 20 << 20
EARLY = (10**10, 0)
LATE = (2 * 10**10, 3 * 10**9)
EXTRA = 16
SPLIT = 5
TILE = 256
CONV_TILE = 512


def silu_slope(value):
    sigma = jax.nn.sigmoid(value)
    return sigma * (1.0 + value * (1.0 - sigma))


def inside(width, row, col):
    pixel = lax.broadcasted_iota(jnp.int32, (1, width), 1)
    r = ((pixel >> 3) & 7) + row
    s = (pixel & 7) + col
    return (r >= 0) & (r < 8) & (s >= 0) & (s < 8)


def shifted(values, row, col):
    step = 8 * row + col
    if step == 0:
        return values
    kept = inside(128, row, col)
    pieces = []
    for start in range(0, values.shape[1], 128):
        moved = pltpu.roll(values[:, start : start + 128], (-step) % 128, 1)
        pieces.append(jnp.where(kept, moved, jnp.zeros_like(moved)))
    return jnp.concatenate(pieces, 1) if len(pieces) > 1 else pieces[0]


def field_kernel(
    core, reinit, slots, noise, buffer, cotangent, field, keep, send, fresh, stored, cot, act, fresh_at, slot_at, sem
):
    pixels = field.shape[1]
    half = pixels // 2
    lane = lax.broadcasted_iota(jnp.int32, (1, 128), 1)
    sources = (reinit, slots, noise, buffer, cotangent)
    places = (fresh_at, slot_at, fresh, stored, cot)
    copies = [
        pltpu.make_async_copy(source, place, sem.at[at])
        for at, (source, place) in enumerate(zip(sources, places))
    ]
    for copy in copies:
        copy.start()
    for copy in copies:
        copy.wait()

    def place(image, block):
        slot = slot_at[image]
        found = stored[:, pl.ds(pl.multiple_of((slot >> 1) * 128, 128), 128)]
        found = jnp.where((slot & 1) == (image & 1), found, pltpu.roll(found, 64, 1))
        return jnp.where(fresh_at[image] == 1, block, found)

    for pair in range(pixels // 128):
        here = pl.ds(pair * 128, 128)
        block = fresh[:, here]
        value = jnp.where(lane < 64, place(2 * pair, block), place(2 * pair + 1, block))
        field[:, here] = value
        value = value.astype(f32)
        act[:, here] = (value * jax.nn.sigmoid(value)).astype(bf16)

    for at, out in ((core[0], keep), (1 - core[0], send)):
        lanes = pl.ds(pl.multiple_of(at * half, 128), half)
        out[:, :half] = act[:, lanes]
        out[:, half:] = cot[:, lanes]


def place_kernel(core, keep, came, block):
    depth, half = keep.shape[0], block.shape[2]
    for at, part in ((core[0], keep), (1 - core[0], came)):
        block[0, pl.ds(pl.multiple_of(at * depth, 16), depth), :] = part[:, :half]


def write_shifts(stack, values, taps=range(9)):
    depth = values.shape[0]
    for at, tap in enumerate(taps):
        row, col = offsets[tap]
        stack[pl.ds(at * depth, depth), :] = shifted(values, -row, -col)


def back_kernel(start, order, own, other, kernel_own, kernel_other, send, keep, stack_own, stack_other, block):
    half, depth, pixels = keep.shape
    write_shifts(stack_own, own[:, start : start + pixels])
    write_shifts(stack_other, other[:, start : start + pixels])

    def step(at, _):
        lanes = pl.ds(pl.multiple_of(at * TILE, TILE), TILE)
        total = None
        for kernel, stack in ((kernel_own, stack_own), (kernel_other, stack_other)):
            part = lax.dot_general(
                kernel[...], stack[:, lanes], (((0,), (0,)), ((), ())), preferred_element_type=f32
            )
            total = part if total is None else total + part
        block[...] = total
        for slot in range(2 * half):
            rows = block[pl.ds(pl.multiple_of(order[slot] * depth, 8), depth), :]
            if slot < half:
                keep[slot, :, lanes] = rows
            else:
                send[slot - half, :, lanes] = rows.astype(bf16)
        return 0

    lax.fori_loop(0, pixels // TILE, step, 0)


def fetch(order, pieces, whole, sem):
    copies = []
    for piece in pieces:
        for at in range(piece.shape[0]):
            slot, depth = len(copies), piece.shape[1]
            start = pl.multiple_of(order[slot] * depth, 16)
            copies.append(
                pltpu.make_async_copy(piece.at[at], whole.at[pl.ds(start, depth), :], sem.at[slot])
            )
            copies[-1].start()
    return copies


def conv_tile(kernel, tile):
    depth = kernel.shape[0] // 9
    spread = jnp.dot(kernel[...], tile, preferred_element_type=f32)
    total = spread[4 * depth : 5 * depth]
    for tap, (row, col) in enumerate(offsets):
        if tap != 4:
            total = total + shifted(spread[tap * depth : (tap + 1) * depth], row, col)
    return total


def conv_one_kernel(
    core, order, own, near, across, beyond, kernel_own, kernel_other, bias_own, bias_other, whole, pre_own, pre_other, act, sem
):
    for copy in fetch(order, (own, near, across, beyond), whole, sem):
        copy.wait()
    depth = pre_own.shape[0]

    def step(at, _):
        lanes = pl.ds(pl.multiple_of(at * CONV_TILE, CONV_TILE), CONV_TILE)
        tile = whole[:, lanes]
        for kernel, bias, pre, place in (
            (kernel_own, bias_own, pre_own, core[0]),
            (kernel_other, bias_other, pre_other, 1 - core[0]),
        ):
            value = conv_tile(kernel, tile) + bias[:, :1].astype(f32)
            pre[:, lanes] = value
            rows = pl.ds(pl.multiple_of(place * depth, 16), depth)
            act[0, rows, lanes] = (value * jax.nn.sigmoid(value)).astype(bf16)
        return 0

    lax.fori_loop(0, whole.shape[1] // CONV_TILE, step, 0)


def conv_two_kernel(whole, kernel_own, kernel_other, out_own, out_other):
    def step(at, _):
        lanes = pl.ds(pl.multiple_of(at * CONV_TILE, CONV_TILE), CONV_TILE)
        tile = whole[:, lanes]
        out_own[:, lanes] = conv_tile(kernel_own, tile)
        out_other[:, lanes] = conv_tile(kernel_other, tile)
        return 0

    lax.fori_loop(0, whole.shape[1] // CONV_TILE, step, 0)


def slope_kernel(core, kept, near, far, pre_own, pre_other, own, other):
    depth = own.shape[0]
    for pre, place, out in ((pre_own, core[0], own), (pre_other, 1 - core[0], other)):
        rows = pl.ds(pl.multiple_of(place * depth, 16), depth)
        upstream = kept[0, rows, :] + near[0, rows, :].astype(f32) + far[0, rows, :].astype(f32)
        out[...] = (upstream * silu_slope(pre[...])).astype(bf16)


def write_grad(low, taps, parts, outs, grad, stacks):
    transposed = (((1,), (1,)), ((), ()))
    depth = parts[0][0].shape[0]
    rows = len(taps) * depth
    total = sums = None
    for at, (values, whole) in enumerate(parts):
        write_shifts(stacks.at[at], values, taps)
        part = lax.dot_general(stacks[at], whole[...], transposed, preferred_element_type=f32)
        total = part if total is None else total + part
        if taps[-1] == 8:
            ones = jnp.ones((EXTRA, values.shape[1]), bf16)
            part = lax.dot_general(ones, values, transposed, preferred_element_type=f32)
            sums = part if sums is None else sums + part
    grad[:rows, :] = total
    if taps[-1] == 8:
        grad[rows:, :] = jnp.zeros((EXTRA, grad.shape[1]), f32)
        grad[rows:, :depth] = sums
    base = 0
    for send, keep in outs:
        size = keep.shape[0]
        mine = pl.multiple_of(base + low[0] * size, 8)
        theirs = pl.multiple_of(base + (1 - low[0]) * size, 8)
        keep[...] = grad[pl.ds(mine, size), :]
        send[...] = grad[pl.ds(theirs, size), :].astype(bf16)
        base += 2 * size


def grad_one_kernel(taps, low, own, came, whole, whole_came, send, keep, grad, stacks):
    parts = (own[...], whole), (came[...], whole_came)
    write_grad(low, taps, parts, ((send, keep),), grad, stacks)


def grad_two_kernel(low, core, cotangent, whole, whole_came, send, keep_a, keep_b, grad, stacks):
    half = whole.shape[1]
    own, came = (
        cotangent[:, pl.ds(pl.multiple_of(at * half, 128), half)] for at in (core[0], 1 - core[0])
    )
    parts = (own, whole), (came, whole_came)
    size = keep_a.shape[0]
    outs = (send.at[:size], keep_a), (send.at[size:], keep_b)
    write_grad(low, tuple(range(9)), parts, outs, grad, stacks)


def add_split_kernel(keep_a, keep_b, near, out_a, out_b):
    size = keep_a.shape[0]
    out_a[...] = (keep_a[...] + near[:size].astype(f32)).astype(bf16)
    out_b[...] = (keep_b[...] + near[size:].astype(f32)).astype(bf16)


def copy_kernel(*refs):
    for values, out in zip(refs[: len(refs) // 2], refs[len(refs) // 2 :]):
        out[...] = values[...]


def add_kernel(left, right, out):
    out[...] = (left[...].astype(f32) + right[...].astype(f32)).astype(bf16)


def join_kernel(*refs):
    out, base = refs[-1], 0
    for left, right in zip(refs[0:-1:2], refs[1:-1:2]):
        size = left.shape[0]
        out[base : base + size, :] = (left[...].astype(f32) + right[...].astype(f32)).astype(bf16)
        base += size


def assemble_kernel(order, *refs):
    *pieces, whole, sem = refs
    for copy in fetch(order, pieces, whole, sem):
        copy.wait()


def sum_kernel(core, kept, near, far, own, other):
    depth = own.shape[0]
    for place, out in ((core[0], own), (1 - core[0], other)):
        rows = pl.ds(pl.multiple_of(place * depth, 16), depth)
        out[...] = kept[0, rows, :] + near[0, rows, :].astype(f32) + far[0, rows, :].astype(f32)


def output_kernel(core, field, own, came, bias, out, total, sem):
    half = own.shape[1]
    column = bias[:, :1].astype(f32)
    for at, part in ((core[0], own), (1 - core[0], came)):
        lanes = pl.ds(pl.multiple_of(at * half, 128), half)
        total[:, lanes] = (field[:, lanes].astype(f32) + part[...] + column).astype(bf16)
    copy = pltpu.make_async_copy(total, out, sem)
    copy.start()
    copy.wait()


def field_grad_kernel(core, field, cotangent, own, came, out, total, sem):
    half = own.shape[1]
    for at, part in ((core[0], own), (1 - core[0], came)):
        lanes = pl.ds(pl.multiple_of(at * half, 128), half)
        slope = silu_slope(field[:, lanes].astype(f32))
        total[:, lanes] = cotangent[:, lanes].astype(f32) + part[...] * slope
    copy = pltpu.make_async_copy(total, out, sem)
    copy.start()
    copy.wait()


def onward_kernel(keep, near, out):
    out[0] = (keep[1] + near[1].astype(f32)).astype(bf16)


def finish_kernel(sizes, low, *refs):
    pieces, (grad, bias, total, sem) = refs[:-4], refs[-4:]
    for place, side in ((low[0], pieces[0::2]), (1 - low[0], pieces[1::2])):
        rows = [(piece, at) for piece in side for at in range(0, piece.shape[0], 8)]
        base, at = 0, 0
        for size in sizes:
            left = size
            while left:
                piece, inner = rows[at // 8]
                count = min(left, piece.shape[0] - inner)
                start = pl.multiple_of(base + place * size + size - left, 8)
                total[pl.ds(start, count), :] = piece[inner : inner + count, :].astype(f32)
                at += count
                left -= count
            base += 2 * size
    copy = pltpu.make_async_copy(total.at[pl.ds(0, grad.shape[0]), :], grad, sem)
    copy.start()
    bias[...] = total[grad.shape[0] : grad.shape[0] + 1, : bias.shape[1]]
    copy.wait()


SMEM = pl.BlockSpec(memory_space=pltpu.SMEM)
VMEM = pl.BlockSpec(memory_space=pltpu.VMEM)
ANY = pl.BlockSpec(memory_space=pl.ANY)
HBM = pl.BlockSpec(memory_space=pltpu.HBM)
SPACES = {id(VMEM): pltpu.VMEM, id(HBM): pltpu.HBM}


def run(body, name, ins, outs, scratch=(), out_specs=None, after=(), cost=0):
    count, total = len(ins), len(ins) + len(after)
    end = total + len(outs)

    def marked(*refs):
        body(*refs[:count], *refs[total:end], *refs[end + 1 :])
        refs[end][...] = jnp.zeros_like(refs[end])

    ins = list(ins) + [(VMEM, value) for value in after]
    args = [
        pltpu.with_memory_space_constraint(arg, SPACES[id(spec)]) if id(spec) in SPACES else arg
        for spec, arg in ins
    ]
    out_specs = list(out_specs or [VMEM] * len(outs)) + [VMEM]
    outs = list(outs) + [jax.ShapeDtypeStruct((8, 128), f32)]
    return pl.pallas_call(
        marked,
        name=name,
        out_shape=[
            SPACES[id(spec)](out.shape, out.dtype) if id(spec) in SPACES else out
            for spec, out in zip(out_specs, outs)
        ],
        in_specs=[spec for spec, _ in ins],
        out_specs=out_specs,
        scratch_shapes=list(scratch),
        cost_estimate=pl.CostEstimate(flops=cost, bytes_accessed=0, transcendentals=0),
        compiler_params=pltpu.CompilerParams(vmem_limit_bytes=VMEM_LIMIT),
    )(*args)


def split_local(
    groups, width, noise, buffer, reinit, slots, kernel_one, bias_one, kernel_two, bias_two, cotangent
):
    depth, pixels = noise.shape
    channels = kernel_one.shape[2]
    half = pixels // 2
    chips = width // 2
    block = 2 * depth
    rows = 9 * depth
    index = lax.axis_index("blk")
    core = index % 2
    chip = index // 2
    group = lax.axis_index("dp")
    shape = jax.ShapeDtypeStruct
    dma = pltpu.SemaphoreType.DMA

    first = [2, 4]

    def swap(values, axis, pairs, name):
        with jax.named_scope(name):
            return lax.ppermute(values, axis, pairs)

    def chip_swap(values, step, name):
        pairs = [(i, i ^ first[(step + i) % 2]) for i in range(width)]
        return swap(values, "blk", pairs, name)

    def core_swap(values, name):
        return swap(values, "blk", [(i, i ^ 1) for i in range(width)], name)

    def group_swap(values, bit, name):
        return swap(values, "dp", [(i, i ^ bit) for i in range(groups)], name)

    def order_of(which):
        swapped = jnp.where(which == 0, jnp.array([0, 1, 2, 3]), jnp.array([0, 2, 1, 3]))
        return jnp.bitwise_xor(chip, swapped).astype(jnp.int32)

    order, order_came = order_of(core), order_of(1 - core)
    core_at = core.reshape(1).astype(jnp.int32)
    low = (group % 2).reshape(1).astype(jnp.int32)

    def vmem(*values):
        return [(VMEM, value) for value in values]

    def like(*values):
        return [shape(value.shape, bf16) for value in values]

    own_one = kernel_one.reshape(rows, channels)
    own_two = kernel_two.reshape(rows, channels)
    other_two = core_swap(own_two, "kernel_two")
    other_one = core_swap(own_one, "kernel_one")
    bias_own = jnp.broadcast_to(bias_one[:, None], (depth, 128))
    bias_other = core_swap(bias_own, "bias")

    marks, costs = [], [EARLY, "place", "copy", "add", "join", "onward", "sum", "assemble", EARLY]

    def step(body, name, ins, outs, scratch=(), out_specs=None):
        *results, mark = run(body, name, ins, outs, scratch, out_specs, marks[-1:], costs[-1][name in costs])
        marks.append(mark)
        return results[0] if len(results) == 1 else results

    part = shape((depth, half), bf16)
    piece = shape((1, block, half), bf16)
    wide = shape((depth, pixels), bf16)
    field, keep, send = step(
        field_kernel,
        "field",
        [(SMEM, core_at)] + [(HBM, v) for v in (reinit, slots, noise, buffer, cotangent)],
        [wide, wide, wide],
        [
            pltpu.VMEM(noise.shape, bf16),
            pltpu.VMEM(buffer.shape, bf16),
            pltpu.VMEM(cotangent.shape, bf16),
            pltpu.VMEM(noise.shape, bf16),
            pltpu.SMEM(reinit.shape, jnp.int32),
            pltpu.SMEM(slots.shape, jnp.int32),
            dma((5,)),
        ],
    )
    came = core_swap(send, "pair")
    zero = step(place_kernel, "place", [(SMEM, core_at)] + vmem(keep, came), [piece])
    zero_near, zero_across = chip_swap(zero, 0, "zero_near"), chip_swap(zero, 1, "zero_across")

    def back(name, start, own, other, kernel_own, kernel_other):
        return step(
            functools.partial(back_kernel, start),
            name,
            [(SMEM, order)] + vmem(own, other, kernel_own, kernel_other),
            [
                shape((chips // 2, block, half), bf16),
                shape((chips // 2, block, half), f32),
            ],
            [
                pltpu.VMEM((rows, half), bf16),
                pltpu.VMEM((rows, half), bf16),
                pltpu.VMEM((channels, TILE), f32),
            ],
        )

    send, keep_two = back("back_two", half, keep, came, own_two, other_two)
    zero_near, zero_across = step(
        copy_kernel, "copy", vmem(zero_near, zero_across), like(zero_near, zero_across)
    )
    zero_beyond = chip_swap(zero_near, 1, "zero_beyond")
    send, field = step(copy_kernel, "copy", vmem(send, field), like(send, field))
    near_two = chip_swap(send, 1, "two_near")

    whole = shape((channels, half), bf16)
    plane = shape((depth, half), f32)
    whole_zero, pre_own, pre_other, one = step(
        conv_one_kernel,
        "conv_one",
        [(SMEM, core_at), (SMEM, order)]
        + vmem(zero, zero_near, zero_across, zero_beyond)
        + vmem(own_one, other_one, bias_own, bias_other),
        [whole, plane, plane, piece],
        [dma((chips,))],
    )
    whole_zero_came = core_swap(whole_zero, "zero_pair")
    onward = step(onward_kernel, "onward", vmem(keep_two, near_two), [piece])
    far_two = chip_swap(onward, 0, "two_far")

    pre_grad, pre_grad_send = step(
        slope_kernel,
        "slope",
        [(SMEM, core_at)] + vmem(keep_two, near_two, far_two, pre_own, pre_other),
        [part, part],
    )
    pre_grad_came = core_swap(pre_grad_send, "pre_grad")
    one = step(copy_kernel, "copy", vmem(one), like(one))
    one_near, one_across = chip_swap(one, 0, "one_near"), chip_swap(one, 1, "one_across")

    chunks = (tuple(range(SPLIT)), tuple(range(SPLIT, 9)))
    sizes = [SPLIT * depth // 2, ((9 - SPLIT) * depth + EXTRA) // 2]

    def grad_outs(size):
        return [shape((size, channels), bf16), shape((size, channels), f32)]

    def grad_scratch(taps):
        extra = EXTRA if taps[-1] == 8 else 0
        return [
            pltpu.VMEM((len(taps) * depth + extra, channels), f32),
            pltpu.VMEM((2, len(taps) * depth, half), bf16),
        ]

    costs[-1] = LATE
    grads = []
    for at, taps in enumerate(chunks):
        send, keep = step(
            functools.partial(grad_one_kernel, taps),
            "grad_one_" + "ab"[at],
            [(SMEM, low)] + vmem(pre_grad, pre_grad_came, whole_zero, whole_zero_came),
            grad_outs(sizes[at]),
            grad_scratch(taps),
        )
        grads.append((keep, group_swap(send, 1, "one_A" + "ab"[at])))

    one_near, one_across, pre_grad, pre_grad_send = step(
        copy_kernel,
        "copy",
        vmem(one_near, one_across, pre_grad, pre_grad_send),
        like(one_near, one_across, pre_grad, pre_grad_send),
    )
    one_beyond = chip_swap(one_near, 1, "one_beyond")
    mine_a = step(add_kernel, "add", vmem(*grads[0]), like(grads[0][1]))
    far_a = group_swap(mine_a, 2, "one_Ba")
    mine_b = step(add_kernel, "add", vmem(*grads[1]), like(grads[1][1]))
    far_b = group_swap(mine_b, 2, "one_Bb")

    whole_one = step(
        assemble_kernel,
        "assemble",
        [(SMEM, order)] + vmem(one, one_near, one_across, one_beyond),
        [whole],
        [dma((chips,))],
    )
    whole_one_came = core_swap(whole_one, "one_pair")
    out_own, out_other = step(
        conv_two_kernel, "conv_two", vmem(whole_one, own_two, other_two), [plane, plane]
    )
    out_came = core_swap(out_other, "out_pair")

    size = sum(sizes)
    send, keep_a, keep_b = step(
        grad_two_kernel,
        "grad_two",
        [(SMEM, low), (SMEM, core_at)] + vmem(cotangent, whole_one, whole_one_came),
        [shape((size, channels), bf16)] + [shape((count, channels), f32) for count in sizes],
        grad_scratch(tuple(range(9))),
    )
    near = group_swap(send, 1, "two_A")
    output = step(
        output_kernel,
        "output",
        [(SMEM, core_at)]
        + vmem(field, out_own, out_came, jnp.broadcast_to(bias_two[:, None], (depth, 128))),
        [wide],
        [pltpu.VMEM((depth, pixels), bf16), dma],
        out_specs=[ANY],
    )

    send, keep_one = back("back_one", 0, pre_grad, pre_grad_send, own_one, other_one)
    near_one = chip_swap(send, 1, "one_near")

    half_one = step(
        join_kernel, "join", vmem(mine_a, far_a, mine_b, far_b), [shape((size, channels), bf16)]
    )
    rest_one = group_swap(half_one, 1, "one_C")
    mine_a, mine_b = step(
        add_split_kernel,
        "add",
        vmem(keep_a, keep_b, near),
        [shape((count, channels), bf16) for count in sizes],
    )
    far_a = group_swap(mine_a, 2, "two_Ba")
    far_b = group_swap(mine_b, 2, "two_Bb")

    def finish(name, pieces):
        kernel_grad, bias_grad = step(
            functools.partial(finish_kernel, sizes),
            name,
            [(SMEM, low)] + vmem(*pieces),
            [shape((rows, channels), f32), shape((1, depth), f32)],
            [pltpu.VMEM((rows + EXTRA, channels), f32), dma],
            out_specs=[ANY, VMEM],
        )
        return kernel_grad.reshape(9, depth, channels), bias_grad.reshape(depth)

    onward = step(onward_kernel, "onward", vmem(keep_one, near_one), [piece])
    far_one = chip_swap(onward, 0, "one_far")
    kernel_grad_one, bias_grad_one = finish("finish_one", [half_one, rest_one])
    own, other = step(
        sum_kernel, "sum", [(SMEM, core_at)] + vmem(keep_one, near_one, far_one), [plane, plane]
    )
    other = core_swap(other, "field_pair")

    half_a = step(add_kernel, "add", vmem(mine_a, far_a), like(mine_a))
    rest_a = group_swap(half_a, 1, "two_Ca")
    half_b = step(add_kernel, "add", vmem(mine_b, far_b), like(mine_b))
    rest_b = group_swap(half_b, 1, "two_Cb")
    grad_field = step(
        field_grad_kernel,
        "field_grad",
        [(SMEM, core_at)] + vmem(field, cotangent, own, other),
        [shape((depth, pixels), f32)],
        [pltpu.VMEM((depth, pixels), f32), dma],
        out_specs=[ANY],
    )
    kernel_grad_two, bias_grad_two = finish("finish_two", [half_a, rest_a, half_b, rest_b])
    return output, grad_field, kernel_grad_one, bias_grad_one, kernel_grad_two, bias_grad_two


def shift_tap(field, row, col):
    depth = field.shape[0]
    grid = field.reshape(depth, -1, 8, 8)
    grid = jnp.pad(grid, ((0, 0), (0, 0), (1, 1), (1, 1)))
    grid = grid[:, :, 1 + row : 9 + row, 1 + col : 9 + col]
    return grid.reshape(depth, -1)


def add_conv(total, piece, kernel):
    for number, (row, col) in enumerate(offsets):
        total = total + jnp.dot(
            kernel[number], shift_tap(piece, row, col), preferred_element_type=f32
        )
    return total


def add_grad(piece, upstream):
    parts = [
        lax.dot_general(
            upstream,
            shift_tap(piece, row, col),
            (((1,), (1,)), ((), ())),
            preferred_element_type=f32,
        )
        for row, col in offsets
    ]
    return jnp.stack(parts, 0)


def back_shifts(upstream):
    return jnp.stack([shift_tap(upstream, -row, -col) for row, col in offsets], 0)


def spread_rows(kernel, moved):
    return lax.dot_general(kernel, moved, (((0, 1), (0, 1)), ((), ())), preferred_element_type=f32)


def plain_local(
    noise, buffer, reinit, slots, kernel_one, bias_one, kernel_two, bias_two, cotangent
):
    depth = noise.shape[0]
    images = reinit.shape[0]
    pixels = images * 64
    stored = buffer.reshape(depth, -1, 64)[:, slots, :]
    fresh = noise.reshape(depth, images, 64)
    field = (
        jnp.where(reinit[None, :, None] == 1, fresh, stored).reshape(depth, pixels).astype(f32)
    )
    act_zero = jax.nn.silu(field).astype(bf16)
    empty = jnp.zeros((depth, pixels), f32)
    whole_zero = lax.all_gather(act_zero, "blk", axis=0, tiled=True)
    pre_one = add_conv(empty, whole_zero, kernel_one)
    pre_one = pre_one + bias_one.astype(f32)[:, None]
    act_one = jax.nn.silu(pre_one).astype(bf16)
    whole_one = lax.all_gather(act_one, "blk", axis=0, tiled=True)
    pre_two = add_conv(empty, whole_one, kernel_two)
    output = (field + pre_two + bias_two.astype(f32)[:, None]).astype(bf16)
    bias_grad_two = jnp.sum(cotangent.astype(f32), axis=1)
    kernel_grad_two = add_grad(whole_one, cotangent)
    grad_act_one = lax.psum_scatter(
        spread_rows(kernel_two, back_shifts(cotangent)), "blk", scatter_dimension=0, tiled=True
    )
    grad_pre_one = (grad_act_one * silu_slope(pre_one)).astype(bf16)
    bias_grad_one = jnp.sum(grad_pre_one.astype(f32), axis=1)
    kernel_grad_one = add_grad(whole_zero, grad_pre_one)
    grad_act_zero = lax.psum_scatter(
        spread_rows(kernel_one, back_shifts(grad_pre_one)).astype(bf16),
        "blk",
        scatter_dimension=0,
        tiled=True,
    ).astype(f32)
    grad_field = cotangent.astype(f32) + grad_act_zero * silu_slope(field)
    summed = lax.psum((kernel_grad_one, bias_grad_one, kernel_grad_two, bias_grad_two), "dp")
    return (output, grad_field, summed[0], summed[1], summed[2], summed[3])


def solution(mesh):
    groups, width = mesh.shape["dp"], mesh.shape["blk"]

    def local(noise, *rest):
        if groups == 4 and width == 8 and noise.shape[0] % 16 == 0 and noise.shape[1] % 512 == 0:
            return split_local(groups, width, noise, *rest)
        return plain_local(noise, *rest)

    return jax.shard_map(
        local,
        mesh=mesh,
        in_specs=(
            P("blk", "dp"),
            P("blk", "dp"),
            P("dp"),
            P("dp"),
            P(None, "blk", None),
            P("blk"),
            P(None, "blk", None),
            P("blk"),
            P("blk", "dp"),
        ),
        out_specs=(
            P("blk", "dp"),
            P("blk", "dp"),
            P(None, "blk", None),
            P("blk"),
            P(None, "blk", None),
            P("blk"),
        ),
        check_vma=False,
    )
```

time: 357 us -> 128 us (0.36)
  local copies, waits for them, and re-layouts: 111 us -> 1.63 us
  waiting for transfers between devices: 160 us -> 59.6 us
  matrix products: 51.3 us -> 0 us
  Pallas kernels: 0 us -> 37.2 us
  starting transfers between devices: 0.87 us -> 28.8 us
  between operations: 14.3 us -> 0.89 us
  blocking collectives: 12.3 us -> 0 us
  other arithmetic: 4.61 us -> 0.01 us
    psum x1 -> x0, waiting for transfers between devices: 112 us -> none  [local(): lax.psum((kernel_grad_one, bias_grad_one, kernel_grad_two, bias_grad_two)...]
    ppermute x0 -> x29, waiting for transfers between devices: none -> 59.6 us  [swap(): return lax.ppermute(values, axis, pairs)]
    dot_general x38 -> x0, matrix products: 51.3 us -> none  [the longest x18 22.6 us: add_conv(): jnp.dot(kernel[number], shift_tap(piece, row, col), preferred_element_typ...]
    slice x4 -> x0, local copies, waits for them, and re-layouts: 37.5 us -> none  [shift_tap(): grid = grid[:, :, 1 + row:9 + row, 1 + col:9 + col]]
    pallas_call x0 -> x28, Pallas kernels: none -> 37.2 us  [run(): pl.pallas_call(marked, name=name, out_shape=[SPACES[id(spec)](out.shape,...]
    unnamed x111 -> x18, local copies, waits for them, and re-layouts: 37.5 us -> 1.48 us
    reduce_scatter x2 -> x0, waiting for transfers between devices: 35.7 us -> none  [the longest x1 29.2 us: local(): lax.psum_scatter(spread_rows(kernel_two, shifted_two), 'blk', scatter_dim...]
    ppermute x0 -> x29, starting transfers between devices: none -> 28.8 us  [swap(): return lax.ppermute(values, axis, pairs)]
  transfers between devices with their start and end apart: 5 -> 29, of which waited for: 4 -> 15; matrix products, arithmetic and copies ran while one was open for 38% -> 1% of each run, Pallas kernels for 0% -> 27%
where the time goes in v2:
time: 128 us
  waiting for transfers between devices  59.6 us (47%)
  Pallas kernels  37.2 us (29%)
  starting transfers between devices  28.8 us (22%)
  local copies, waits for them, and re-layouts  1.63 us (1%)
    ppermute x29, waiting for transfers between devices, swap(): return lax.ppermute(values, axis, pairs)  59.6 us
    pallas_call x28, Pallas kernels, run(): pl.pallas_call(marked, name=name, out_shape=[SPACES[id(spec)](out.shape,...  37.2 us
    ppermute x29, starting transfers between devices, swap(): return lax.ppermute(values, axis, pairs)  28.8 us
  transfers between devices with their start and end apart: 29, of which 15 were waited for; matrix products, arithmetic and copies ran while one was open for 1% of the time, Pallas kernels for 27%

profile of v2, /device:TPU:0, one launch (start us, length us, event | category | flops | bytes accessed | tf_op | source)
XLA Modules:
  0.0 128.1 jit_solution(4443808461109952399)
XLA Ops:
  1.2 2.1 %field.1 = (bf16[80,2048]{1,0:T(8,128)(2,1)S(1)}, bf16[80,2048]{1,0:T(8,128)(2,1)S(1)}, bf16[80,2048]{1,0:T(8,128)(2,1)S(1)}, f32[8,128]{1,0:T(8,128)S(1)}) custom-call(s32[1]{0:T(128)} %bitcast.refs_0_.refs_1_, s32[32]{0:T(128)} %refs_1_.1, s32[32]{0:T(128)} %refs_2_.3, bf16[80,2048]{1,0:T(8,128)(2,1)} %refs_3_.1, bf16[80,8192]{1,0:T(8,128)(2,1)} %refs_4_.1, ...), custom_call_target="tpu_custom_call" | custom-call | flops 10000000000 | tf_op jit(solution)/shard_map/field/pallas_call | solution.py:334
  5.0 2.7 %collective-permute-start.2 = (bf16[1,160,1024]{2,1,0:T(8,128)(2,1)S(1)}, bf16[1,160,1024]{2,1,0:T(8,128)(2,1)S(1)}, u32[]{:S(2)}, u32[]{:S(2)}) collective-permute-start(bf16[1,160,1024]{2,1,0:T(8,128)(2,1)S(1)} %get-tuple-element.89.refs_2_), channel_id=1, source_target_pairs={{0,2},{1,5},{2,0},{3,7},{4,6},{5,1},{6,4},{7,3},{8,10},{9,13},{10,... | collective-permute-start | bytes 983048 | tf_op jit(solution)/shard_map/zero_near/ppermute | solution.py:369
  9.2 5.2 %back_two.1 = (bf16[2,160,1024]{2,1,0:T(8,128)(2,1)S(1)}, f32[2,160,1024]{2,1,0:T(8,128)S(1)}, f32[8,128]{1,0:T(8,128)S(1)}) custom-call(s32[4]{0:T(128)S(1)} %fusion.refs_0_.refs_1_, bf16[80,2048]{1,0:T(8,128)(2,1)S(1)} %get-tuple-element.83.refs_1_, bf16[80,2048]{1,0:T(8,128)(2,1)S(1)} %collective-permute-done.refs_2_, bf16[720,640]{1,0:T(8,128)(2,1)S(1)} %bitcast.11, ...), custom_call_target="tpu_custom_call" | custom-call | flops 10000000000 | tf_op jit(solution)/shard_map/back_two/pallas_call | solution.py:334
  19.3 3.8 %collective-permute-done.4.refs_5_ = bf16[1,160,1024]{2,1,0:T(8,128)(2,1)S(1)} collective-permute-done((bf16[1,160,1024]{2,1,0:T(8,128)(2,1)S(1)}, bf16[1,160,1024]{2,1,0:T(8,128)(2,1)S(1)}, u32[]{:S(2)}, u32[]{:S(2)}) %collective-permute-start.4) | collective-permute-done | bytes 327712 | tf_op jit(solution)/shard_map/zero_beyond/ppermute | solution.py:369
  23.2 4.8 %conv_one.1 = (bf16[640,1024]{1,0:T(8,128)(2,1)S(1)}, f32[80,1024]{1,0:T(8,128)S(1)}, f32[80,1024]{1,0:T(8,128)S(1)}, bf16[1,160,1024]{2,1,0:T(8,128)(2,1)S(1)}, f32[8,128]{1,0:T(8,128)S(1)}) custom-call(s32[1]{0:T(128)} %bitcast.refs_0_.refs_1_, s32[4]{0:T(128)S(1)} %fusion.refs_0_.refs_1_, bf16[1,160,1024]{2,1,0:T(8,128)(2,1)S(1)} %get-tuple-element.89.refs_2_, ...), custom_call_target="tpu_custom_call" | custom-call | flops 10000000000 | tf_op jit(solution)/shard_map/conv_one/pallas_call | solution.py:334
  27.9 2.2 %collective-permute-done.7.refs_1_.refs_2_ = bf16[2,160,1024]{2,1,0:T(8,128)(2,1)S(1)} collective-permute-done((bf16[2,160,1024]{2,1,0:T(8,128)(2,1)S(1)}, bf16[2,160,1024]{2,1,0:T(8,128)(2,1)S(1)}, u32[]{:S(2)}, u32[]{:S(2)}) %collective-permute-start.7) | collective-permute-done | bytes 655392 | tf_op jit(solution)/shard_map/two_near/ppermute | solution.py:369
  32.0 5.4 %collective-permute-done.8.refs_3_ = bf16[1,160,1024]{2,1,0:T(8,128)(2,1)S(1)} collective-permute-done((bf16[1,160,1024]{2,1,0:T(8,128)(2,1)S(1)}, bf16[1,160,1024]{2,1,0:T(8,128)(2,1)S(1)}, u32[]{:S(2)}, u32[]{:S(2)}) %collective-permute-start.8) | collective-permute-done | bytes 327712 | tf_op jit(solution)/shard_map/two_far/ppermute | solution.py:369
  41.3 2.9 %grad_one_a.1 = (bf16[200,640]{1,0:T(8,128)(2,1)S(1)}, f32[200,640]{1,0:T(8,128)S(1)}, f32[8,128]{1,0:T(8,128)S(1)}) custom-call(s32[1]{0:T(128)} %bitcast.3.refs_0_, bf16[80,1024]{1,0:T(8,128)(2,1)S(1)} %get-tuple-element.106.refs_1_.refs_2_, bf16[80,1024]{1,0:T(8,128)(2,1)S(1)} %collective-permute-done.11.refs_2_, ...), custom_call_target="tpu_custom_call" | custom-call | flops 20000000000 | tf_op jit(solution)/shard_map/grad_one_a/pallas_call | solution.py:334
  45.8 2.7 %grad_one_b.1 = (bf16[168,640]{1,0:T(8,128)(2,1)S(1)}, f32[168,640]{1,0:T(8,128)S(1)}, f32[8,128]{1,0:T(8,128)S(1)}) custom-call(s32[1]{0:T(128)} %bitcast.3.refs_0_, bf16[80,1024]{1,0:T(8,128)(2,1)S(1)} %get-tuple-element.106.refs_1_.refs_2_, bf16[80,1024]{1,0:T(8,128)(2,1)S(1)} %collective-permute-done.11.refs_2_, ...), custom_call_target="tpu_custom_call" | custom-call | flops 20000000000 | tf_op jit(solution)/shard_map/grad_one_b/pallas_call | solution.py:334
  49.9 3.4 %collective-permute-done.15.refs_1_ = bf16[200,640]{1,0:T(8,128)(2,1)S(1)} collective-permute-done((bf16[200,640]{1,0:T(8,128)(2,1)S(1)}, bf16[200,640]{1,0:T(8,128)(2,1)S(1)}, u32[]{:S(2)}, u32[]{:S(2)}) %collective-permute-start.15) | collective-permute-done | bytes 256032 | tf_op jit(solution)/shard_map/one_Aa/ppermute | solution.py:369
  53.4 3.5 %collective-permute-done.14.refs_1_ = bf16[168,640]{1,0:T(8,128)(2,1)S(1)} collective-permute-done((bf16[168,640]{1,0:T(8,128)(2,1)S(1)}, bf16[168,640]{1,0:T(8,128)(2,1)S(1)}, u32[]{:S(2)}, u32[]{:S(2)}) %collective-permute-start.14) | collective-permute-done | bytes 215072 | tf_op jit(solution)/shard_map/one_Ab/ppermute | solution.py:369
  56.9 2.7 %collective-permute-start.21 = (bf16[168,640]{1,0:T(8,128)(2,1)S(1)}, bf16[168,640]{1,0:T(8,128)(2,1)S(1)}, u32[]{:S(2)}, u32[]{:S(2)}) collective-permute-start(bf16[168,640]{1,0:T(8,128)(2,1)S(1)} %get-tuple-element.137.refs_2_), channel_id=1, source_target_pairs={{0,16},{8,24},{16,0},{24,8},{1,17},{9,25},{17,1},{25,9},{2,18},{10... | collective-permute-start | bytes 645128 | tf_op jit(solution)/shard_map/one_Bb/ppermute | solution.py:369
  61.0 4.3 %conv_two.1 = (f32[80,1024]{1,0:T(8,128)S(1)}, f32[80,1024]{1,0:T(8,128)S(1)}, f32[8,128]{1,0:T(8,128)S(1)}) custom-call(bf16[640,1024]{1,0:T(8,128)(2,1)S(1)} %get-tuple-element.121.refs_0_.refs_3_, bf16[720,640]{1,0:T(8,128)(2,1)S(1)} %bitcast.12, bf16[720,640]{1,0:T(8,128)(2,1)} %collective-permute-done.1.refs_4_.refs_2_, ...), custom_call_target="tpu_custom_call" | custom-call | flops 20000000000 | tf_op jit(solution)/shard_map/conv_two/pallas_call | solution.py:334
  65.9 2.7 %grad_two.1 = (bf16[368,640]{1,0:T(8,128)(2,1)S(1)}, f32[200,640]{1,0:T(8,128)S(1)}, f32[168,640]{1,0:T(8,128)S(1)}, f32[8,128]{1,0:T(8,128)S(1)}) custom-call(s32[1]{0:T(128)} %bitcast.3.refs_0_, s32[1]{0:T(128)} %bitcast.refs_0_.refs_1_, bf16[80,2048]{1,0:T(8,128)(2,1)S(1)} %copy-done.4, bf16[640,1024]{1,0:T(8,128)(2,1)S(1)} %get-tuple-element.121.refs_0_.refs_3_, ...), custom_call_target="tpu_custom_call" | custom-call | flops 20000000000 | tf_op jit(solution)/shard_map/grad_two/pallas_call | solution.py:334
  71.6 5.1 %back_one.1 = (bf16[2,160,1024]{2,1,0:T(8,128)(2,1)S(1)}, f32[2,160,1024]{2,1,0:T(8,128)S(1)}, f32[8,128]{1,0:T(8,128)S(1)}) custom-call(s32[4]{0:T(128)S(1)} %fusion.refs_0_.refs_1_, bf16[80,1024]{1,0:T(8,128)(2,1)S(1)} %get-tuple-element.128.refs_1_, bf16[80,1024]{1,0:T(8,128)(2,1)S(1)} %get-tuple-element.129.refs_2_, bf16[720,640]{1,0:T(8,128)(2,1)S(1)} %bitcast.15, ...), custom_call_target="tpu_custom_call" | custom-call | flops 20000000000 | tf_op jit(solution)/shard_map/back_one/pallas_call | solution.py:334
  77.1 2.7 %collective-permute-done.20.refs_1_ = bf16[200,640]{1,0:T(8,128)(2,1)S(1)} collective-permute-done((bf16[200,640]{1,0:T(8,128)(2,1)S(1)}, bf16[200,640]{1,0:T(8,128)(2,1)S(1)}, u32[]{:S(2)}, u32[]{:S(2)}) %collective-permute-start.20) | collective-permute-done | bytes 256032 | tf_op jit(solution)/shard_map/one_Ba/ppermute | solution.py:369
  80.6 9.3 %collective-permute-done.19.refs_2_ = bf16[368,640]{1,0:T(8,128)(2,1)S(1)} collective-permute-done((bf16[368,640]{1,0:T(8,128)(2,1)S(1)}, bf16[368,640]{1,0:T(8,128)(2,1)S(1)}, u32[]{:S(2)}, u32[]{:S(2)}) %collective-permute-start.19) | collective-permute-done | bytes 471072 | tf_op jit(solution)/shard_map/two_A/ppermute | solution.py:369
  93.6 7.3 %collective-permute-done.23.refs_2_ = bf16[368,640]{1,0:T(8,128)(2,1)S(1)} collective-permute-done((bf16[368,640]{1,0:T(8,128)(2,1)S(1)}, bf16[368,640]{1,0:T(8,128)(2,1)S(1)}, u32[]{:S(2)}, u32[]{:S(2)}) %collective-permute-start.23) | collective-permute-done | bytes 471072 | tf_op jit(solution)/shard_map/one_C/ppermute | solution.py:369
  103.0 7.0 %collective-permute-done.26.refs_1_ = bf16[200,640]{1,0:T(8,128)(2,1)S(1)} collective-permute-done((bf16[200,640]{1,0:T(8,128)(2,1)S(1)}, bf16[200,640]{1,0:T(8,128)(2,1)S(1)}, u32[]{:S(2)}, u32[]{:S(2)}) %collective-permute-start.26) | collective-permute-done | bytes 256032 | tf_op jit(solution)/shard_map/two_Ba/ppermute | solution.py:369
  110.1 3.6 %collective-permute-done.25.refs_1_ = bf16[168,640]{1,0:T(8,128)(2,1)S(1)} collective-permute-done((bf16[168,640]{1,0:T(8,128)(2,1)S(1)}, bf16[168,640]{1,0:T(8,128)(2,1)S(1)}, u32[]{:S(2)}, u32[]{:S(2)}) %collective-permute-start.25) | collective-permute-done | bytes 215072 | tf_op jit(solution)/shard_map/two_Bb/ppermute | solution.py:369
  113.8 2.0 %collective-permute-start.27 = (bf16[200,640]{1,0:T(8,128)(2,1)S(1)}, bf16[200,640]{1,0:T(8,128)(2,1)S(1)}, u32[]{:S(2)}, u32[]{:S(2)}) collective-permute-start(bf16[200,640]{1,0:T(8,128)(2,1)S(1)} %get-tuple-element.155.refs_1_), channel_id=1, source_target_pairs={{0,8},{8,0},{16,24},{24,16},{1,9},{9,1},{17,25},{25,17},{2,10},{10... | collective-permute-start | bytes 768008 | tf_op jit(solution)/shard_map/two_Ca/ppermute | solution.py:369
  116.9 5.1 %collective-permute-done.28.refs_4_ = bf16[168,640]{1,0:T(8,128)(2,1)S(1)} collective-permute-done((bf16[168,640]{1,0:T(8,128)(2,1)S(1)}, bf16[168,640]{1,0:T(8,128)(2,1)S(1)}, u32[]{:S(2)}, u32[]{:S(2)}) %collective-permute-start.28) | collective-permute-done | bytes 215072 | tf_op jit(solution)/shard_map/two_Cb/ppermute | solution.py:369
  122.0 3.6 %collective-permute-done.27.refs_2_ = bf16[200,640]{1,0:T(8,128)(2,1)S(1)} collective-permute-done((bf16[200,640]{1,0:T(8,128)(2,1)S(1)}, bf16[200,640]{1,0:T(8,128)(2,1)S(1)}, u32[]{:S(2)}, u32[]{:S(2)}) %collective-permute-start.27) | collective-permute-done | bytes 256032 | tf_op jit(solution)/shard_map/two_Ca/ppermute | solution.py:369
  125.6 2.0 %finish_two.1 = (f32[720,640]{1,0:T(8,128)}, f32[1,80]{1,0:T(1,128)S(1)}, f32[8,128]{1,0:T(8,128)}) custom-call(s32[1]{0:T(128)} %bitcast.3.refs_0_, bf16[200,640]{1,0:T(8,128)(2,1)S(1)} %get-tuple-element.155.refs_1_, bf16[200,640]{1,0:T(8,128)(2,1)S(1)} %collective-permute-done.27.refs_2_, bf16[168,640]{1,0:T(8,128)(2,1)S(1)} %get-tuple-element.156.refs_3_, ...), custom_call_target="tpu_custom_call" | custom-call | flops 20000000000 | tf_op jit(solution)/shard_map/finish_two/pallas_call | solution.py:334
  (83 shorter events, 31.3 us)
Async XLA Ops:
  0.6 8.6 %collective-permute-start.1 = (bf16[720,640]{1,0:T(8,128)(2,1)}, bf16[720,640]{1,0:T(8,128)(2,1)}, u32[]{:S(2)}, u32[]{:S(2)}) collective-permute-start(bf16[720,640]{1,0:T(8,128)(2,1)} %bitcast.10), channel_id=1, source_target_pairs={{0,1},{1,0},{2,3},{3,2},{4,5},{5,4},{6,7},{7,6},{8,9},{9,8},{10,11... | collective-permute-start | bytes 2764808 | tf_op jit(solution)/shard_map/kernel_two/ppermute | solution.py:369
  3.4 15.9 %collective-permute-start.5 = (bf16[720,640]{1,0:T(8,128)(2,1)S(1)}, bf16[720,640]{1,0:T(8,128)(2,1)}, u32[]{:S(2)}, u32[]{:S(2)}) collective-permute-start(bf16[720,640]{1,0:T(8,128)(2,1)S(1)} %bitcast.13), channel_id=1, source_target_pairs={{0,1},{1,0},{2,3},{3,2},{4,5},{5,4},{6,7},{7,6},{8,9},{9,8},{10,11... | collective-permute-start | bytes 2764808 | tf_op jit(solution)/shard_map/kernel_one/ppermute | solution.py:369
  5.0 10.2 %collective-permute-start.2 = (bf16[1,160,1024]{2,1,0:T(8,128)(2,1)S(1)}, bf16[1,160,1024]{2,1,0:T(8,128)(2,1)S(1)}, u32[]{:S(2)}, u32[]{:S(2)}) collective-permute-start(bf16[1,160,1024]{2,1,0:T(8,128)(2,1)S(1)} %get-tuple-element.89.refs_2_), channel_id=1, source_target_pairs={{0,2},{1,5},{2,0},{3,7},{4,6},{5,1},{6,4},{7,3},{8,10},{9,13},{10,... | collective-permute-start | bytes 983048 | tf_op jit(solution)/shard_map/zero_near/ppermute | solution.py:369
  7.7 8.3 %collective-permute-start.3 = (bf16[1,160,1024]{2,1,0:T(8,128)(2,1)S(1)}, bf16[1,160,1024]{2,1,0:T(8,128)(2,1)S(1)}, u32[]{:S(2)}, u32[]{:S(2)}) collective-permute-start(bf16[1,160,1024]{2,1,0:T(8,128)(2,1)S(1)} %get-tuple-element.89.refs_2_), channel_id=1, source_target_pairs={{0,4},{1,3},{2,6},{3,1},{4,0},{5,7},{6,2},{7,5},{8,12},{9,11},{10,... | collective-permute-start | bytes 983048 | tf_op jit(solution)/shard_map/zero_across/ppermute | solution.py:369
  16.0 7.1 %collective-permute-start.4 = (bf16[1,160,1024]{2,1,0:T(8,128)(2,1)S(1)}, bf16[1,160,1024]{2,1,0:T(8,128)(2,1)S(1)}, u32[]{:S(2)}, u32[]{:S(2)}) collective-permute-start(bf16[1,160,1024]{2,1,0:T(8,128)(2,1)S(1)} %get-tuple-element.93.refs_3_), channel_id=1, source_target_pairs={{0,4},{1,3},{2,6},{3,1},{4,0},{5,7},{6,2},{7,5},{8,12},{9,11},{10,... | collective-permute-start | bytes 983048 | tf_op jit(solution)/shard_map/zero_beyond/ppermute | solution.py:369
  18.1 12.1 %collective-permute-start.7 = (bf16[2,160,1024]{2,1,0:T(8,128)(2,1)S(1)}, bf16[2,160,1024]{2,1,0:T(8,128)(2,1)S(1)}, u32[]{:S(2)}, u32[]{:S(2)}) collective-permute-start(bf16[2,160,1024]{2,1,0:T(8,128)(2,1)S(1)} %get-tuple-element.98), channel_id=1, source_target_pairs={{0,4},{1,3},{2,6},{3,1},{4,0},{5,7},{6,2},{7,5},{8,12},{9,11},{10,... | collective-permute-start | bytes 1966088 | tf_op jit(solution)/shard_map/two_near/ppermute | solution.py:369
  30.2 7.1 %collective-permute-start.8 = (bf16[1,160,1024]{2,1,0:T(8,128)(2,1)S(1)}, bf16[1,160,1024]{2,1,0:T(8,128)(2,1)S(1)}, u32[]{:S(2)}, u32[]{:S(2)}) collective-permute-start(bf16[1,160,1024]{2,1,0:T(8,128)(2,1)S(1)} %get-tuple-element.100), channel_id=1, source_target_pairs={{0,2},{1,5},{2,0},{3,7},{4,6},{5,1},{6,4},{7,3},{8,10},{9,13},{10,... | collective-permute-start | bytes 983048 | tf_op jit(solution)/shard_map/two_far/ppermute | solution.py:369
  32.0 9.3 %collective-permute-start.12 = (bf16[640,1024]{1,0:T(8,128)(2,1)S(1)}, bf16[640,1024]{1,0:T(8,128)(2,1)}, u32[]{:S(2)}, u32[]{:S(2)}) collective-permute-start(bf16[640,1024]{1,0:T(8,128)(2,1)S(1)} %get-tuple-element.108.refs_3_), channel_id=1, source_target_pairs={{0,1},{1,0},{2,3},{3,2},{4,5},{5,4},{6,7},{7,6},{8,9},{9,8},{10,11... | collective-permute-start | bytes 3932168 | tf_op jit(solution)/shard_map/zero_pair/ppermute | solution.py:369
  37.8 11.3 %collective-permute-start.10 = (bf16[1,160,1024]{2,1,0:T(8,128)(2,1)S(1)}, bf16[1,160,1024]{2,1,0:T(8,128)(2,1)S(1)}, u32[]{:S(2)}, u32[]{:S(2)}) collective-permute-start(bf16[1,160,1024]{2,1,0:T(8,128)(2,1)S(1)} %get-tuple-element.105.refs_1_), channel_id=1, source_target_pairs={{0,4},{1,3},{2,6},{3,1},{4,0},{5,7},{6,2},{7,5},{8,12},{9,11},{10,... | collective-permute-start | bytes 983048 | tf_op jit(solution)/shard_map/one_across/ppermute | solution.py:369
  39.7 9.4 %collective-permute-start.9 = (bf16[1,160,1024]{2,1,0:T(8,128)(2,1)S(1)}, bf16[1,160,1024]{2,1,0:T(8,128)(2,1)S(1)}, u32[]{:S(2)}, u32[]{:S(2)}) collective-permute-start(bf16[1,160,1024]{2,1,0:T(8,128)(2,1)S(1)} %get-tuple-element.105.refs_1_), channel_id=1, source_target_pairs={{0,2},{1,5},{2,0},{3,7},{4,6},{5,1},{6,4},{7,3},{8,10},{9,13},{10,... | collective-permute-start | bytes 983048 | tf_op jit(solution)/shard_map/one_near/ppermute | solution.py:369
  44.2 9.1 %collective-permute-start.15 = (bf16[200,640]{1,0:T(8,128)(2,1)S(1)}, bf16[200,640]{1,0:T(8,128)(2,1)S(1)}, u32[]{:S(2)}, u32[]{:S(2)}) collective-permute-start(bf16[200,640]{1,0:T(8,128)(2,1)S(1)} %get-tuple-element.117), channel_id=1, source_target_pairs={{0,8},{8,0},{16,24},{24,16},{1,9},{9,1},{17,25},{25,17},{2,10},{10... | collective-permute-start | bytes 768008 | tf_op jit(solution)/shard_map/one_Aa/ppermute | solution.py:369
  48.5 8.3 %collective-permute-start.14 = (bf16[168,640]{1,0:T(8,128)(2,1)S(1)}, bf16[168,640]{1,0:T(8,128)(2,1)S(1)}, u32[]{:S(2)}, u32[]{:S(2)}) collective-permute-start(bf16[168,640]{1,0:T(8,128)(2,1)S(1)} %get-tuple-element.115), channel_id=1, source_target_pairs={{0,8},{8,0},{16,24},{24,16},{1,9},{9,1},{17,25},{25,17},{2,10},{10... | collective-permute-start | bytes 645128 | tf_op jit(solution)/shard_map/one_Ab/ppermute | solution.py:369
  49.1 10.8 %collective-permute-start.13 = (bf16[1,160,1024]{2,1,0:T(8,128)(2,1)S(1)}, bf16[1,160,1024]{2,1,0:T(8,128)(2,1)S(1)}, u32[]{:S(2)}, u32[]{:S(2)}) collective-permute-start(bf16[1,160,1024]{2,1,0:T(8,128)(2,1)S(1)} %get-tuple-element.112.refs_2_), channel_id=1, source_target_pairs={{0,4},{1,3},{2,6},{3,1},{4,0},{5,7},{6,2},{7,5},{8,12},{9,11},{10,... | collective-permute-start | bytes 983048 | tf_op jit(solution)/shard_map/one_beyond/ppermute | solution.py:369
  56.9 20.2 %collective-permute-start.21 = (bf16[168,640]{1,0:T(8,128)(2,1)S(1)}, bf16[168,640]{1,0:T(8,128)(2,1)S(1)}, u32[]{:S(2)}, u32[]{:S(2)}) collective-permute-start(bf16[168,640]{1,0:T(8,128)(2,1)S(1)} %get-tuple-element.137.refs_2_), channel_id=1, source_target_pairs={{0,16},{8,24},{16,0},{24,8},{1,17},{9,25},{17,1},{25,9},{2,18},{10... | collective-permute-start | bytes 645128 | tf_op jit(solution)/shard_map/one_Bb/ppermute | solution.py:369
  59.6 20.3 %collective-permute-start.20 = (bf16[200,640]{1,0:T(8,128)(2,1)S(1)}, bf16[200,640]{1,0:T(8,128)(2,1)S(1)}, u32[]{:S(2)}, u32[]{:S(2)}) collective-permute-start(bf16[200,640]{1,0:T(8,128)(2,1)S(1)} %get-tuple-element.136.refs_0_), channel_id=1, source_target_pairs={{0,16},{8,24},{16,0},{24,8},{1,17},{9,25},{17,1},{25,9},{2,18},{10... | collective-permute-start | bytes 768008 | tf_op jit(solution)/shard_map/one_Ba/ppermute | solution.py:369
  68.6 21.3 %collective-permute-start.19 = (bf16[368,640]{1,0:T(8,128)(2,1)S(1)}, bf16[368,640]{1,0:T(8,128)(2,1)S(1)}, u32[]{:S(2)}, u32[]{:S(2)}) collective-permute-start(bf16[368,640]{1,0:T(8,128)(2,1)S(1)} %get-tuple-element.135), channel_id=1, source_target_pairs={{0,8},{8,0},{16,24},{24,16},{1,9},{9,1},{17,25},{25,17},{2,10},{10... | collective-permute-start | bytes 1413128 | tf_op jit(solution)/shard_map/two_A/ppermute | solution.py:369
  76.8 16.2 %collective-permute-start.18 = (bf16[2,160,1024]{2,1,0:T(8,128)(2,1)S(1)}, bf16[2,160,1024]{2,1,0:T(8,128)(2,1)S(1)}, u32[]{:S(2)}, u32[]{:S(2)}) collective-permute-start(bf16[2,160,1024]{2,1,0:T(8,128)(2,1)S(1)} %get-tuple-element.132), channel_id=1, source_target_pairs={{0,4},{1,3},{2,6},{3,1},{4,0},{5,7},{6,2},{7,5},{8,12},{9,11},{10,... | collective-permute-start | bytes 1966088 | tf_op jit(solution)/shard_map/one_near/ppermute | solution.py:369
  79.9 21.0 %collective-permute-start.23 = (bf16[368,640]{1,0:T(8,128)(2,1)S(1)}, bf16[368,640]{1,0:T(8,128)(2,1)S(1)}, u32[]{:S(2)}, u32[]{:S(2)}) collective-permute-start(bf16[368,640]{1,0:T(8,128)(2,1)S(1)} %get-tuple-element.142.refs_1_), channel_id=1, source_target_pairs={{0,8},{8,0},{16,24},{24,16},{1,9},{9,1},{17,25},{25,17},{2,10},{10... | collective-permute-start | bytes 1413128 | tf_op jit(solution)/shard_map/one_C/ppermute | solution.py:369
  90.0 20.1 %collective-permute-start.26 = (bf16[200,640]{1,0:T(8,128)(2,1)S(1)}, bf16[200,640]{1,0:T(8,128)(2,1)S(1)}, u32[]{:S(2)}, u32[]{:S(2)}) collective-permute-start(bf16[200,640]{1,0:T(8,128)(2,1)S(1)} %get-tuple-element.148.refs_0_), channel_id=1, source_target_pairs={{0,16},{8,24},{16,0},{24,8},{1,17},{9,25},{17,1},{25,9},{2,18},{10... | collective-permute-start | bytes 768008 | tf_op jit(solution)/shard_map/two_Ba/ppermute | solution.py:369
  91.6 22.1 %collective-permute-start.25 = (bf16[168,640]{1,0:T(8,128)(2,1)S(1)}, bf16[168,640]{1,0:T(8,128)(2,1)S(1)}, u32[]{:S(2)}, u32[]{:S(2)}) collective-permute-start(bf16[168,640]{1,0:T(8,128)(2,1)S(1)} %get-tuple-element.147.refs_0_), channel_id=1, source_target_pairs={{0,16},{8,24},{16,0},{24,8},{1,17},{9,25},{17,1},{25,9},{2,18},{10... | collective-permute-start | bytes 645128 | tf_op jit(solution)/shard_map/two_Bb/ppermute | solution.py:369
  93.1 9.8 %collective-permute-start.22 = (bf16[1,160,1024]{2,1,0:T(8,128)(2,1)S(1)}, bf16[1,160,1024]{2,1,0:T(8,128)(2,1)S(1)}, u32[]{:S(2)}, u32[]{:S(2)}) collective-permute-start(bf16[1,160,1024]{2,1,0:T(8,128)(2,1)S(1)} %get-tuple-element.141), channel_id=1, source_target_pairs={{0,2},{1,5},{2,0},{3,7},{4,6},{5,1},{6,4},{7,3},{8,10},{9,13},{10,... | collective-permute-start | bytes 983048 | tf_op jit(solution)/shard_map/one_far/ppermute | solution.py:369
  102.9 12.9 %collective-permute-start.24 = (f32[80,1024]{1,0:T(8,128)S(1)}, f32[80,1024]{1,0:T(8,128)S(1)}, u32[]{:S(2)}, u32[]{:S(2)}) collective-permute-start(f32[80,1024]{1,0:T(8,128)S(1)} %get-tuple-element.146), channel_id=1, source_target_pairs={{0,1},{1,0},{2,3},{3,2},{4,5},{5,4},{6,7},{7,6},{8,9},{9,8},{10,11... | collective-permute-start | bytes 983048 | tf_op jit(solution)/shard_map/field_pair/ppermute | solution.py:369
  113.7 8.3 %collective-permute-start.28 = (bf16[168,640]{1,0:T(8,128)(2,1)S(1)}, bf16[168,640]{1,0:T(8,128)(2,1)S(1)}, u32[]{:S(2)}, u32[]{:S(2)}) collective-permute-start(bf16[168,640]{1,0:T(8,128)(2,1)S(1)} %get-tuple-element.156.refs_3_), channel_id=1, source_target_pairs={{0,8},{8,0},{16,24},{24,16},{1,9},{9,1},{17,25},{25,17},{2,10},{10... | collective-permute-start | bytes 645128 | tf_op jit(solution)/shard_map/two_Cb/ppermute | solution.py:369
  113.8 11.8 %collective-permute-start.27 = (bf16[200,640]{1,0:T(8,128)(2,1)S(1)}, bf16[200,640]{1,0:T(8,128)(2,1)S(1)}, u32[]{:S(2)}, u32[]{:S(2)}) collective-permute-start(bf16[200,640]{1,0:T(8,128)(2,1)S(1)} %get-tuple-element.155.refs_1_), channel_id=1, source_target_pairs={{0,8},{8,0},{16,24},{24,16},{1,9},{9,1},{17,25},{25,17},{2,10},{10... | collective-permute-start | bytes 768008 | tf_op jit(solution)/shard_map/two_Ca/ppermute | solution.py:369
  (13 other events, 57.6 us)

commit v3 on v2

--- a/solution.py
+++ b/solution.py
@@ -11,10 +11,13 @@
 f32 = jnp.float32
 offsets = [(row, col) for row in (-1, 0, 1) for col in (-1, 0, 1)]
 VMEM_LIMIT = 20 << 20
-EARLY = (10**10, 0)
-LATE = (2 * 10**10, 3 * 10**9)
+COSTS = {
+    "early": {"big": 10**10, "small": 0},
+    "late": {"big": 2 * 10**10, "small": 10**9},
+}
+SMALL = ("place", "copy", "add", "join", "onward", "sum", "assemble")
 EXTRA = 16
-SPLIT = 5
+PARTS_ONE, PARTS_TWO = (4, 9), (5, 9)
 TILE = 256
 CONV_TILE = 512
 
@@ -93,15 +96,20 @@
         stack[pl.ds(at * depth, depth), :] = shifted(values, -row, -col)
 
 
-def back_kernel(start, order, own, other, kernel_own, kernel_other, send, keep, stack_own, stack_other, block):
+def back_kernel(start, order, own, other, kernel_own, kernel_other, *refs):
+    *sends, keep, stack_own, stack_other, block, held, sem = refs
+    copy = pltpu.make_async_copy(kernel_own, held, sem)
+    copy.start()
     half, depth, pixels = keep.shape
+    places = [send.at[at] for send in sends for at in range(send.shape[0])]
     write_shifts(stack_own, own[:, start : start + pixels])
     write_shifts(stack_other, other[:, start : start + pixels])
+    copy.wait()
 
     def step(at, _):
         lanes = pl.ds(pl.multiple_of(at * TILE, TILE), TILE)
         total = None
-        for kernel, stack in ((kernel_own, stack_own), (kernel_other, stack_other)):
+        for kernel, stack in ((held, stack_own), (kernel_other, stack_other)):
             part = lax.dot_general(
                 kernel[...], stack[:, lanes], (((0,), (0,)), ((), ())), preferred_element_type=f32
             )
@@ -112,7 +120,7 @@
             if slot < half:
                 keep[slot, :, lanes] = rows
             else:
-                send[slot - half, :, lanes] = rows.astype(bf16)
+                places[slot - half][:, lanes] = rows.astype(bf16)
         return 0
 
     lax.fori_loop(0, pixels // TILE, step, 0)
@@ -142,9 +150,9 @@
 
 
 def conv_one_kernel(
-    core, order, own, near, across, beyond, kernel_own, kernel_other, bias_own, bias_other, whole, pre_own, pre_other, act, sem
+    core, order, three, beyond, kernel_own, kernel_other, bias_own, bias_other, whole, pre_own, pre_other, act, sem
 ):
-    for copy in fetch(order, (own, near, across, beyond), whole, sem):
+    for copy in fetch(order, (three, beyond), whole, sem):
         copy.wait()
     depth = pre_own.shape[0]
 
@@ -183,7 +191,7 @@
         out[...] = (upstream * silu_slope(pre[...])).astype(bf16)
 
 
-def write_grad(low, taps, parts, outs, grad, stacks):
+def write_grad(taps, parts, outs, grad, stacks):
     transposed = (((1,), (1,)), ((), ()))
     depth = parts[0][0].shape[0]
     rows = len(taps) * depth
@@ -203,33 +211,24 @@
     base = 0
     for send, keep in outs:
         size = keep.shape[0]
-        mine = pl.multiple_of(base + low[0] * size, 8)
-        theirs = pl.multiple_of(base + (1 - low[0]) * size, 8)
-        keep[...] = grad[pl.ds(mine, size), :]
-        send[...] = grad[pl.ds(theirs, size), :].astype(bf16)
-        base += 2 * size
-
-
-def grad_one_kernel(taps, low, own, came, whole, whole_came, send, keep, grad, stacks):
+        keep[...] = grad[base : base + size, :]
+        send[...] = grad[base : base + size, :].astype(bf16)
+        base += size
+
+
+def grad_one_kernel(taps, own, came, whole, whole_came, send, keep, grad, stacks):
     parts = (own[...], whole), (came[...], whole_came)
-    write_grad(low, taps, parts, ((send, keep),), grad, stacks)
-
-
-def grad_two_kernel(low, core, cotangent, whole, whole_came, send, keep_a, keep_b, grad, stacks):
+    write_grad(taps, parts, ((send, keep),), grad, stacks)
+
+
+def grad_two_kernel(core, cotangent, whole, whole_came, *refs):
+    *outs, grad, stacks = refs
     half = whole.shape[1]
     own, came = (
         cotangent[:, pl.ds(pl.multiple_of(at * half, 128), half)] for at in (core[0], 1 - core[0])
     )
     parts = (own, whole), (came, whole_came)
-    size = keep_a.shape[0]
-    outs = (send.at[:size], keep_a), (send.at[size:], keep_b)
-    write_grad(low, tuple(range(9)), parts, outs, grad, stacks)
-
-
-def add_split_kernel(keep_a, keep_b, near, out_a, out_b):
-    size = keep_a.shape[0]
-    out_a[...] = (keep_a[...] + near[:size].astype(f32)).astype(bf16)
-    out_b[...] = (keep_b[...] + near[size:].astype(f32)).astype(bf16)
+    write_grad(tuple(range(9)), parts, list(zip(outs[0::2], outs[1::2])), grad, stacks)
 
 
 def copy_kernel(*refs):
@@ -241,12 +240,11 @@
     out[...] = (left[...].astype(f32) + right[...].astype(f32)).astype(bf16)
 
 
-def join_kernel(*refs):
-    out, base = refs[-1], 0
-    for left, right in zip(refs[0:-1:2], refs[1:-1:2]):
-        size = left.shape[0]
-        out[base : base + size, :] = (left[...].astype(f32) + right[...].astype(f32)).astype(bf16)
-        base += size
+def join_kernel(own, near, across, send, field, joined, *outs):
+    for at, block in enumerate((own, near, across)):
+        joined[at] = block[0]
+    for values, out in zip((near, send, field), outs):
+        out[...] = values[...]
 
 
 def assemble_kernel(order, *refs):
@@ -285,28 +283,23 @@
 
 
 def onward_kernel(keep, near, out):
-    out[0] = (keep[1] + near[1].astype(f32)).astype(bf16)
-
-
-def finish_kernel(sizes, low, *refs):
+    out[0] = (keep[1] + near[near.shape[0] - 1].astype(f32)).astype(bf16)
+
+
+def finish_kernel(inner, *refs):
     pieces, (grad, bias, total, sem) = refs[:-4], refs[-4:]
-    for place, side in ((low[0], pieces[0::2]), (1 - low[0], pieces[1::2])):
-        rows = [(piece, at) for piece in side for at in range(0, piece.shape[0], 8)]
-        base, at = 0, 0
-        for size in sizes:
-            left = size
-            while left:
-                piece, inner = rows[at // 8]
-                count = min(left, piece.shape[0] - inner)
-                start = pl.multiple_of(base + place * size + size - left, 8)
-                total[pl.ds(start, count), :] = piece[inner : inner + count, :].astype(f32)
-                at += count
-                left -= count
-            base += 2 * size
-    copy = pltpu.make_async_copy(total.at[pl.ds(0, grad.shape[0]), :], grad, sem)
-    copy.start()
-    bias[...] = total[grad.shape[0] : grad.shape[0] + 1, : bias.shape[1]]
-    copy.wait()
+    base, copies, rows = 0, [], grad.shape[0]
+    for at, (made, came) in enumerate(zip(pieces[0::2], pieces[1::2])):
+        size = made.shape[0]
+        value = jnp.where(inner[0] == 1, made[...], came[...])
+        total[base : base + size, :] = value.astype(f32)
+        span = pl.ds(base, min(size, rows - base))
+        copies.append(pltpu.make_async_copy(total.at[span, :], grad.at[span, :], sem.at[at]))
+        copies[-1].start()
+        base += size
+    bias[...] = total[rows : rows + 1, : bias.shape[1]]
+    for copy in copies:
+        copy.wait()
 
 
 SMEM = pl.BlockSpec(memory_space=pltpu.SMEM)
@@ -314,6 +307,10 @@
 ANY = pl.BlockSpec(memory_space=pl.ANY)
 HBM = pl.BlockSpec(memory_space=pltpu.HBM)
 SPACES = {id(VMEM): pltpu.VMEM, id(HBM): pltpu.HBM}
+
+
+def in_hbm(values):
+    return pltpu.with_memory_space_constraint(values, pltpu.HBM)
 
 
 def run(body, name, ins, outs, scratch=(), out_specs=None, after=(), cost=0):
@@ -375,8 +372,10 @@
     def core_swap(values, name):
         return swap(values, "blk", [(i, i ^ 1) for i in range(width)], name)
 
-    def group_swap(values, bit, name):
-        return swap(values, "dp", [(i, i ^ bit) for i in range(groups)], name)
+    line = {"in": [(0, 1), (3, 2)], "middle": [(1, 2), (2, 1)], "out": [(1, 0), (2, 3)]}
+
+    def group_send(values, way, name):
+        return swap(values, "dp", line[way], name + "_" + way)
 
     def order_of(which):
         swapped = jnp.where(which == 0, jnp.array([0, 1, 2, 3]), jnp.array([0, 2, 1, 3]))
@@ -384,7 +383,7 @@
 
     order, order_came = order_of(core), order_of(1 - core)
     core_at = core.reshape(1).astype(jnp.int32)
-    low = (group % 2).reshape(1).astype(jnp.int32)
+    inner = ((group == 1) | (group == 2)).reshape(1).astype(jnp.int32)
 
     def vmem(*values):
         return [(VMEM, value) for value in values]
@@ -399,10 +398,13 @@
     bias_own = jnp.broadcast_to(bias_one[:, None], (depth, 128))
     bias_other = core_swap(bias_own, "bias")
 
-    marks, costs = [], [EARLY, "place", "copy", "add", "join", "onward", "sum", "assemble", EARLY]
-
-    def step(body, name, ins, outs, scratch=(), out_specs=None):
-        *results, mark = run(body, name, ins, outs, scratch, out_specs, marks[-1:], costs[-1][name in costs])
+    marks, phase = [], ["early"]
+
+    def step(body, name, ins, outs, scratch=(), out_specs=None, also=()):
+        after = marks[-1:] + list(also)
+        costs = COSTS[phase[0]]
+        cost = costs.get(name, costs["small" if name in SMALL else "big"])
+        *results, mark = run(body, name, ins, outs, scratch, out_specs, after, cost)
         marks.append(mark)
         return results[0] if len(results) == 1 else results
 
@@ -428,29 +430,41 @@
     zero = step(place_kernel, "place", [(SMEM, core_at)] + vmem(keep, came), [piece])
     zero_near, zero_across = chip_swap(zero, 0, "zero_near"), chip_swap(zero, 1, "zero_across")
 
-    def back(name, start, own, other, kernel_own, kernel_other):
+    def back(name, start, sends, *values):
         return step(
             functools.partial(back_kernel, start),
             name,
-            [(SMEM, order)] + vmem(own, other, kernel_own, kernel_other),
-            [
-                shape((chips // 2, block, half), bf16),
-                shape((chips // 2, block, half), f32),
-            ],
+            [(SMEM, order)]
+            + vmem(*values[:2])
+            + [(HBM, in_hbm(values[2])), (VMEM, values[3])],
+            [shape((count, block, half), bf16) for count in sends]
+            + [shape((chips // 2, block, half), f32)],
             [
                 pltpu.VMEM((rows, half), bf16),
                 pltpu.VMEM((rows, half), bf16),
                 pltpu.VMEM((channels, TILE), f32),
+                pltpu.VMEM((rows, channels), bf16),
+                dma,
             ],
         )
 
-    send, keep_two = back("back_two", half, keep, came, own_two, other_two)
-    zero_near, zero_across = step(
-        copy_kernel, "copy", vmem(zero_near, zero_across), like(zero_near, zero_across)
+    send, last, keep_two = back("back_two", half, (1, 1), keep, came, own_two, other_two)
+    last_two = chip_swap(last, 1, "two_last")
+    zero, zero_near, send, field = step(
+        join_kernel,
+        "join",
+        vmem(zero, zero_near, zero_across, send, field),
+        [shape((3, block, half), bf16)] + like(zero_near, send, field),
+        also=[other_one, bias_other],
     )
     zero_beyond = chip_swap(zero_near, 1, "zero_beyond")
-    send, field = step(copy_kernel, "copy", vmem(send, field), like(send, field))
+    zero_came = core_swap(zero, "zero_pair")
+    onward = step(onward_kernel, "onward", vmem(keep_two, last_two), [piece])
+    far_two = chip_swap(onward, 0, "two_far")
+    send = step(copy_kernel, "copy", vmem(send), like(send))
     near_two = chip_swap(send, 1, "two_near")
+    zero_beyond = step(copy_kernel, "copy", vmem(zero_beyond), like(zero_beyond))
+    beyond_came = core_swap(zero_beyond, "zero_pair_beyond")
 
     whole = shape((channels, half), bf16)
     plane = shape((depth, half), f32)
@@ -458,14 +472,18 @@
         conv_one_kernel,
         "conv_one",
         [(SMEM, core_at), (SMEM, order)]
-        + vmem(zero, zero_near, zero_across, zero_beyond)
+        + vmem(zero, zero_beyond)
         + vmem(own_one, other_one, bias_own, bias_other),
         [whole, plane, plane, piece],
         [dma((chips,))],
     )
-    whole_zero_came = core_swap(whole_zero, "zero_pair")
-    onward = step(onward_kernel, "onward", vmem(keep_two, near_two), [piece])
-    far_two = chip_swap(onward, 0, "two_far")
+    whole_zero_came = step(
+        assemble_kernel,
+        "assemble",
+        [(SMEM, order_came)] + vmem(zero_came, beyond_came),
+        [whole],
+        [dma((chips,))],
+    )
 
     pre_grad, pre_grad_send = step(
         slope_kernel,
@@ -477,31 +495,36 @@
     one = step(copy_kernel, "copy", vmem(one), like(one))
     one_near, one_across = chip_swap(one, 0, "one_near"), chip_swap(one, 1, "one_across")
 
-    chunks = (tuple(range(SPLIT)), tuple(range(SPLIT, 9)))
-    sizes = [SPLIT * depth // 2, ((9 - SPLIT) * depth + EXTRA) // 2]
-
-    def grad_outs(size):
-        return [shape((size, channels), bf16), shape((size, channels), f32)]
+    def sizes(taps):
+        return len(taps) * depth + (EXTRA if taps[-1] == 8 else 0)
+
+    def grad_outs(taps):
+        return [shape((sizes(taps), channels), bf16), shape((sizes(taps), channels), f32)]
 
     def grad_scratch(taps):
-        extra = EXTRA if taps[-1] == 8 else 0
         return [
-            pltpu.VMEM((len(taps) * depth + extra, channels), f32),
+            pltpu.VMEM((sizes(taps), channels), f32),
             pltpu.VMEM((2, len(taps) * depth, half), bf16),
         ]
 
-    costs[-1] = LATE
+    def parts(ends):
+        return [tuple(range(start, end)) for start, end in zip((0,) + ends[:-1], ends)]
+
+    def add(left, right):
+        return step(add_kernel, "add", vmem(left, right), like(left))
+
+    phase[0] = "late"
     grads = []
-    for at, taps in enumerate(chunks):
+    for at, taps in enumerate(parts(PARTS_ONE)):
         send, keep = step(
             functools.partial(grad_one_kernel, taps),
             "grad_one_" + "ab"[at],
-            [(SMEM, low)] + vmem(pre_grad, pre_grad_came, whole_zero, whole_zero_came),
-            grad_outs(sizes[at]),
+            vmem(pre_grad, pre_grad_came, whole_zero, whole_zero_came),
+            grad_outs(taps),
             grad_scratch(taps),
         )
-        grads.append((keep, group_swap(send, 1, "one_A" + "ab"[at])))
-
+        grads.append((send, keep))
+    near_a = group_send(grads[0][0], "in", "one_a")
     one_near, one_across, pre_grad, pre_grad_send = step(
         copy_kernel,
         "copy",
@@ -509,10 +532,13 @@
         like(one_near, one_across, pre_grad, pre_grad_send),
     )
     one_beyond = chip_swap(one_near, 1, "one_beyond")
-    mine_a = step(add_kernel, "add", vmem(*grads[0]), like(grads[0][1]))
-    far_a = group_swap(mine_a, 2, "one_Ba")
-    mine_b = step(add_kernel, "add", vmem(*grads[1]), like(grads[1][1]))
-    far_b = group_swap(mine_b, 2, "one_Bb")
+
+    send, keep_one = back("back_one", 0, (2,), pre_grad, pre_grad_send, own_one, other_one)
+    send_one = send
+    send_b = step(copy_kernel, "copy", vmem(grads[1][0]), like(grads[1][0]))
+    near_b = group_send(send_b, "in", "one_b")
+    mine_a = add(grads[0][1], near_a)
+    far_a = group_send(mine_a, "middle", "one_a")
 
     whole_one = step(
         assemble_kernel,
@@ -522,20 +548,59 @@
         [dma((chips,))],
     )
     whole_one_came = core_swap(whole_one, "one_pair")
+    send_a, keep_a, send_b, keep_b = step(
+        grad_two_kernel,
+        "grad_two",
+        [(SMEM, core_at)] + vmem(cotangent, whole_one, whole_one_came),
+        [out for taps in parts(PARTS_TWO) for out in grad_outs(taps)],
+        grad_scratch(tuple(range(9))),
+    )
+    near_a = group_send(send_a, "in", "two_a")
+    send_one = step(copy_kernel, "copy", vmem(send_one), like(send_one))
+    near_one = chip_swap(send_one, 1, "one_near")
     out_own, out_other = step(
         conv_two_kernel, "conv_two", vmem(whole_one, own_two, other_two), [plane, plane]
     )
+    mine_b = add(grads[1][1], near_b)
+    far_b = group_send(mine_b, "middle", "one_b")
+    onward = step(onward_kernel, "onward", vmem(keep_one, near_one), [piece])
+    half_a = add(mine_a, far_a)
+    rest_a = group_send(half_a, "out", "one_a")
+    send_b = step(copy_kernel, "copy", vmem(send_b), like(send_b))
+    near_b = group_send(send_b, "in", "two_b")
+    mine_two_a = add(keep_a, near_a)
+    far_two_a = group_send(mine_two_a, "middle", "two_a")
+    half_b = add(mine_b, far_b)
+    rest_b = group_send(half_b, "out", "one_b")
+    rest_a = step(copy_kernel, "copy", vmem(rest_a), like(rest_a))
+    mine_two_b = add(keep_b, near_b)
+    far_two_b = group_send(mine_two_b, "middle", "two_b")
+    onward = step(copy_kernel, "copy", vmem(onward), like(onward))
+    far_one = chip_swap(onward, 0, "one_far")
+    half_two_a = add(mine_two_a, far_two_a)
+    rest_two_a = group_send(half_two_a, "out", "two_a")
+
+    def finish(name, pieces):
+        kernel_grad, bias_grad = step(
+            finish_kernel,
+            name,
+            [(SMEM, inner)] + vmem(*pieces),
+            [shape((rows, channels), f32), shape((1, depth), f32)],
+            [pltpu.VMEM((rows + EXTRA, channels), f32), dma((len(pieces) // 2,))],
+            out_specs=[ANY, VMEM],
+        )
+        return kernel_grad.reshape(9, depth, channels), bias_grad.reshape(depth)
+
+    kernel_grad_one, bias_grad_one = finish("finish_one", [half_a, rest_a, half_b, rest_b])
+    out_other = step(copy_kernel, "copy", vmem(out_other), [plane])
     out_came = core_swap(out_other, "out_pair")
-
-    size = sum(sizes)
-    send, keep_a, keep_b = step(
-        grad_two_kernel,
-        "grad_two",
-        [(SMEM, low), (SMEM, core_at)] + vmem(cotangent, whole_one, whole_one_came),
-        [shape((size, channels), bf16)] + [shape((count, channels), f32) for count in sizes],
-        grad_scratch(tuple(range(9))),
-    )
-    near = group_swap(send, 1, "two_A")
+    own, other = step(
+        sum_kernel, "sum", [(SMEM, core_at)] + vmem(keep_one, near_one, far_one), [plane, plane]
+    )
+    other = core_swap(other, "field_pair")
+    half_two_b = add(mine_two_b, far_two_b)
+    rest_two_b = group_send(half_two_b, "out", "two_b")
+    rest_two_a = step(copy_kernel, "copy", vmem(rest_two_a), like(rest_two_a))
     output = step(
         output_kernel,
         "output",
@@ -545,46 +610,6 @@
         [pltpu.VMEM((depth, pixels), bf16), dma],
         out_specs=[ANY],
     )
-
-    send, keep_one = back("back_one", 0, pre_grad, pre_grad_send, own_one, other_one)
-    near_one = chip_swap(send, 1, "one_near")
-
-    half_one = step(
-        join_kernel, "join", vmem(mine_a, far_a, mine_b, far_b), [shape((size, channels), bf16)]
-    )
-    rest_one = group_swap(half_one, 1, "one_C")
-    mine_a, mine_b = step(
-        add_split_kernel,
-        "add",
-        vmem(keep_a, keep_b, near),
-        [shape((count, channels), bf16) for count in sizes],
-    )
-    far_a = group_swap(mine_a, 2, "two_Ba")
-    far_b = group_swap(mine_b, 2, "two_Bb")
-
-    def finish(name, pieces):
-        kernel_grad, bias_grad = step(
-            functools.partial(finish_kernel, sizes),
-            name,
-            [(SMEM, low)] + vmem(*pieces),
-            [shape((rows, channels), f32), shape((1, depth), f32)],
-            [pltpu.VMEM((rows + EXTRA, channels), f32), dma],
-            out_specs=[ANY, VMEM],
-        )
-        return kernel_grad.reshape(9, depth, channels), bias_grad.reshape(depth)
-
-    onward = step(onward_kernel, "onward", vmem(keep_one, near_one), [piece])
-    far_one = chip_swap(onward, 0, "one_far")
-    kernel_grad_one, bias_grad_one = finish("finish_one", [half_one, rest_one])
-    own, other = step(
-        sum_kernel, "sum", [(SMEM, core_at)] + vmem(keep_one, near_one, far_one), [plane, plane]
-    )
-    other = core_swap(other, "field_pair")
-
-    half_a = step(add_kernel, "add", vmem(mine_a, far_a), like(mine_a))
-    rest_a = group_swap(half_a, 1, "two_Ca")
-    half_b = step(add_kernel, "add", vmem(mine_b, far_b), like(mine_b))
-    rest_b = group_swap(half_b, 1, "two_Cb")
     grad_field = step(
         field_grad_kernel,
         "field_grad",
@@ -593,7 +618,9 @@
         [pltpu.VMEM((depth, pixels), f32), dma],
         out_specs=[ANY],
     )
-    kernel_grad_two, bias_grad_two = finish("finish_two", [half_a, rest_a, half_b, rest_b])
+    kernel_grad_two, bias_grad_two = finish(
+        "finish_two", [half_two_a, rest_two_a, half_two_b, rest_two_b]
+    )
     return output, grad_field, kernel_grad_one, bias_grad_one, kernel_grad_two, bias_grad_two
 
 

time: 128 us -> 121 us (0.945)
  waiting for transfers between devices: 59.6 us -> 37.8 us
  starting transfers between devices: 28.8 us -> 37.3 us
  local copies, waits for them, and re-layouts: 1.63 us -> 4.56 us
  Pallas kernels: 37.2 us -> 40 us
    ppermute x29 -> x33, waiting for transfers between devices: 59.6 us -> 37.8 us  [swap(): return lax.ppermute(values, axis, pairs)]
    ppermute x29 -> x33, starting transfers between devices: 28.8 us -> 37.3 us  [swap(): return lax.ppermute(values, axis, pairs)]
    unnamed x18 -> x38, local copies, waits for them, and re-layouts: 1.48 us -> 4.41 us
    pallas_call x28 -> x39, Pallas kernels: 37.2 us -> 40 us  [run(): pl.pallas_call(marked, name=name, out_shape=[SPACES[id(spec)](out.shape,...]
  transfers between devices with their start and end apart: 29 -> 33, of which waited for: 15 -> 14; matrix products, arithmetic and copies ran while one was open for 1% -> 1% of each run, Pallas kernels for 27% -> 30%
where the time goes in v3:
time: 121 us
  Pallas kernels  40 us (33%)
  waiting for transfers between devices  37.8 us (31%)
  starting transfers between devices  37.3 us (31%)
  local copies, waits for them, and re-layouts  4.56 us (4%)
    pallas_call x39, Pallas kernels, run(): pl.pallas_call(marked, name=name, out_shape=[SPACES[id(spec)](out.shape,...  40 us
    ppermute x33, waiting for transfers between devices, swap(): return lax.ppermute(values, axis, pairs)  37.8 us
    ppermute x33, starting transfers between devices, swap(): return lax.ppermute(values, axis, pairs)  37.3 us
    unnamed x38, local copies, waits for them, and re-layouts  4.41 us
  transfers between devices with their start and end apart: 33, of which 14 were waited for; matrix products, arithmetic and copies ran while one was open for 1% of the time, Pallas kernels for 30%

profile of v3, /device:TPU:0, one launch (start us, length us, event | category | flops | bytes accessed | tf_op | source)
XLA Modules:
  0.0 120.8 jit_solution(18291126508860783751)
XLA Ops:
  1.2 2.1 %field.1 = (bf16[80,2048]{1,0:T(8,128)(2,1)S(1)}, bf16[80,2048]{1,0:T(8,128)(2,1)S(1)}, bf16[80,2048]{1,0:T(8,128)(2,1)S(1)}, f32[8,128]{1,0:T(8,128)S(1)}) custom-call(s32[1]{0:T(128)} %bitcast.refs_0_, s32[32]{0:T(128)} %refs_1_.2, s32[32]{0:T(128)} %refs_2_.2, bf16[80,2048]{1,0:T(8,128)(2,1)} %refs_3_.1, bf16[80,8192]{1,0:T(8,128)(2,1)} %refs_4_.1, ...), custom_call_target="tpu_custom_call" | custom-call | flops 10000000000 | tf_op jit(solution)/shard_map/field/pallas_call | solution.py:331
  5.0 2.7 %collective-permute-start.1 = (bf16[1,160,1024]{2,1,0:T(8,128)(2,1)S(1)}, bf16[1,160,1024]{2,1,0:T(8,128)(2,1)S(1)}, u32[]{:S(2)}, u32[]{:S(2)}) collective-permute-start(bf16[1,160,1024]{2,1,0:T(8,128)(2,1)S(1)} %get-tuple-element.110.refs_0_), channel_id=1, source_target_pairs={{0,2},{1,5},{2,0},{3,7},{4,6},{5,1},{6,4},{7,3},{8,10},{9,13},{10,... | collective-permute-start | bytes 983048 | tf_op jit(solution)/shard_map/zero_near/ppermute | solution.py:366
  7.6 1.5 %collective-permute-start.2 = (bf16[1,160,1024]{2,1,0:T(8,128)(2,1)S(1)}, bf16[1,160,1024]{2,1,0:T(8,128)(2,1)S(1)}, u32[]{:S(2)}, u32[]{:S(2)}) collective-permute-start(bf16[1,160,1024]{2,1,0:T(8,128)(2,1)S(1)} %get-tuple-element.110.refs_0_), channel_id=1, source_target_pairs={{0,4},{1,3},{2,6},{3,1},{4,0},{5,7},{6,2},{7,5},{8,12},{9,11},{10,... | collective-permute-start | bytes 983048 | tf_op jit(solution)/shard_map/zero_across/ppermute | solution.py:366
  9.2 5.9 %back_two.1 = (bf16[1,160,1024]{2,1,0:T(8,128)(2,1)S(1)}, bf16[1,160,1024]{2,1,0:T(8,128)(2,1)S(1)}, f32[2,160,1024]{2,1,0:T(8,128)S(1)}, f32[8,128]{1,0:T(8,128)S(1)}) custom-call(s32[4]{0:T(128)S(1)} %get-tuple-element.209.refs_0_.refs_1_, bf16[80,2048]{1,0:T(8,128)(2,1)S(1)} %get-tuple-element.107.refs_1_, ...), custom_call_target="tpu_custom_call" | custom-call | flops 10000000000 | tf_op jit(solution)/shard_map/back_two/pallas_call | solution.py:331
  16.1 1.9 %collective-permute-start.6 = (bf16[1,160,1024]{2,1,0:T(8,128)(2,1)S(1)}, bf16[1,160,1024]{2,1,0:T(8,128)(2,1)S(1)}, u32[]{:S(2)}, u32[]{:S(2)}) collective-permute-start(bf16[1,160,1024]{2,1,0:T(8,128)(2,1)S(1)} %get-tuple-element.117), channel_id=1, source_target_pairs={{0,4},{1,3},{2,6},{3,1},{4,0},{5,7},{6,2},{7,5},{8,12},{9,11},{10,... | collective-permute-start | bytes 983048 | tf_op jit(solution)/shard_map/zero_beyond/ppermute | solution.py:366
  18.0 4.3 %collective-permute-done.7.refs_1_ = bf16[1,160,1024]{2,1,0:T(8,128)(2,1)S(1)} collective-permute-done((bf16[1,160,1024]{2,1,0:T(8,128)(2,1)S(1)}, bf16[1,160,1024]{2,1,0:T(8,128)(2,1)S(1)}, u32[]{:S(2)}, u32[]{:S(2)}) %collective-permute-start.7) | collective-permute-done | bytes 327712 | tf_op jit(solution)/shard_map/two_last/ppermute | solution.py:366
  23.1 4.1 %collective-permute-done.6.refs_0_ = bf16[1,160,1024]{2,1,0:T(8,128)(2,1)S(1)} collective-permute-done((bf16[1,160,1024]{2,1,0:T(8,128)(2,1)S(1)}, bf16[1,160,1024]{2,1,0:T(8,128)(2,1)S(1)}, u32[]{:S(2)}, u32[]{:S(2)}) %collective-permute-start.6) | collective-permute-done | bytes 327712 | tf_op jit(solution)/shard_map/zero_beyond/ppermute | solution.py:366
  27.3 4.1 %conv_one.1 = (bf16[640,1024]{1,0:T(8,128)(2,1)S(1)}, f32[80,1024]{1,0:T(8,128)S(1)}, f32[80,1024]{1,0:T(8,128)S(1)}, bf16[1,160,1024]{2,1,0:T(8,128)(2,1)S(1)}, f32[8,128]{1,0:T(8,128)S(1)}) custom-call(s32[1]{0:T(128)} %bitcast.refs_0_, s32[4]{0:T(128)S(1)} %get-tuple-element.209.refs_0_.refs_1_, bf16[3,160,1024]{2,1,0:T(8,128)(2,1)S(1)} %get-tuple-element.116.refs_2_, ...), custom_call_target="tpu_custom_call" | custom-call | flops 10000000000 | tf_op jit(solution)/shard_map/conv_one/pallas_call | solution.py:331
  35.8 3.5 %collective-permute-start.16 = (bf16[320,640]{1,0:T(8,128)(2,1)S(1)}, bf16[320,640]{1,0:T(8,128)(2,1)S(1)}, u32[]{:S(2)}, u32[]{:S(2)}) collective-permute-start(bf16[320,640]{1,0:T(8,128)(2,1)S(1)} %get-tuple-element.145), channel_id=1, source_target_pairs={{0,8},{24,16},{1,9},{25,17},{2,10},{26,18},{3,11},{27,19},{4,12},{... | collective-permute-start | bytes 1228808 | tf_op jit(solution)/shard_map/one_a_in/ppermute | solution.py:366
  39.3 1.6 %grad_one_b.1 = (bf16[416,640]{1,0:T(8,128)(2,1)S(1)}, f32[416,640]{1,0:T(8,128)S(1)}, f32[8,128]{1,0:T(8,128)S(1)}) custom-call(bf16[80,1024]{1,0:T(8,128)(2,1)S(1)} %get-tuple-element.135.refs_0_.refs_2_, bf16[80,1024]{1,0:T(8,128)(2,1)S(1)} %collective-permute-done.14.refs_1_, bf16[640,1024]{1,0:T(8,128)(2,1)S(1)} %get-tuple-element.137.refs_2_, ...), custom_call_target="tpu_custom_call" | custom-call | flops 20000000000 | tf_op jit(solution)/shard_map/grad_one_b/pallas_call | solution.py:331
  40.8 2.8 %collective-permute-done.12.refs_0_ = bf16[1,160,1024]{2,1,0:T(8,128)(2,1)S(1)} collective-permute-done((bf16[1,160,1024]{2,1,0:T(8,128)(2,1)S(1)}, bf16[1,160,1024]{2,1,0:T(8,128)(2,1)S(1)}, u32[]{:S(2)}, u32[]{:S(2)}) %collective-permute-start.12) | collective-permute-done | bytes 327712 | tf_op jit(solution)/shard_map/one_near/ppermute | solution.py:366
  44.0 5.3 %back_one.1 = (bf16[2,160,1024]{2,1,0:T(8,128)(2,1)S(1)}, f32[2,160,1024]{2,1,0:T(8,128)S(1)}, f32[8,128]{1,0:T(8,128)S(1)}) custom-call(s32[4]{0:T(128)S(1)} %get-tuple-element.209.refs_0_.refs_1_, bf16[80,1024]{1,0:T(8,128)(2,1)S(1)} %get-tuple-element.147.refs_1_, bf16[80,1024]{1,0:T(8,128)(2,1)S(1)} %get-tuple-element.148.refs_2_, ...), custom_call_target="tpu_custom_call" | custom-call | flops 20000000000 | tf_op jit(solution)/shard_map/back_one/pallas_call | solution.py:331
  51.9 3.5 %collective-permute-start.20 = (bf16[416,640]{1,0:T(8,128)(2,1)S(1)}, bf16[416,640]{1,0:T(8,128)(2,1)S(1)}, u32[]{:S(2)}, u32[]{:S(2)}) collective-permute-start(bf16[416,640]{1,0:T(8,128)(2,1)S(1)} %get-tuple-element.164), channel_id=1, source_target_pairs={{0,8},{24,16},{1,9},{25,17},{2,10},{26,18},{3,11},{27,19},{4,12},{... | collective-permute-start | bytes 1597448 | tf_op jit(solution)/shard_map/one_b_in/ppermute | solution.py:366
  56.3 2.6 %grad_two.1 = (bf16[400,640]{1,0:T(8,128)(2,1)S(1)}, f32[400,640]{1,0:T(8,128)S(1)}, bf16[336,640]{1,0:T(8,128)(2,1)S(1)}, f32[336,640]{1,0:T(8,128)S(1)}, f32[8,128]{1,0:T(8,128)S(1)}) custom-call(s32[1]{0:T(128)} %bitcast.refs_0_, bf16[80,2048]{1,0:T(8,128)(2,1)S(1)} %copy-done.2, bf16[640,1024]{1,0:T(8,128)(2,1)S(1)} %get-tuple-element.153.refs_2_.refs_0_, ...), custom_call_target="tpu_custom_call" | custom-call | flops 20000000000 | tf_op jit(solution)/shard_map/grad_two/pallas_call | solution.py:331
  60.3 4.1 %collective-permute-start.23 = (bf16[400,640]{1,0:T(8,128)(2,1)S(1)}, bf16[400,640]{1,0:T(8,128)(2,1)S(1)}, u32[]{:S(2)}, u32[]{:S(2)}) collective-permute-start(bf16[400,640]{1,0:T(8,128)(2,1)S(1)} %get-tuple-element.171), channel_id=1, source_target_pairs={{0,8},{24,16},{1,9},{25,17},{2,10},{26,18},{3,11},{27,19},{4,12},{... | collective-permute-start | bytes 1536008 | tf_op jit(solution)/shard_map/two_a_in/ppermute | solution.py:366
  64.4 4.3 %conv_two.1 = (f32[80,1024]{1,0:T(8,128)S(1)}, f32[80,1024]{1,0:T(8,128)S(1)}, f32[8,128]{1,0:T(8,128)S(1)}) custom-call(bf16[640,1024]{1,0:T(8,128)(2,1)S(1)} %get-tuple-element.153.refs_2_.refs_0_, bf16[720,640]{1,0:T(8,128)(2,1)S(1)} %bitcast.15, bf16[720,640]{1,0:T(8,128)(2,1)} %collective-permute-done.3.refs_4_.refs_2_, ...), custom_call_target="tpu_custom_call" | custom-call | flops 20000000000 | tf_op jit(solution)/shard_map/conv_two/pallas_call | solution.py:331
  73.4 6.2 %collective-permute-start.26 = (bf16[336,640]{1,0:T(8,128)(2,1)}, bf16[336,640]{1,0:T(8,128)(2,1)S(1)}, u32[]{:S(2)}, u32[]{:S(2)}) collective-permute-start(bf16[336,640]{1,0:T(8,128)(2,1)} %get-tuple-element.182), channel_id=1, source_target_pairs={{0,8},{24,16},{1,9},{25,17},{2,10},{26,18},{3,11},{27,19},{4,12},{... | collective-permute-start | bytes 1290248 | tf_op jit(solution)/shard_map/two_b_in/ppermute | solution.py:366
  82.0 3.2 %collective-permute-done.21.refs_0_ = bf16[320,640]{1,0:T(8,128)(2,1)} collective-permute-done((bf16[320,640]{1,0:T(8,128)(2,1)}, bf16[320,640]{1,0:T(8,128)(2,1)}, u32[]{:S(2)}, u32[]{:S(2)}) %collective-permute-start.21) | collective-permute-done | bytes 409632 | tf_op jit(solution)/shard_map/one_a_out/ppermute | solution.py:366
  86.2 2.1 %collective-permute-done.26.refs_1_ = bf16[336,640]{1,0:T(8,128)(2,1)S(1)} collective-permute-done((bf16[336,640]{1,0:T(8,128)(2,1)}, bf16[336,640]{1,0:T(8,128)(2,1)S(1)}, u32[]{:S(2)}, u32[]{:S(2)}) %collective-permute-start.26) | collective-permute-done | bytes 430112 | tf_op jit(solution)/shard_map/two_b_in/ppermute | solution.py:366
  91.6 6.0 %collective-permute-done.24.refs_4_ = bf16[416,640]{1,0:T(8,128)(2,1)S(1)} collective-permute-done((bf16[416,640]{1,0:T(8,128)(2,1)S(1)}, bf16[416,640]{1,0:T(8,128)(2,1)S(1)}, u32[]{:S(2)}, u32[]{:S(2)}) %collective-permute-start.24) | collective-permute-done | bytes 532512 | tf_op jit(solution)/shard_map/one_b_out/ppermute | solution.py:366
  97.7 2.4 %finish_one.1 = (f32[720,640]{1,0:T(8,128)}, f32[1,80]{1,0:T(1,128)S(1)}, f32[8,128]{1,0:T(8,128)S(1)}) custom-call(s32[1]{0:T(128)} %bitcast.3.refs_0_, bf16[320,640]{1,0:T(8,128)(2,1)} %get-tuple-element.168.refs_1_, bf16[320,640]{1,0:T(8,128)(2,1)S(1)} %get-tuple-element.177.refs_2_, bf16[416,640]{1,0:T(8,128)(2,1)S(1)} %get-tuple-element.178.refs_3_, ...), custom_call_target="tpu_custom_call" | custom-call | flops 20000000000 | tf_op jit(solution)/shard_map/finish_one/pallas_call | solution.py:331
  103.0 7.8 %collective-permute-done.28.refs_0_ = bf16[400,640]{1,0:T(8,128)(2,1)S(1)} collective-permute-done((bf16[400,640]{1,0:T(8,128)(2,1)S(1)}, bf16[400,640]{1,0:T(8,128)(2,1)S(1)}, u32[]{:S(2)}, u32[]{:S(2)}) %collective-permute-start.28) | collective-permute-done | bytes 512032 | tf_op jit(solution)/shard_map/two_a_out/ppermute | solution.py:366
  113.9 4.4 %collective-permute-done.32.refs_4_ = bf16[336,640]{1,0:T(8,128)(2,1)S(1)} collective-permute-done((bf16[336,640]{1,0:T(8,128)(2,1)S(1)}, bf16[336,640]{1,0:T(8,128)(2,1)S(1)}, u32[]{:S(2)}, u32[]{:S(2)}) %collective-permute-start.32) | collective-permute-done | bytes 430112 | tf_op jit(solution)/shard_map/two_b_out/ppermute | solution.py:366
  118.3 2.0 %finish_two.1 = (f32[720,640]{1,0:T(8,128)}, f32[1,80]{1,0:T(1,128)S(1)}, f32[8,128]{1,0:T(8,128)}) custom-call(s32[1]{0:T(128)} %bitcast.3.refs_0_, bf16[400,640]{1,0:T(8,128)(2,1)S(1)} %get-tuple-element.189.refs_1_, bf16[400,640]{1,0:T(8,128)(2,1)S(1)} %get-tuple-element.203.refs_2_, bf16[336,640]{1,0:T(8,128)(2,1)S(1)} %get-tuple-element.204.refs_3_, ...), custom_call_target="tpu_custom_call" | custom-call | flops 20000000000 | tf_op jit(solution)/shard_map/finish_two/pallas_call | solution.py:331
  (122 shorter events, 31.4 us)
Async XLA Ops:
  3.4 12.6 %collective-permute-start.4 = (bf16[720,640]{1,0:T(8,128)(2,1)S(1)}, bf16[720,640]{1,0:T(8,128)(2,1)S(1)}, u32[]{:S(2)}, u32[]{:S(2)}) collective-permute-start(bf16[720,640]{1,0:T(8,128)(2,1)S(1)} %bitcast.11), channel_id=1, source_target_pairs={{0,1},{1,0},{2,3},{3,2},{4,5},{5,4},{6,7},{7,6},{8,9},{9,8},{10,11... | collective-permute-start | bytes 2764808 | tf_op jit(solution)/shard_map/kernel_one/ppermute | solution.py:366
  3.9 11.8 %collective-permute-start.5 = (bf16[80,128]{1,0:T(8,128)(2,1)S(1)}, bf16[80,128]{1,0:T(8,128)(2,1)S(1)}, u32[]{:S(2)}, u32[]{:S(2)}) collective-permute-start(bf16[80,128]{1,0:T(8,128)(2,1)S(1)} %broadcast_in_dim.4.refs_6_), channel_id=1, source_target_pairs={{0,1},{1,0},{2,3},{3,2},{4,5},{5,4},{6,7},{7,6},{8,9},{9,8},{10,11... | collective-permute-start | bytes 61448 | tf_op jit(solution)/shard_map/bias/ppermute | solution.py:366
  5.0 10.8 %collective-permute-start.1 = (bf16[1,160,1024]{2,1,0:T(8,128)(2,1)S(1)}, bf16[1,160,1024]{2,1,0:T(8,128)(2,1)S(1)}, u32[]{:S(2)}, u32[]{:S(2)}) collective-permute-start(bf16[1,160,1024]{2,1,0:T(8,128)(2,1)S(1)} %get-tuple-element.110.refs_0_), channel_id=1, source_target_pairs={{0,2},{1,5},{2,0},{3,7},{4,6},{5,1},{6,4},{7,3},{8,10},{9,13},{10,... | collective-permute-start | bytes 983048 | tf_op jit(solution)/shard_map/zero_near/ppermute | solution.py:366
  16.1 11.1 %collective-permute-start.6 = (bf16[1,160,1024]{2,1,0:T(8,128)(2,1)S(1)}, bf16[1,160,1024]{2,1,0:T(8,128)(2,1)S(1)}, u32[]{:S(2)}, u32[]{:S(2)}) collective-permute-start(bf16[1,160,1024]{2,1,0:T(8,128)(2,1)S(1)} %get-tuple-element.117), channel_id=1, source_target_pairs={{0,4},{1,3},{2,6},{3,1},{4,0},{5,7},{6,2},{7,5},{8,12},{9,11},{10,... | collective-permute-start | bytes 983048 | tf_op jit(solution)/shard_map/zero_beyond/ppermute | solution.py:366
  18.0 13.5 %collective-permute-start.10 = (bf16[3,160,1024]{2,1,0:T(8,128)(2,1)S(1)}, bf16[3,160,1024]{2,1,0:T(8,128)(2,1)S(1)}, u32[]{:S(2)}, u32[]{:S(2)}) collective-permute-start(bf16[3,160,1024]{2,1,0:T(8,128)(2,1)S(1)} %get-tuple-element.116.refs_2_), channel_id=1, source_target_pairs={{0,1},{1,0},{2,3},{3,2},{4,5},{5,4},{6,7},{7,6},{8,9},{9,8},{10,11... | collective-permute-start | bytes 2949128 | tf_op jit(solution)/shard_map/zero_pair/ppermute | solution.py:366
  22.4 10.4 %collective-permute-start.8 = (bf16[1,160,1024]{2,1,0:T(8,128)(2,1)S(1)}, bf16[1,160,1024]{2,1,0:T(8,128)(2,1)S(1)}, u32[]{:S(2)}, u32[]{:S(2)}) collective-permute-start(bf16[1,160,1024]{2,1,0:T(8,128)(2,1)S(1)} %get-tuple-element.127), channel_id=1, source_target_pairs={{0,4},{1,3},{2,6},{3,1},{4,0},{5,7},{6,2},{7,5},{8,12},{9,11},{10,... | collective-permute-start | bytes 983048 | tf_op jit(solution)/shard_map/two_near/ppermute | solution.py:366
  23.0 9.8 %collective-permute-start.9 = (bf16[1,160,1024]{2,1,0:T(8,128)(2,1)S(1)}, bf16[1,160,1024]{2,1,0:T(8,128)(2,1)S(1)}, u32[]{:S(2)}, u32[]{:S(2)}) collective-permute-start(bf16[1,160,1024]{2,1,0:T(8,128)(2,1)S(1)} %get-tuple-element.128), channel_id=1, source_target_pairs={{0,2},{1,5},{2,0},{3,7},{4,6},{5,1},{6,4},{7,3},{8,10},{9,13},{10,... | collective-permute-start | bytes 983048 | tf_op jit(solution)/shard_map/two_far/ppermute | solution.py:366
  33.3 10.3 %collective-permute-start.12 = (bf16[1,160,1024]{2,1,0:T(8,128)(2,1)S(1)}, bf16[1,160,1024]{2,1,0:T(8,128)(2,1)S(1)}, u32[]{:S(2)}, u32[]{:S(2)}) collective-permute-start(bf16[1,160,1024]{2,1,0:T(8,128)(2,1)S(1)} %get-tuple-element.134.refs_1_), channel_id=1, source_target_pairs={{0,2},{1,5},{2,0},{3,7},{4,6},{5,1},{6,4},{7,3},{8,10},{9,13},{10,... | collective-permute-start | bytes 983048 | tf_op jit(solution)/shard_map/one_near/ppermute | solution.py:366
  35.8 13.6 %collective-permute-start.16 = (bf16[320,640]{1,0:T(8,128)(2,1)S(1)}, bf16[320,640]{1,0:T(8,128)(2,1)S(1)}, u32[]{:S(2)}, u32[]{:S(2)}) collective-permute-start(bf16[320,640]{1,0:T(8,128)(2,1)S(1)} %get-tuple-element.145), channel_id=1, source_target_pairs={{0,8},{24,16},{1,9},{25,17},{2,10},{26,18},{3,11},{27,19},{4,12},{... | collective-permute-start | bytes 1228808 | tf_op jit(solution)/shard_map/one_a_in/ppermute | solution.py:366
  51.9 16.7 %collective-permute-start.20 = (bf16[416,640]{1,0:T(8,128)(2,1)S(1)}, bf16[416,640]{1,0:T(8,128)(2,1)S(1)}, u32[]{:S(2)}, u32[]{:S(2)}) collective-permute-start(bf16[416,640]{1,0:T(8,128)(2,1)S(1)} %get-tuple-element.164), channel_id=1, source_target_pairs={{0,8},{24,16},{1,9},{25,17},{2,10},{26,18},{3,11},{27,19},{4,12},{... | collective-permute-start | bytes 1597448 | tf_op jit(solution)/shard_map/one_b_in/ppermute | solution.py:366
  55.4 15.1 %collective-permute-start.18 = (bf16[320,640]{1,0:T(8,128)(2,1)S(1)}, bf16[320,640]{1,0:T(8,128)(2,1)S(1)}, u32[]{:S(2)}, u32[]{:S(2)}) collective-permute-start(bf16[320,640]{1,0:T(8,128)(2,1)S(1)} %get-tuple-element.160.refs_0_), channel_id=1, source_target_pairs={{8,16},{16,8},{9,17},{17,9},{10,18},{18,10},{11,19},{19,11},{12,20... | collective-permute-start | bytes 1228808 | tf_op jit(solution)/shard_map/one_a_middle/ppermute | solution.py:366
  59.8 10.6 %collective-permute-start.19 = (bf16[2,160,1024]{2,1,0:T(8,128)(2,1)S(1)}, bf16[2,160,1024]{2,1,0:T(8,128)(2,1)S(1)}, u32[]{:S(2)}, u32[]{:S(2)}) collective-permute-start(bf16[2,160,1024]{2,1,0:T(8,128)(2,1)S(1)} %get-tuple-element.162), channel_id=1, source_target_pairs={{0,4},{1,3},{2,6},{3,1},{4,0},{5,7},{6,2},{7,5},{8,12},{9,11},{10,... | collective-permute-start | bytes 1966088 | tf_op jit(solution)/shard_map/one_near/ppermute | solution.py:366
  60.3 19.4 %collective-permute-start.23 = (bf16[400,640]{1,0:T(8,128)(2,1)S(1)}, bf16[400,640]{1,0:T(8,128)(2,1)S(1)}, u32[]{:S(2)}, u32[]{:S(2)}) collective-permute-start(bf16[400,640]{1,0:T(8,128)(2,1)S(1)} %get-tuple-element.171), channel_id=1, source_target_pairs={{0,8},{24,16},{1,9},{25,17},{2,10},{26,18},{3,11},{27,19},{4,12},{... | collective-permute-start | bytes 1536008 | tf_op jit(solution)/shard_map/two_a_in/ppermute | solution.py:366
  69.5 11.0 %collective-permute-start.22 = (bf16[416,640]{1,0:T(8,128)(2,1)S(1)}, bf16[416,640]{1,0:T(8,128)(2,1)S(1)}, u32[]{:S(2)}, u32[]{:S(2)}) collective-permute-start(bf16[416,640]{1,0:T(8,128)(2,1)S(1)} %get-tuple-element.169.refs_0_), channel_id=1, source_target_pairs={{8,16},{16,8},{9,17},{17,9},{10,18},{18,10},{11,19},{19,11},{12,20... | collective-permute-start | bytes 1597448 | tf_op jit(solution)/shard_map/one_b_middle/ppermute | solution.py:366
  71.4 13.8 %collective-permute-start.21 = (bf16[320,640]{1,0:T(8,128)(2,1)}, bf16[320,640]{1,0:T(8,128)(2,1)}, u32[]{:S(2)}, u32[]{:S(2)}) collective-permute-start(bf16[320,640]{1,0:T(8,128)(2,1)} %get-tuple-element.168.refs_1_), channel_id=1, source_target_pairs={{8,0},{16,24},{9,1},{17,25},{10,2},{18,26},{11,3},{19,27},{12,4},{... | collective-permute-start | bytes 1228808 | tf_op jit(solution)/shard_map/one_a_out/ppermute | solution.py:366
  73.4 14.8 %collective-permute-start.26 = (bf16[336,640]{1,0:T(8,128)(2,1)}, bf16[336,640]{1,0:T(8,128)(2,1)S(1)}, u32[]{:S(2)}, u32[]{:S(2)}) collective-permute-start(bf16[336,640]{1,0:T(8,128)(2,1)} %get-tuple-element.182), channel_id=1, source_target_pairs={{0,8},{24,16},{1,9},{25,17},{2,10},{26,18},{3,11},{27,19},{4,12},{... | collective-permute-start | bytes 1290248 | tf_op jit(solution)/shard_map/two_b_in/ppermute | solution.py:366
  79.8 10.4 %collective-permute-start.25 = (bf16[400,640]{1,0:T(8,128)(2,1)S(1)}, bf16[400,640]{1,0:T(8,128)(2,1)S(1)}, u32[]{:S(2)}, u32[]{:S(2)}) collective-permute-start(bf16[400,640]{1,0:T(8,128)(2,1)S(1)} %get-tuple-element.179.refs_0_), channel_id=1, source_target_pairs={{8,16},{16,8},{9,17},{17,9},{10,18},{18,10},{11,19},{19,11},{12,20... | collective-permute-start | bytes 1536008 | tf_op jit(solution)/shard_map/two_a_middle/ppermute | solution.py:366
  80.6 17.0 %collective-permute-start.24 = (bf16[416,640]{1,0:T(8,128)(2,1)S(1)}, bf16[416,640]{1,0:T(8,128)(2,1)S(1)}, u32[]{:S(2)}, u32[]{:S(2)}) collective-permute-start(bf16[416,640]{1,0:T(8,128)(2,1)S(1)} %get-tuple-element.178.refs_3_), channel_id=1, source_target_pairs={{8,0},{16,24},{9,1},{17,25},{10,2},{18,26},{11,3},{19,27},{12,4},{... | collective-permute-start | bytes 1597448 | tf_op jit(solution)/shard_map/one_b_out/ppermute | solution.py:366
  88.4 13.2 %collective-permute-start.29 = (bf16[336,640]{1,0:T(8,128)(2,1)S(1)}, bf16[336,640]{1,0:T(8,128)(2,1)S(1)}, u32[]{:S(2)}, u32[]{:S(2)}) collective-permute-start(bf16[336,640]{1,0:T(8,128)(2,1)S(1)} %get-tuple-element.190.refs_0_), channel_id=1, source_target_pairs={{8,16},{16,8},{9,17},{17,9},{10,18},{18,10},{11,19},{19,11},{12,20... | collective-permute-start | bytes 1290248 | tf_op jit(solution)/shard_map/two_b_middle/ppermute | solution.py:366
  89.3 11.4 %collective-permute-start.30 = (bf16[1,160,1024]{2,1,0:T(8,128)(2,1)S(1)}, bf16[1,160,1024]{2,1,0:T(8,128)(2,1)S(1)}, u32[]{:S(2)}, u32[]{:S(2)}) collective-permute-start(bf16[1,160,1024]{2,1,0:T(8,128)(2,1)S(1)} %get-tuple-element.191), channel_id=1, source_target_pairs={{0,2},{1,5},{2,0},{3,7},{4,6},{5,1},{6,4},{7,3},{8,10},{9,13},{10,... | collective-permute-start | bytes 983048 | tf_op jit(solution)/shard_map/one_far/ppermute | solution.py:366
  90.3 20.5 %collective-permute-start.28 = (bf16[400,640]{1,0:T(8,128)(2,1)S(1)}, bf16[400,640]{1,0:T(8,128)(2,1)S(1)}, u32[]{:S(2)}, u32[]{:S(2)}) collective-permute-start(bf16[400,640]{1,0:T(8,128)(2,1)S(1)} %get-tuple-element.189.refs_1_), channel_id=1, source_target_pairs={{8,0},{16,24},{9,1},{17,25},{10,2},{18,26},{11,3},{19,27},{12,4},{... | collective-permute-start | bytes 1536008 | tf_op jit(solution)/shard_map/two_a_out/ppermute | solution.py:366
  100.1 10.8 %collective-permute-start.27 = (f32[80,1024]{1,0:T(8,128)S(1)}, f32[80,1024]{1,0:T(8,128)S(1)}, u32[]{:S(2)}, u32[]{:S(2)}) collective-permute-start(f32[80,1024]{1,0:T(8,128)S(1)} %get-tuple-element.188), channel_id=1, source_target_pairs={{0,1},{1,0},{2,3},{3,2},{4,5},{5,4},{6,7},{7,6},{8,9},{9,8},{10,11... | collective-permute-start | bytes 983048 | tf_op jit(solution)/shard_map/out_pair/ppermute | solution.py:366
  101.5 11.3 %collective-permute-start.31 = (f32[80,1024]{1,0:T(8,128)S(1)}, f32[80,1024]{1,0:T(8,128)S(1)}, u32[]{:S(2)}, u32[]{:S(2)}) collective-permute-start(f32[80,1024]{1,0:T(8,128)S(1)} %get-tuple-element.198), channel_id=1, source_target_pairs={{0,1},{1,0},{2,3},{3,2},{4,5},{5,4},{6,7},{7,6},{8,9},{9,8},{10,11... | collective-permute-start | bytes 983048 | tf_op jit(solution)/shard_map/field_pair/ppermute | solution.py:366
  101.7 16.6 %collective-permute-start.32 = (bf16[336,640]{1,0:T(8,128)(2,1)S(1)}, bf16[336,640]{1,0:T(8,128)(2,1)S(1)}, u32[]{:S(2)}, u32[]{:S(2)}) collective-permute-start(bf16[336,640]{1,0:T(8,128)(2,1)S(1)} %get-tuple-element.204.refs_3_), channel_id=1, source_target_pairs={{8,0},{16,24},{9,1},{17,25},{10,2},{18,26},{11,3},{19,27},{12,4},{... | collective-permute-start | bytes 1290248 | tf_op jit(solution)/shard_map/two_b_out/ppermute | solution.py:366
  (27 other events, 117.6 us)

commit v4 on v3

--- a/solution.py
+++ b/solution.py
@@ -11,13 +11,10 @@
 f32 = jnp.float32
 offsets = [(row, col) for row in (-1, 0, 1) for col in (-1, 0, 1)]
 VMEM_LIMIT = 20 << 20
-COSTS = {
-    "early": {"big": 10**10, "small": 0},
-    "late": {"big": 2 * 10**10, "small": 10**9},
-}
+COSTS = {'early': {'big': 10000000000, 'small': 0, 'slope': 0}, 'late': {'big': 20000000000, 'small': 500000000, 'assemble_one': 30000000000, 'copy': 0, 'add_one_a': 100000000, 'assemble_one_came': 500000000, 'add_one_b': 10000000000, 'copy_6': 1000000000, 'add_one_a_half': 1000000000, 'add_one_b_half': 500000000, 'copy_7': 3000000000, 'back_one': 30000000000, 'conv_two': 100000000, 'grad_one_b': 1000000000, 'copy_beyond_one': 100000000, 'output': 100000000000, 'copy_10': 30000000000, 'field_grad': 10000000000, 'finish_two': 100000000000, 'sum': 1000000000, 'join_one': 30000000000, 'finish_one': 10000000000, 'add_two_a': 1000000000, 'add_two_b_half': 100000000, 'onward_2': 0, 'grad_one_a': 500000000}}
 SMALL = ("place", "copy", "add", "join", "onward", "sum", "assemble")
 EXTRA = 16
-PARTS_ONE, PARTS_TWO = (4, 9), (5, 9)
+PARTS_ONE, PARTS_TWO = (5, 9), (5, 9)
 TILE = 256
 CONV_TILE = 512
 
@@ -209,16 +206,15 @@
         grad[rows:, :] = jnp.zeros((EXTRA, grad.shape[1]), f32)
         grad[rows:, :depth] = sums
     base = 0
-    for send, keep in outs:
-        size = keep.shape[0]
-        keep[...] = grad[base : base + size, :]
-        send[...] = grad[base : base + size, :].astype(bf16)
+    for out in outs:
+        size = out.shape[0]
+        out[...] = grad[base : base + size, :].astype(bf16)
         base += size
 
 
-def grad_one_kernel(taps, own, came, whole, whole_came, send, keep, grad, stacks):
+def grad_one_kernel(taps, own, came, whole, whole_came, out, grad, stacks):
     parts = (own[...], whole), (came[...], whole_came)
-    write_grad(taps, parts, ((send, keep),), grad, stacks)
+    write_grad(taps, parts, (out,), grad, stacks)
 
 
 def grad_two_kernel(core, cotangent, whole, whole_came, *refs):
@@ -228,7 +224,7 @@
         cotangent[:, pl.ds(pl.multiple_of(at * half, 128), half)] for at in (core[0], 1 - core[0])
     )
     parts = (own, whole), (came, whole_came)
-    write_grad(tuple(range(9)), parts, list(zip(outs[0::2], outs[1::2])), grad, stacks)
+    write_grad(tuple(range(9)), parts, outs, grad, stacks)
 
 
 def copy_kernel(*refs):
@@ -240,10 +236,11 @@
     out[...] = (left[...].astype(f32) + right[...].astype(f32)).astype(bf16)
 
 
-def join_kernel(own, near, across, send, field, joined, *outs):
+def join_kernel(own, near, across, *refs):
+    others, (joined, *outs) = refs[: len(refs) // 2 - 1], refs[len(refs) // 2 - 1 :]
     for at, block in enumerate((own, near, across)):
         joined[at] = block[0]
-    for values, out in zip((near, send, field), outs):
+    for values, out in zip((near, *others), outs):
         out[...] = values[...]
 
 
@@ -403,7 +400,7 @@
     def step(body, name, ins, outs, scratch=(), out_specs=None, also=()):
         after = marks[-1:] + list(also)
         costs = COSTS[phase[0]]
-        cost = costs.get(name, costs["small" if name in SMALL else "big"])
+        cost = costs.get(name, costs["small" if name.split("_")[0] in SMALL else "big"])
         *results, mark = run(body, name, ins, outs, scratch, out_specs, after, cost)
         marks.append(mark)
         return results[0] if len(results) == 1 else results
@@ -450,20 +447,20 @@
 
     send, last, keep_two = back("back_two", half, (1, 1), keep, came, own_two, other_two)
     last_two = chip_swap(last, 1, "two_last")
-    zero, zero_near, send, field = step(
+    zero, zero_near, send = step(
         join_kernel,
-        "join",
-        vmem(zero, zero_near, zero_across, send, field),
-        [shape((3, block, half), bf16)] + like(zero_near, send, field),
+        "join_1",
+        vmem(zero, zero_near, zero_across, send),
+        [shape((3, block, half), bf16)] + like(zero_near, send),
         also=[other_one, bias_other],
     )
     zero_beyond = chip_swap(zero_near, 1, "zero_beyond")
     zero_came = core_swap(zero, "zero_pair")
-    onward = step(onward_kernel, "onward", vmem(keep_two, last_two), [piece])
+    onward = step(onward_kernel, "onward_1", vmem(keep_two, last_two), [piece])
     far_two = chip_swap(onward, 0, "two_far")
-    send = step(copy_kernel, "copy", vmem(send), like(send))
+    send, field = step(copy_kernel, "copy_1", vmem(send, field), like(send, field))
     near_two = chip_swap(send, 1, "two_near")
-    zero_beyond = step(copy_kernel, "copy", vmem(zero_beyond), like(zero_beyond))
+    zero_beyond = step(copy_kernel, "copy_2", vmem(zero_beyond), like(zero_beyond))
     beyond_came = core_swap(zero_beyond, "zero_pair_beyond")
 
     whole = shape((channels, half), bf16)
@@ -477,13 +474,6 @@
         [whole, plane, plane, piece],
         [dma((chips,))],
     )
-    whole_zero_came = step(
-        assemble_kernel,
-        "assemble",
-        [(SMEM, order_came)] + vmem(zero_came, beyond_came),
-        [whole],
-        [dma((chips,))],
-    )
 
     pre_grad, pre_grad_send = step(
         slope_kernel,
@@ -492,14 +482,19 @@
         [part, part],
     )
     pre_grad_came = core_swap(pre_grad_send, "pre_grad")
-    one = step(copy_kernel, "copy", vmem(one), like(one))
-    one_near, one_across = chip_swap(one, 0, "one_near"), chip_swap(one, 1, "one_across")
+    whole_zero_came = step(
+        assemble_kernel,
+        "assemble_1",
+        [(SMEM, order_came)] + vmem(zero_came, beyond_came),
+        [whole],
+        [dma((chips,))],
+    )
 
     def sizes(taps):
         return len(taps) * depth + (EXTRA if taps[-1] == 8 else 0)
 
     def grad_outs(taps):
-        return [shape((sizes(taps), channels), bf16), shape((sizes(taps), channels), f32)]
+        return [shape((sizes(taps), channels), bf16)]
 
     def grad_scratch(taps):
         return [
@@ -510,45 +505,58 @@
     def parts(ends):
         return [tuple(range(start, end)) for start, end in zip((0,) + ends[:-1], ends)]
 
-    def add(left, right):
-        return step(add_kernel, "add", vmem(left, right), like(left))
+    def add(name, left, right):
+        return step(add_kernel, "add_" + name, vmem(left, right), like(left))
 
     phase[0] = "late"
     grads = []
     for at, taps in enumerate(parts(PARTS_ONE)):
-        send, keep = step(
+        send = step(
             functools.partial(grad_one_kernel, taps),
             "grad_one_" + "ab"[at],
             vmem(pre_grad, pre_grad_came, whole_zero, whole_zero_came),
             grad_outs(taps),
             grad_scratch(taps),
         )
-        grads.append((send, keep))
-    near_a = group_send(grads[0][0], "in", "one_a")
-    one_near, one_across, pre_grad, pre_grad_send = step(
-        copy_kernel,
-        "copy",
-        vmem(one_near, one_across, pre_grad, pre_grad_send),
-        like(one_near, one_across, pre_grad, pre_grad_send),
-    )
-    one_beyond = chip_swap(one_near, 1, "one_beyond")
-
+        grads.append(send)
+        if at == 0:
+            one = step(copy_kernel, "copy_3", vmem(one), like(one))
+            one_near, one_across = chip_swap(one, 0, "one_near"), chip_swap(one, 1, "one_across")
+    near_a = group_send(grads[0], "in", "one_a")
     send, keep_one = back("back_one", 0, (2,), pre_grad, pre_grad_send, own_one, other_one)
     send_one = send
-    send_b = step(copy_kernel, "copy", vmem(grads[1][0]), like(grads[1][0]))
+    three, one_near = step(
+        join_kernel,
+        "join_one",
+        vmem(one, one_near, one_across),
+        [shape((3, block, half), bf16)] + like(one_near),
+    )
+    one_beyond = chip_swap(one_near, 1, "one_beyond")
+    three_came = core_swap(three, "one_pair")
+
+    send_b = step(copy_kernel, "copy_4", vmem(grads[1]), like(grads[1]))
     near_b = group_send(send_b, "in", "one_b")
-    mine_a = add(grads[0][1], near_a)
+    mine_a = add("one_a", grads[0], near_a)
     far_a = group_send(mine_a, "middle", "one_a")
 
+    one_beyond = step(copy_kernel, "copy_beyond_one", vmem(one_beyond), like(one_beyond))
+    beyond_came = core_swap(one_beyond, "one_pair_beyond")
     whole_one = step(
         assemble_kernel,
-        "assemble",
-        [(SMEM, order)] + vmem(one, one_near, one_across, one_beyond),
+        "assemble_one",
+        [(SMEM, order)] + vmem(three, one_beyond),
         [whole],
         [dma((chips,))],
     )
-    whole_one_came = core_swap(whole_one, "one_pair")
-    send_a, keep_a, send_b, keep_b = step(
+    whole_one_came = step(
+        assemble_kernel,
+        "assemble_one_came",
+        [(SMEM, order_came)] + vmem(three_came, beyond_came),
+        [whole],
+        [dma((chips,))],
+    )
+
+    send_a, keep_b = step(
         grad_two_kernel,
         "grad_two",
         [(SMEM, core_at)] + vmem(cotangent, whole_one, whole_one_came),
@@ -556,28 +564,25 @@
         grad_scratch(tuple(range(9))),
     )
     near_a = group_send(send_a, "in", "two_a")
-    send_one = step(copy_kernel, "copy", vmem(send_one), like(send_one))
-    near_one = chip_swap(send_one, 1, "one_near")
+    mine_b = add("one_b", send_b, near_b)
+    far_b = group_send(mine_b, "middle", "one_b")
+    send_b = step(copy_kernel, "copy_6", vmem(keep_b), like(keep_b))
+    near_b = group_send(send_b, "in", "two_b")
+    half_a = add("one_a_half", mine_a, far_a)
+    rest_a = group_send(half_a, "out", "one_a")
     out_own, out_other = step(
         conv_two_kernel, "conv_two", vmem(whole_one, own_two, other_two), [plane, plane]
     )
-    mine_b = add(grads[1][1], near_b)
-    far_b = group_send(mine_b, "middle", "one_b")
-    onward = step(onward_kernel, "onward", vmem(keep_one, near_one), [piece])
-    half_a = add(mine_a, far_a)
-    rest_a = group_send(half_a, "out", "one_a")
-    send_b = step(copy_kernel, "copy", vmem(send_b), like(send_b))
-    near_b = group_send(send_b, "in", "two_b")
-    mine_two_a = add(keep_a, near_a)
+    mine_two_a = add("two_a", send_a, near_a)
     far_two_a = group_send(mine_two_a, "middle", "two_a")
-    half_b = add(mine_b, far_b)
+    half_b = add("one_b_half", mine_b, far_b)
     rest_b = group_send(half_b, "out", "one_b")
-    rest_a = step(copy_kernel, "copy", vmem(rest_a), like(rest_a))
-    mine_two_b = add(keep_b, near_b)
+    mine_two_b = add("two_b", send_b, near_b)
     far_two_b = group_send(mine_two_b, "middle", "two_b")
-    onward = step(copy_kernel, "copy", vmem(onward), like(onward))
-    far_one = chip_swap(onward, 0, "one_far")
-    half_two_a = add(mine_two_a, far_two_a)
+    rest_a = step(copy_kernel, "copy_7", vmem(rest_a), like(rest_a))
+    send_one = step(copy_kernel, "copy_5", vmem(send_one), like(send_one))
+    near_one = chip_swap(send_one, 1, "one_near")
+    half_two_a = add("two_a_half", mine_two_a, far_two_a)
     rest_two_a = group_send(half_two_a, "out", "two_a")
 
     def finish(name, pieces):
@@ -592,15 +597,17 @@
         return kernel_grad.reshape(9, depth, channels), bias_grad.reshape(depth)
 
     kernel_grad_one, bias_grad_one = finish("finish_one", [half_a, rest_a, half_b, rest_b])
-    out_other = step(copy_kernel, "copy", vmem(out_other), [plane])
+    half_two_b = add("two_b_half", mine_two_b, far_two_b)
+    rest_two_b = group_send(half_two_b, "out", "two_b")
+    onward = step(onward_kernel, "onward_2", vmem(keep_one, near_one), [piece])
+    far_one = chip_swap(onward, 0, "one_far")
+    out_other = step(copy_kernel, "copy_9", vmem(out_other), [plane])
     out_came = core_swap(out_other, "out_pair")
     own, other = step(
         sum_kernel, "sum", [(SMEM, core_at)] + vmem(keep_one, near_one, far_one), [plane, plane]
     )
     other = core_swap(other, "field_pair")
-    half_two_b = add(mine_two_b, far_two_b)
-    rest_two_b = group_send(half_two_b, "out", "two_b")
-    rest_two_a = step(copy_kernel, "copy", vmem(rest_two_a), like(rest_two_a))
+    rest_two_a = step(copy_kernel, "copy_10", vmem(rest_two_a), like(rest_two_a))
     output = step(
         output_kernel,
         "output",

time: 121 us -> 118 us (0.975)
  waiting for transfers between devices: 37.8 us -> 34.2 us
    ppermute x33 -> x34, waiting for transfers between devices: 37.8 us -> 34.2 us  [swap(): return lax.ppermute(values, axis, pairs)]
    pallas_call x39 -> x40, Pallas kernels: 40 us -> 40.4 us  [run(): pl.pallas_call(marked, name=name, out_shape=[SPACES[id(spec)](out.shape,...]
    unnamed x38 -> x30, local copies, waits for them, and re-layouts: 4.41 us -> 4.3 us
    ppermute x33 -> x34, starting transfers between devices: 37.3 us -> 37.2 us  [swap(): return lax.ppermute(values, axis, pairs)]
  transfers between devices with their start and end apart: 33 -> 34, of which waited for: 14 -> 15; matrix products, arithmetic and copies ran while one was open for 1% -> 1% of each run, Pallas kernels for 30% -> 31%
where the time goes in v4:
time: 118 us; the launch traced here: 117 us
  Pallas kernels  40.4 us (34%)
  starting transfers between devices  37.2 us (32%)
  waiting for transfers between devices  34.2 us (29%)
  local copies, waits for them, and re-layouts  4.44 us (4%)
  between operations  1.18 us (1%)
    pallas_call x40, Pallas kernels, run(): pl.pallas_call(marked, name=name, out_shape=[SPACES[id(spec)](out.shape,...  40.4 us
    ppermute x34, starting transfers between devices, swap(): return lax.ppermute(values, axis, pairs)  37.2 us
    ppermute x34, waiting for transfers between devices, swap(): return lax.ppermute(values, axis, pairs)  34.2 us
    unnamed x30, local copies, waits for them, and re-layouts  4.3 us
  transfers between devices with their start and end apart: 34, of which 15 were waited for; matrix products, arithmetic and copies ran while one was open for 1% of the time, Pallas kernels for 31%

profile of v4, /device:TPU:0, one launch (start us, length us, event | category | flops | bytes accessed | tf_op | source)
XLA Modules:
  0.0 117.4 jit_solution(4123134248694829579)
XLA Ops:
  1.2 2.0 %field.1 = (bf16[80,2048]{1,0:T(8,128)(2,1)S(1)}, bf16[80,2048]{1,0:T(8,128)(2,1)S(1)}, bf16[80,2048]{1,0:T(8,128)(2,1)S(1)}, f32[8,128]{1,0:T(8,128)S(1)}) custom-call(s32[1]{0:T(128)} %bitcast.refs_0_, s32[32]{0:T(128)} %refs_1_.2, s32[32]{0:T(128)} %refs_2_.2, bf16[80,2048]{1,0:T(8,128)(2,1)} %refs_3_.1, bf16[80,8192]{1,0:T(8,128)(2,1)} %refs_4_.1, ...), custom_call_target="tpu_custom_call" | custom-call | flops 10000000000 | tf_op jit(solution)/shard_map/field/pallas_call | solution.py:328
  4.9 2.7 %collective-permute-start.1 = (bf16[1,160,1024]{2,1,0:T(8,128)(2,1)S(1)}, bf16[1,160,1024]{2,1,0:T(8,128)(2,1)S(1)}, u32[]{:S(2)}, u32[]{:S(2)}) collective-permute-start(bf16[1,160,1024]{2,1,0:T(8,128)(2,1)S(1)} %get-tuple-element.106.refs_0_), channel_id=1, source_target_pairs={{0,2},{1,5},{2,0},{3,7},{4,6},{5,1},{6,4},{7,3},{8,10},{9,13},{10,... | collective-permute-start | bytes 983048 | tf_op jit(solution)/shard_map/zero_near/ppermute | solution.py:363
  7.6 1.5 %collective-permute-start.2 = (bf16[1,160,1024]{2,1,0:T(8,128)(2,1)S(1)}, bf16[1,160,1024]{2,1,0:T(8,128)(2,1)S(1)}, u32[]{:S(2)}, u32[]{:S(2)}) collective-permute-start(bf16[1,160,1024]{2,1,0:T(8,128)(2,1)S(1)} %get-tuple-element.106.refs_0_), channel_id=1, source_target_pairs={{0,4},{1,3},{2,6},{3,1},{4,0},{5,7},{6,2},{7,5},{8,12},{9,11},{10,... | collective-permute-start | bytes 983048 | tf_op jit(solution)/shard_map/zero_across/ppermute | solution.py:363
  9.1 5.3 %back_two.1 = (bf16[1,160,1024]{2,1,0:T(8,128)(2,1)S(1)}, bf16[1,160,1024]{2,1,0:T(8,128)(2,1)S(1)}, f32[2,160,1024]{2,1,0:T(8,128)S(1)}, f32[8,128]{1,0:T(8,128)S(1)}) custom-call(s32[4]{0:T(128)S(1)} %get-tuple-element.201.refs_0_.refs_1_, bf16[80,2048]{1,0:T(8,128)(2,1)S(1)} %get-tuple-element.103.refs_1_, ...), custom_call_target="tpu_custom_call" | custom-call | flops 10000000000 | tf_op jit(solution)/shard_map/back_two/pallas_call | solution.py:328
  16.0 2.1 %collective-permute-start.7 = (bf16[1,160,1024]{2,1,0:T(8,128)(2,1)S(1)}, bf16[1,160,1024]{2,1,0:T(8,128)(2,1)S(1)}, u32[]{:S(2)}, u32[]{:S(2)}) collective-permute-start(bf16[1,160,1024]{2,1,0:T(8,128)(2,1)S(1)} %get-tuple-element.118), channel_id=1, source_target_pairs={{0,4},{1,3},{2,6},{3,1},{4,0},{5,7},{6,2},{7,5},{8,12},{9,11},{10,... | collective-permute-start | bytes 983048 | tf_op jit(solution)/shard_map/zero_beyond/ppermute | solution.py:363
  18.1 3.5 %collective-permute-done.6.refs_1_ = bf16[1,160,1024]{2,1,0:T(8,128)(2,1)S(1)} collective-permute-done((bf16[1,160,1024]{2,1,0:T(8,128)(2,1)S(1)}, bf16[1,160,1024]{2,1,0:T(8,128)(2,1)S(1)}, u32[]{:S(2)}, u32[]{:S(2)}) %collective-permute-start.6) | collective-permute-done | bytes 327712 | tf_op jit(solution)/shard_map/two_last/ppermute | solution.py:363
  22.8 2.9 %collective-permute-done.7.refs_0_ = bf16[1,160,1024]{2,1,0:T(8,128)(2,1)S(1)} collective-permute-done((bf16[1,160,1024]{2,1,0:T(8,128)(2,1)S(1)}, bf16[1,160,1024]{2,1,0:T(8,128)(2,1)S(1)}, u32[]{:S(2)}, u32[]{:S(2)}) %collective-permute-start.7) | collective-permute-done | bytes 327712 | tf_op jit(solution)/shard_map/zero_beyond/ppermute | solution.py:363
  25.9 4.8 %conv_one.1 = (bf16[640,1024]{1,0:T(8,128)(2,1)S(1)}, f32[80,1024]{1,0:T(8,128)S(1)}, f32[80,1024]{1,0:T(8,128)S(1)}, bf16[1,160,1024]{2,1,0:T(8,128)(2,1)S(1)}, f32[8,128]{1,0:T(8,128)S(1)}) custom-call(s32[1]{0:T(128)} %bitcast.refs_0_, s32[4]{0:T(128)S(1)} %get-tuple-element.201.refs_0_.refs_1_, bf16[3,160,1024]{2,1,0:T(8,128)(2,1)S(1)} %get-tuple-element.117.refs_2_, ...), custom_call_target="tpu_custom_call" | custom-call | flops 10000000000 | tf_op jit(solution)/shard_map/conv_one/pallas_call | solution.py:328
  30.7 1.4 %collective-permute-done.8.refs_2_ = bf16[1,160,1024]{2,1,0:T(8,128)(2,1)S(1)} collective-permute-done((bf16[1,160,1024]{2,1,0:T(8,128)(2,1)S(1)}, bf16[1,160,1024]{2,1,0:T(8,128)(2,1)S(1)}, u32[]{:S(2)}, u32[]{:S(2)}) %collective-permute-start.8) | collective-permute-done | bytes 327712 | tf_op jit(solution)/shard_map/two_near/ppermute | solution.py:363
  33.8 1.5 %grad_one_a.1 = (bf16[400,640]{1,0:T(8,128)(2,1)S(1)}, f32[8,128]{1,0:T(8,128)S(1)}) custom-call(bf16[80,1024]{1,0:T(8,128)(2,1)S(1)} %get-tuple-element.128.refs_0_.refs_1_, bf16[80,1024]{1,0:T(8,128)(2,1)S(1)} %collective-permute-done.10.refs_1_, bf16[640,1024]{1,0:T(8,128)(2,1)S(1)} %get-tuple-element.130.refs_2_, ...), custom_call_target="tpu_custom_call" | custom-call | flops 500000000 | tf_op jit(solution)/shard_map/grad_one_a/pallas_call | solution.py:328
  37.2 3.5 %collective-permute-start.16 = (bf16[400,640]{1,0:T(8,128)(2,1)S(1)}, bf16[400,640]{1,0:T(8,128)(2,1)S(1)}, u32[]{:S(2)}, u32[]{:S(2)}) collective-permute-start(bf16[400,640]{1,0:T(8,128)(2,1)S(1)} %get-tuple-element.141.refs_0_), channel_id=1, source_target_pairs={{0,8},{24,16},{1,9},{25,17},{2,10},{26,18},{3,11},{27,19},{4,12},{... | collective-permute-start | bytes 1536008 | tf_op jit(solution)/shard_map/one_a_in/ppermute | solution.py:363
  42.0 5.3 %back_one.1 = (bf16[2,160,1024]{2,1,0:T(8,128)(2,1)S(1)}, f32[2,160,1024]{2,1,0:T(8,128)S(1)}, f32[8,128]{1,0:T(8,128)S(1)}) custom-call(s32[4]{0:T(128)S(1)} %get-tuple-element.201.refs_0_.refs_1_, bf16[80,1024]{1,0:T(8,128)(2,1)S(1)} %get-tuple-element.128.refs_0_.refs_1_, bf16[80,1024]{1,0:T(8,128)(2,1)S(1)} %get-tuple-element.129.refs_2_, ...), custom_call_target="tpu_custom_call" | custom-call | flops 30000001024 | tf_op jit(solution)/shard_map/back_one/pallas_call | solution.py:328
  52.4 3.1 %collective-permute-done.15.refs_0_ = bf16[1,160,1024]{2,1,0:T(8,128)(2,1)S(1)} collective-permute-done((bf16[1,160,1024]{2,1,0:T(8,128)(2,1)S(1)}, bf16[1,160,1024]{2,1,0:T(8,128)(2,1)S(1)}, u32[]{:S(2)}, u32[]{:S(2)}) %collective-permute-start.15) | collective-permute-done | bytes 327712 | tf_op jit(solution)/shard_map/one_beyond/ppermute | solution.py:363
  58.2 2.6 %grad_two.1 = (bf16[400,640]{1,0:T(8,128)(2,1)S(1)}, bf16[336,640]{1,0:T(8,128)(2,1)S(1)}, f32[8,128]{1,0:T(8,128)S(1)}) custom-call(s32[1]{0:T(128)} %bitcast.refs_0_, bf16[80,2048]{1,0:T(8,128)(2,1)S(1)} %copy-done.1, bf16[640,1024]{1,0:T(8,128)(2,1)S(1)} %get-tuple-element.148.refs_2_.refs_0_, bf16[640,1024]{1,0:T(8,128)(2,1)S(1)} %get-tuple-element.151.refs_3_, ...), custom_call_target="tpu_custom_call" | custom-call | flops 20000000000 | tf_op jit(solution)/shard_map/grad_two/pallas_call | solution.py:328
  60.8 4.2 %collective-permute-start.24 = (bf16[400,640]{1,0:T(8,128)(2,1)S(1)}, bf16[400,640]{1,0:T(8,128)(2,1)S(1)}, u32[]{:S(2)}, u32[]{:S(2)}) collective-permute-start(bf16[400,640]{1,0:T(8,128)(2,1)S(1)} %get-tuple-element.166.refs_0_), channel_id=1, source_target_pairs={{0,8},{24,16},{1,9},{25,17},{2,10},{26,18},{3,11},{27,19},{4,12},{... | collective-permute-start | bytes 1536008 | tf_op jit(solution)/shard_map/two_a_in/ppermute | solution.py:363
  68.1 6.1 %collective-permute-start.22 = (bf16[336,640]{1,0:T(8,128)(2,1)}, bf16[336,640]{1,0:T(8,128)(2,1)}, u32[]{:S(2)}, u32[]{:S(2)}) collective-permute-start(bf16[336,640]{1,0:T(8,128)(2,1)} %get-tuple-element.164.refs_0_), channel_id=1, source_target_pairs={{0,8},{24,16},{1,9},{25,17},{2,10},{26,18},{3,11},{27,19},{4,12},{... | collective-permute-start | bytes 1290248 | tf_op jit(solution)/shard_map/two_b_in/ppermute | solution.py:363
  74.3 3.1 %conv_two.1 = (f32[80,1024]{1,0:T(8,128)S(1)}, f32[80,1024]{1,0:T(8,128)S(1)}, f32[8,128]{1,0:T(8,128)S(1)}) custom-call(bf16[640,1024]{1,0:T(8,128)(2,1)S(1)} %get-tuple-element.148.refs_2_.refs_0_, bf16[720,640]{1,0:T(8,128)(2,1)S(1)} %bitcast.12, bf16[720,640]{1,0:T(8,128)(2,1)S(1)} %collective-permute-done.3.refs_4_.refs_2_, ...), custom_call_target="tpu_custom_call" | custom-call | flops 100000000 | tf_op jit(solution)/shard_map/conv_two/pallas_call | solution.py:328
  81.0 4.5 %collective-permute-done.22.refs_1_ = bf16[336,640]{1,0:T(8,128)(2,1)} collective-permute-done((bf16[336,640]{1,0:T(8,128)(2,1)}, bf16[336,640]{1,0:T(8,128)(2,1)}, u32[]{:S(2)}, u32[]{:S(2)}) %collective-permute-start.22) | collective-permute-done | bytes 430112 | tf_op jit(solution)/shard_map/two_b_in/ppermute | solution.py:363
  91.0 1.8 %collective-permute-done.27.refs_4_ = bf16[336,640]{1,0:T(8,128)(2,1)} collective-permute-done((bf16[336,640]{1,0:T(8,128)(2,1)S(1)}, bf16[336,640]{1,0:T(8,128)(2,1)}, u32[]{:S(2)}, u32[]{:S(2)}) %collective-permute-start.27) | collective-permute-done | bytes 430112 | tf_op jit(solution)/shard_map/one_b_out/ppermute | solution.py:363
  92.8 2.4 %finish_one.1 = (f32[720,640]{1,0:T(8,128)}, f32[1,80]{1,0:T(1,128)S(1)}, f32[8,128]{1,0:T(8,128)S(1)}) custom-call(s32[1]{0:T(128)} %bitcast.3.refs_0_, bf16[400,640]{1,0:T(8,128)(2,1)S(1)} %get-tuple-element.163.refs_1_, bf16[400,640]{1,0:T(8,128)(2,1)S(1)} %get-tuple-element.174.refs_2_, bf16[336,640]{1,0:T(8,128)(2,1)S(1)} %get-tuple-element.175.refs_3_, ...), custom_call_target="tpu_custom_call" | custom-call | flops 10000000000 | tf_op jit(solution)/shard_map/finish_one/pallas_call | solution.py:328
  95.3 4.0 %collective-permute-done.25.refs_1_.refs_2_ = bf16[2,160,1024]{2,1,0:T(8,128)(2,1)S(1)} collective-permute-done((bf16[2,160,1024]{2,1,0:T(8,128)(2,1)S(1)}, bf16[2,160,1024]{2,1,0:T(8,128)(2,1)S(1)}, u32[]{:S(2)}, u32[]{:S(2)}) %collective-permute-start.25) | collective-permute-done | bytes 655392 | tf_op jit(solution)/shard_map/one_near/ppermute | solution.py:363
  102.1 4.4 %collective-permute-done.31.refs_3_ = bf16[1,160,1024]{2,1,0:T(8,128)(2,1)S(1)} collective-permute-done((bf16[1,160,1024]{2,1,0:T(8,128)(2,1)S(1)}, bf16[1,160,1024]{2,1,0:T(8,128)(2,1)S(1)}, u32[]{:S(2)}, u32[]{:S(2)}) %collective-permute-start.31) | collective-permute-done | bytes 327712 | tf_op jit(solution)/shard_map/one_far/ppermute | solution.py:363
  109.9 5.0 %collective-permute-done.33.refs_4_ = bf16[336,640]{1,0:T(8,128)(2,1)S(1)} collective-permute-done((bf16[336,640]{1,0:T(8,128)(2,1)S(1)}, bf16[336,640]{1,0:T(8,128)(2,1)S(1)}, u32[]{:S(2)}, u32[]{:S(2)}) %collective-permute-start.33) | collective-permute-done | bytes 430112 | tf_op jit(solution)/shard_map/two_b_out/ppermute | solution.py:363
  114.9 2.0 %finish_two.1 = (f32[720,640]{1,0:T(8,128)}, f32[1,80]{1,0:T(1,128)S(1)}, f32[8,128]{1,0:T(8,128)}) custom-call(s32[1]{0:T(128)} %bitcast.3.refs_0_, bf16[400,640]{1,0:T(8,128)(2,1)S(1)} %get-tuple-element.183.refs_1_, bf16[400,640]{1,0:T(8,128)(2,1)S(1)} %get-tuple-element.195.refs_2_, bf16[336,640]{1,0:T(8,128)(2,1)S(1)} %get-tuple-element.196.refs_3_, ...), custom_call_target="tpu_custom_call" | custom-call | flops 99999997952 | tf_op jit(solution)/shard_map/finish_two/pallas_call | solution.py:328
  (117 shorter events, 36.5 us)
Async XLA Ops:
  0.6 8.5 %collective-permute-start.3 = (bf16[720,640]{1,0:T(8,128)(2,1)}, bf16[720,640]{1,0:T(8,128)(2,1)S(1)}, u32[]{:S(2)}, u32[]{:S(2)}) collective-permute-start(bf16[720,640]{1,0:T(8,128)(2,1)} %bitcast.10), channel_id=1, source_target_pairs={{0,1},{1,0},{2,3},{3,2},{4,5},{5,4},{6,7},{7,6},{8,9},{9,8},{10,11... | collective-permute-start | bytes 2764808 | tf_op jit(solution)/shard_map/kernel_two/ppermute | solution.py:363
  3.3 12.6 %collective-permute-start.4 = (bf16[720,640]{1,0:T(8,128)(2,1)}, bf16[720,640]{1,0:T(8,128)(2,1)S(1)}, u32[]{:S(2)}, u32[]{:S(2)}) collective-permute-start(bf16[720,640]{1,0:T(8,128)(2,1)} %bitcast.2.refs_4_.refs_3_), channel_id=1, source_target_pairs={{0,1},{1,0},{2,3},{3,2},{4,5},{5,4},{6,7},{7,6},{8,9},{9,8},{10,11... | collective-permute-start | bytes 2764808 | tf_op jit(solution)/shard_map/kernel_one/ppermute | solution.py:363
  3.8 11.2 %collective-permute-start.5 = (bf16[80,128]{1,0:T(8,128)(2,1)S(1)}, bf16[80,128]{1,0:T(8,128)(2,1)S(1)}, u32[]{:S(2)}, u32[]{:S(2)}) collective-permute-start(bf16[80,128]{1,0:T(8,128)(2,1)S(1)} %broadcast_in_dim.4.refs_6_), channel_id=1, source_target_pairs={{0,1},{1,0},{2,3},{3,2},{4,5},{5,4},{6,7},{7,6},{8,9},{9,8},{10,11... | collective-permute-start | bytes 61448 | tf_op jit(solution)/shard_map/bias/ppermute | solution.py:363
  4.9 10.2 %collective-permute-start.1 = (bf16[1,160,1024]{2,1,0:T(8,128)(2,1)S(1)}, bf16[1,160,1024]{2,1,0:T(8,128)(2,1)S(1)}, u32[]{:S(2)}, u32[]{:S(2)}) collective-permute-start(bf16[1,160,1024]{2,1,0:T(8,128)(2,1)S(1)} %get-tuple-element.106.refs_0_), channel_id=1, source_target_pairs={{0,2},{1,5},{2,0},{3,7},{4,6},{5,1},{6,4},{7,3},{8,10},{9,13},{10,... | collective-permute-start | bytes 983048 | tf_op jit(solution)/shard_map/zero_near/ppermute | solution.py:363
  7.6 8.3 %collective-permute-start.2 = (bf16[1,160,1024]{2,1,0:T(8,128)(2,1)S(1)}, bf16[1,160,1024]{2,1,0:T(8,128)(2,1)S(1)}, u32[]{:S(2)}, u32[]{:S(2)}) collective-permute-start(bf16[1,160,1024]{2,1,0:T(8,128)(2,1)S(1)} %get-tuple-element.106.refs_0_), channel_id=1, source_target_pairs={{0,4},{1,3},{2,6},{3,1},{4,0},{5,7},{6,2},{7,5},{8,12},{9,11},{10,... | collective-permute-start | bytes 983048 | tf_op jit(solution)/shard_map/zero_across/ppermute | solution.py:363
  16.0 9.8 %collective-permute-start.7 = (bf16[1,160,1024]{2,1,0:T(8,128)(2,1)S(1)}, bf16[1,160,1024]{2,1,0:T(8,128)(2,1)S(1)}, u32[]{:S(2)}, u32[]{:S(2)}) collective-permute-start(bf16[1,160,1024]{2,1,0:T(8,128)(2,1)S(1)} %get-tuple-element.118), channel_id=1, source_target_pairs={{0,4},{1,3},{2,6},{3,1},{4,0},{5,7},{6,2},{7,5},{8,12},{9,11},{10,... | collective-permute-start | bytes 983048 | tf_op jit(solution)/shard_map/zero_beyond/ppermute | solution.py:363
  18.1 14.4 %collective-permute-start.11 = (bf16[3,160,1024]{2,1,0:T(8,128)(2,1)S(1)}, bf16[3,160,1024]{2,1,0:T(8,128)(2,1)S(1)}, u32[]{:S(2)}, u32[]{:S(2)}) collective-permute-start(bf16[3,160,1024]{2,1,0:T(8,128)(2,1)S(1)} %get-tuple-element.117.refs_2_), channel_id=1, source_target_pairs={{0,1},{1,0},{2,3},{3,2},{4,5},{5,4},{6,7},{7,6},{8,9},{9,8},{10,11... | collective-permute-start | bytes 2949128 | tf_op jit(solution)/shard_map/zero_pair/ppermute | solution.py:363
  21.7 10.4 %collective-permute-start.8 = (bf16[1,160,1024]{2,1,0:T(8,128)(2,1)S(1)}, bf16[1,160,1024]{2,1,0:T(8,128)(2,1)S(1)}, u32[]{:S(2)}, u32[]{:S(2)}) collective-permute-start(bf16[1,160,1024]{2,1,0:T(8,128)(2,1)S(1)} %get-tuple-element.123), channel_id=1, source_target_pairs={{0,4},{1,3},{2,6},{3,1},{4,0},{5,7},{6,2},{7,5},{8,12},{9,11},{10,... | collective-permute-start | bytes 983048 | tf_op jit(solution)/shard_map/two_near/ppermute | solution.py:363
  22.3 9.8 %collective-permute-start.9 = (bf16[1,160,1024]{2,1,0:T(8,128)(2,1)S(1)}, bf16[1,160,1024]{2,1,0:T(8,128)(2,1)S(1)}, u32[]{:S(2)}, u32[]{:S(2)}) collective-permute-start(bf16[1,160,1024]{2,1,0:T(8,128)(2,1)S(1)} %get-tuple-element.124), channel_id=1, source_target_pairs={{0,2},{1,5},{2,0},{3,7},{4,6},{5,1},{6,4},{7,3},{8,10},{9,13},{10,... | collective-permute-start | bytes 983048 | tf_op jit(solution)/shard_map/two_far/ppermute | solution.py:363
  35.3 12.8 %collective-permute-start.13 = (bf16[1,160,1024]{2,1,0:T(8,128)(2,1)S(1)}, bf16[1,160,1024]{2,1,0:T(8,128)(2,1)S(1)}, u32[]{:S(2)}, u32[]{:S(2)}) collective-permute-start(bf16[1,160,1024]{2,1,0:T(8,128)(2,1)S(1)} %get-tuple-element.135.refs_0_), channel_id=1, source_target_pairs={{0,2},{1,5},{2,0},{3,7},{4,6},{5,1},{6,4},{7,3},{8,10},{9,13},{10,... | collective-permute-start | bytes 983048 | tf_op jit(solution)/shard_map/one_near/ppermute | solution.py:363
  35.9 12.2 %collective-permute-start.14 = (bf16[1,160,1024]{2,1,0:T(8,128)(2,1)S(1)}, bf16[1,160,1024]{2,1,0:T(8,128)(2,1)S(1)}, u32[]{:S(2)}, u32[]{:S(2)}) collective-permute-start(bf16[1,160,1024]{2,1,0:T(8,128)(2,1)S(1)} %get-tuple-element.135.refs_0_), channel_id=1, source_target_pairs={{0,4},{1,3},{2,6},{3,1},{4,0},{5,7},{6,2},{7,5},{8,12},{9,11},{10,... | collective-permute-start | bytes 983048 | tf_op jit(solution)/shard_map/one_across/ppermute | solution.py:363
  37.2 14.1 %collective-permute-start.16 = (bf16[400,640]{1,0:T(8,128)(2,1)S(1)}, bf16[400,640]{1,0:T(8,128)(2,1)S(1)}, u32[]{:S(2)}, u32[]{:S(2)}) collective-permute-start(bf16[400,640]{1,0:T(8,128)(2,1)S(1)} %get-tuple-element.141.refs_0_), channel_id=1, source_target_pairs={{0,8},{24,16},{1,9},{25,17},{2,10},{26,18},{3,11},{27,19},{4,12},{... | collective-permute-start | bytes 1536008 | tf_op jit(solution)/shard_map/one_a_in/ppermute | solution.py:363
  49.2 15.8 %collective-permute-start.20 = (bf16[336,640]{1,0:T(8,128)(2,1)S(1)}, bf16[336,640]{1,0:T(8,128)(2,1)S(1)}, u32[]{:S(2)}, u32[]{:S(2)}) collective-permute-start(bf16[336,640]{1,0:T(8,128)(2,1)S(1)} %get-tuple-element.154.refs_0_), channel_id=1, source_target_pairs={{0,8},{24,16},{1,9},{25,17},{2,10},{26,18},{3,11},{27,19},{4,12},{... | collective-permute-start | bytes 1290248 | tf_op jit(solution)/shard_map/one_b_in/ppermute | solution.py:363
  51.5 15.1 %collective-permute-start.17 = (bf16[400,640]{1,0:T(8,128)(2,1)S(1)}, bf16[400,640]{1,0:T(8,128)(2,1)S(1)}, u32[]{:S(2)}, u32[]{:S(2)}) collective-permute-start(bf16[400,640]{1,0:T(8,128)(2,1)S(1)} %get-tuple-element.149.refs_0_), channel_id=1, source_target_pairs={{8,16},{16,8},{9,17},{17,9},{10,18},{18,10},{11,19},{19,11},{12,20... | collective-permute-start | bytes 1536008 | tf_op jit(solution)/shard_map/one_a_middle/ppermute | solution.py:363
  60.8 17.3 %collective-permute-start.24 = (bf16[400,640]{1,0:T(8,128)(2,1)S(1)}, bf16[400,640]{1,0:T(8,128)(2,1)S(1)}, u32[]{:S(2)}, u32[]{:S(2)}) collective-permute-start(bf16[400,640]{1,0:T(8,128)(2,1)S(1)} %get-tuple-element.166.refs_0_), channel_id=1, source_target_pairs={{0,8},{24,16},{1,9},{25,17},{2,10},{26,18},{3,11},{27,19},{4,12},{... | collective-permute-start | bytes 1536008 | tf_op jit(solution)/shard_map/two_a_in/ppermute | solution.py:363
  65.1 14.4 %collective-permute-start.23 = (bf16[336,640]{1,0:T(8,128)(2,1)S(1)}, bf16[336,640]{1,0:T(8,128)(2,1)S(1)}, u32[]{:S(2)}, u32[]{:S(2)}) collective-permute-start(bf16[336,640]{1,0:T(8,128)(2,1)S(1)} %get-tuple-element.165.refs_0_), channel_id=1, source_target_pairs={{8,16},{16,8},{9,17},{17,9},{10,18},{18,10},{11,19},{19,11},{12,20... | collective-permute-start | bytes 1290248 | tf_op jit(solution)/shard_map/one_b_middle/ppermute | solution.py:363
  66.7 20.7 %collective-permute-start.21 = (bf16[400,640]{1,0:T(8,128)(2,1)S(1)}, bf16[400,640]{1,0:T(8,128)(2,1)}, u32[]{:S(2)}, u32[]{:S(2)}) collective-permute-start(bf16[400,640]{1,0:T(8,128)(2,1)S(1)} %get-tuple-element.163.refs_1_), channel_id=1, source_target_pairs={{8,0},{16,24},{9,1},{17,25},{10,2},{18,26},{11,3},{19,27},{12,4},{... | collective-permute-start | bytes 1536008 | tf_op jit(solution)/shard_map/one_a_out/ppermute | solution.py:363
  68.1 17.3 %collective-permute-start.22 = (bf16[336,640]{1,0:T(8,128)(2,1)}, bf16[336,640]{1,0:T(8,128)(2,1)}, u32[]{:S(2)}, u32[]{:S(2)}) collective-permute-start(bf16[336,640]{1,0:T(8,128)(2,1)} %get-tuple-element.164.refs_0_), channel_id=1, source_target_pairs={{0,8},{24,16},{1,9},{25,17},{2,10},{26,18},{3,11},{27,19},{4,12},{... | collective-permute-start | bytes 1290248 | tf_op jit(solution)/shard_map/two_b_in/ppermute | solution.py:363
  78.8 10.7 %collective-permute-start.28 = (bf16[400,640]{1,0:T(8,128)(2,1)S(1)}, bf16[400,640]{1,0:T(8,128)(2,1)S(1)}, u32[]{:S(2)}, u32[]{:S(2)}) collective-permute-start(bf16[400,640]{1,0:T(8,128)(2,1)S(1)} %get-tuple-element.176.refs_0_), channel_id=1, source_target_pairs={{8,16},{16,8},{9,17},{17,9},{10,18},{18,10},{11,19},{19,11},{12,20... | collective-permute-start | bytes 1536008 | tf_op jit(solution)/shard_map/two_a_middle/ppermute | solution.py:363
  79.7 13.1 %collective-permute-start.27 = (bf16[336,640]{1,0:T(8,128)(2,1)S(1)}, bf16[336,640]{1,0:T(8,128)(2,1)}, u32[]{:S(2)}, u32[]{:S(2)}) collective-permute-start(bf16[336,640]{1,0:T(8,128)(2,1)S(1)} %get-tuple-element.175.refs_3_), channel_id=1, source_target_pairs={{8,0},{16,24},{9,1},{17,25},{10,2},{18,26},{11,3},{19,27},{12,4},{... | collective-permute-start | bytes 1290248 | tf_op jit(solution)/shard_map/one_b_out/ppermute | solution.py:363
  86.7 8.5 %collective-permute-start.26 = (bf16[336,640]{1,0:T(8,128)(2,1)S(1)}, bf16[336,640]{1,0:T(8,128)(2,1)S(1)}, u32[]{:S(2)}, u32[]{:S(2)}) collective-permute-start(bf16[336,640]{1,0:T(8,128)(2,1)S(1)} %get-tuple-element.173.refs_0_), channel_id=1, source_target_pairs={{8,16},{16,8},{9,17},{17,9},{10,18},{18,10},{11,19},{19,11},{12,20... | collective-permute-start | bytes 1290248 | tf_op jit(solution)/shard_map/two_b_middle/ppermute | solution.py:363
  88.7 10.7 %collective-permute-start.25 = (bf16[2,160,1024]{2,1,0:T(8,128)(2,1)S(1)}, bf16[2,160,1024]{2,1,0:T(8,128)(2,1)S(1)}, u32[]{:S(2)}, u32[]{:S(2)}) collective-permute-start(bf16[2,160,1024]{2,1,0:T(8,128)(2,1)S(1)} %get-tuple-element.172), channel_id=1, source_target_pairs={{0,4},{1,3},{2,6},{3,1},{4,0},{5,7},{6,2},{7,5},{8,12},{9,11},{10,... | collective-permute-start | bytes 1966088 | tf_op jit(solution)/shard_map/one_near/ppermute | solution.py:363
  89.7 17.1 %collective-permute-start.30 = (bf16[400,640]{1,0:T(8,128)(2,1)S(1)}, bf16[400,640]{1,0:T(8,128)(2,1)S(1)}, u32[]{:S(2)}, u32[]{:S(2)}) collective-permute-start(bf16[400,640]{1,0:T(8,128)(2,1)S(1)} %get-tuple-element.183.refs_1_), channel_id=1, source_target_pairs={{8,0},{16,24},{9,1},{17,25},{10,2},{18,26},{11,3},{19,27},{12,4},{... | collective-permute-start | bytes 1536008 | tf_op jit(solution)/shard_map/two_a_out/ppermute | solution.py:363
  100.2 14.6 %collective-permute-start.33 = (bf16[336,640]{1,0:T(8,128)(2,1)S(1)}, bf16[336,640]{1,0:T(8,128)(2,1)S(1)}, u32[]{:S(2)}, u32[]{:S(2)}) collective-permute-start(bf16[336,640]{1,0:T(8,128)(2,1)S(1)} %get-tuple-element.196.refs_3_), channel_id=1, source_target_pairs={{8,0},{16,24},{9,1},{17,25},{10,2},{18,26},{11,3},{19,27},{12,4},{... | collective-permute-start | bytes 1290248 | tf_op jit(solution)/shard_map/two_b_out/ppermute | solution.py:363
  (24 other events, 85.5 us)

commit v5 on v4

--- a/solution.py
+++ b/solution.py
@@ -294,9 +294,26 @@
         copies.append(pltpu.make_async_copy(total.at[span, :], grad.at[span, :], sem.at[at]))
         copies[-1].start()
         base += size
-    bias[...] = total[rows : rows + 1, : bias.shape[1]]
+    bias[...] = total[rows, : bias.shape[0]]
     for copy in copies:
         copy.wait()
+
+
+def finish_first_kernel(inner, made, came, grad, total, sem):
+    total[...] = jnp.where(inner[0] == 1, made[...], came[...]).astype(f32)
+    copy = pltpu.make_async_copy(total, grad.at[pl.ds(0, total.shape[0]), :], sem)
+    copy.start()
+    copy.wait()
+
+
+def finish_last_kernel(inner, made, came, begun, grad, bias, total, sem):
+    total[...] = jnp.where(inner[0] == 1, made[...], came[...]).astype(f32)
+    count = total.shape[0] - EXTRA
+    rows = pl.ds(grad.shape[0] - count, count)
+    copy = pltpu.make_async_copy(total.at[pl.ds(0, count), :], grad.at[rows, :], sem)
+    copy.start()
+    bias[...] = total[count, : bias.shape[0]]
+    copy.wait()
 
 
 SMEM = pl.BlockSpec(memory_space=pltpu.SMEM)
@@ -310,7 +327,7 @@
     return pltpu.with_memory_space_constraint(values, pltpu.HBM)
 
 
-def run(body, name, ins, outs, scratch=(), out_specs=None, after=(), cost=0):
+def run(body, name, ins, outs, scratch=(), out_specs=None, after=(), cost=0, aliases=None):
     count, total = len(ins), len(ins) + len(after)
     end = total + len(outs)
 
@@ -335,6 +352,7 @@
         in_specs=[spec for spec, _ in ins],
         out_specs=out_specs,
         scratch_shapes=list(scratch),
+        input_output_aliases=aliases or {},
         cost_estimate=pl.CostEstimate(flops=cost, bytes_accessed=0, transcendentals=0),
         compiler_params=pltpu.CompilerParams(vmem_limit_bytes=VMEM_LIMIT),
     )(*args)
@@ -397,11 +415,11 @@
 
     marks, phase = [], ["early"]
 
-    def step(body, name, ins, outs, scratch=(), out_specs=None, also=()):
+    def step(body, name, ins, outs, scratch=(), out_specs=None, also=(), aliases=None):
         after = marks[-1:] + list(also)
         costs = COSTS[phase[0]]
         cost = costs.get(name, costs["small" if name.split("_")[0] in SMALL else "big"])
-        *results, mark = run(body, name, ins, outs, scratch, out_specs, after, cost)
+        *results, mark = run(body, name, ins, outs, scratch, out_specs, after, cost, aliases)
         marks.append(mark)
         return results[0] if len(results) == 1 else results
 
@@ -590,11 +608,11 @@
             finish_kernel,
             name,
             [(SMEM, inner)] + vmem(*pieces),
-            [shape((rows, channels), f32), shape((1, depth), f32)],
+            [shape((rows, channels), f32), shape((depth,), f32)],
             [pltpu.VMEM((rows + EXTRA, channels), f32), dma((len(pieces) // 2,))],
             out_specs=[ANY, VMEM],
         )
-        return kernel_grad.reshape(9, depth, channels), bias_grad.reshape(depth)
+        return kernel_grad.reshape(9, depth, channels), bias_grad
 
     kernel_grad_one, bias_grad_one = finish("finish_one", [half_a, rest_a, half_b, rest_b])
     half_two_b = add("two_b_half", mine_two_b, far_two_b)
@@ -607,7 +625,14 @@
         sum_kernel, "sum", [(SMEM, core_at)] + vmem(keep_one, near_one, far_one), [plane, plane]
     )
     other = core_swap(other, "field_pair")
-    rest_two_a = step(copy_kernel, "copy_10", vmem(rest_two_a), like(rest_two_a))
+    begun = step(
+        finish_first_kernel,
+        "finish_two_first",
+        [(SMEM, inner)] + vmem(half_two_a, rest_two_a),
+        [shape((rows, channels), f32)],
+        [pltpu.VMEM(half_two_a.shape, f32), dma],
+        out_specs=[ANY],
+    )
     output = step(
         output_kernel,
         "output",
@@ -625,9 +650,17 @@
         [pltpu.VMEM((depth, pixels), f32), dma],
         out_specs=[ANY],
     )
-    kernel_grad_two, bias_grad_two = finish(
-        "finish_two", [half_two_a, rest_two_a, half_two_b, rest_two_b]
-    )
+    count = half_two_b.shape[0]
+    kernel_grad_two, bias_grad_two = step(
+        finish_last_kernel,
+        "finish_two",
+        [(SMEM, inner)] + vmem(half_two_b, rest_two_b) + [(ANY, begun)],
+        [shape((rows, channels), f32), shape((depth,), f32)],
+        [pltpu.VMEM((count, channels), f32), dma],
+        out_specs=[ANY, VMEM],
+        aliases={3: 0},
+    )
+    kernel_grad_two = kernel_grad_two.reshape(9, depth, channels)
     return output, grad_field, kernel_grad_one, bias_grad_one, kernel_grad_two, bias_grad_two
 
 

time: 118 us -> 118 us (level)
  transfers between devices with their start and end apart: 34 -> 34, of which waited for: 15 -> 15; matrix products, arithmetic and copies ran while one was open for 1% -> 1% of each run, Pallas kernels for 31% -> 32%
where the time goes in v5:
time: 118 us; the launch traced here: 117 us
  Pallas kernels  41 us (35%)
  starting transfers between devices  37.2 us (32%)
  waiting for transfers between devices  34 us (29%)
  local copies, waits for them, and re-layouts  3.52 us (3%)
  between operations  1.21 us (1%)
    pallas_call x40, Pallas kernels, run(): pl.pallas_call(marked, name=name, out_shape=[SPACES[id(spec)](out.shape,...  41 us
    ppermute x34, starting transfers between devices, swap(): return lax.ppermute(values, axis, pairs)  37.2 us
    ppermute x34, waiting for transfers between devices, swap(): return lax.ppermute(values, axis, pairs)  34 us
    unnamed x30, local copies, waits for them, and re-layouts  3.37 us
  transfers between devices with their start and end apart: 34, of which 15 were waited for; matrix products, arithmetic and copies ran while one was open for 1% of the time, Pallas kernels for 32%

profile of v5, /device:TPU:0, one launch (start us, length us, event | category | flops | bytes accessed | tf_op | source)
XLA Modules:
  0.0 117.0 jit_solution(964940600984311638)
XLA Ops:
  1.2 2.0 %field.1 = (bf16[80,2048]{1,0:T(8,128)(2,1)S(1)}, bf16[80,2048]{1,0:T(8,128)(2,1)S(1)}, bf16[80,2048]{1,0:T(8,128)(2,1)S(1)}, f32[8,128]{1,0:T(8,128)S(1)}) custom-call(s32[1]{0:T(128)} %bitcast.refs_0_, s32[32]{0:T(128)} %refs_1_.2, s32[32]{0:T(128)} %refs_2_.2, bf16[80,2048]{1,0:T(8,128)(2,1)} %refs_3_.1, bf16[80,8192]{1,0:T(8,128)(2,1)} %refs_4_.1, ...), custom_call_target="tpu_custom_call" | custom-call | flops 10000000000 | tf_op jit(solution)/shard_map/field/pallas_call | solution.py:345
  4.9 2.7 %collective-permute-start.1 = (bf16[1,160,1024]{2,1,0:T(8,128)(2,1)S(1)}, bf16[1,160,1024]{2,1,0:T(8,128)(2,1)S(1)}, u32[]{:S(2)}, u32[]{:S(2)}) collective-permute-start(bf16[1,160,1024]{2,1,0:T(8,128)(2,1)S(1)} %get-tuple-element.106.refs_0_), channel_id=1, source_target_pairs={{0,2},{1,5},{2,0},{3,7},{4,6},{5,1},{6,4},{7,3},{8,10},{9,13},{10,... | collective-permute-start | bytes 983048 | tf_op jit(solution)/shard_map/zero_near/ppermute | solution.py:381
  7.6 1.5 %collective-permute-start.2 = (bf16[1,160,1024]{2,1,0:T(8,128)(2,1)S(1)}, bf16[1,160,1024]{2,1,0:T(8,128)(2,1)S(1)}, u32[]{:S(2)}, u32[]{:S(2)}) collective-permute-start(bf16[1,160,1024]{2,1,0:T(8,128)(2,1)S(1)} %get-tuple-element.106.refs_0_), channel_id=1, source_target_pairs={{0,4},{1,3},{2,6},{3,1},{4,0},{5,7},{6,2},{7,5},{8,12},{9,11},{10,... | collective-permute-start | bytes 983048 | tf_op jit(solution)/shard_map/zero_across/ppermute | solution.py:381
  9.1 5.3 %back_two.1 = (bf16[1,160,1024]{2,1,0:T(8,128)(2,1)S(1)}, bf16[1,160,1024]{2,1,0:T(8,128)(2,1)S(1)}, f32[2,160,1024]{2,1,0:T(8,128)S(1)}, f32[8,128]{1,0:T(8,128)S(1)}) custom-call(s32[4]{0:T(128)S(1)} %get-tuple-element.201.refs_0_.refs_1_, bf16[80,2048]{1,0:T(8,128)(2,1)S(1)} %get-tuple-element.103.refs_1_, ...), custom_call_target="tpu_custom_call" | custom-call | flops 10000000000 | tf_op jit(solution)/shard_map/back_two/pallas_call | solution.py:345
  16.0 2.1 %collective-permute-start.7 = (bf16[1,160,1024]{2,1,0:T(8,128)(2,1)S(1)}, bf16[1,160,1024]{2,1,0:T(8,128)(2,1)S(1)}, u32[]{:S(2)}, u32[]{:S(2)}) collective-permute-start(bf16[1,160,1024]{2,1,0:T(8,128)(2,1)S(1)} %get-tuple-element.118), channel_id=1, source_target_pairs={{0,4},{1,3},{2,6},{3,1},{4,0},{5,7},{6,2},{7,5},{8,12},{9,11},{10,... | collective-permute-start | bytes 983048 | tf_op jit(solution)/shard_map/zero_beyond/ppermute | solution.py:381
  18.1 3.5 %collective-permute-done.6.refs_1_ = bf16[1,160,1024]{2,1,0:T(8,128)(2,1)S(1)} collective-permute-done((bf16[1,160,1024]{2,1,0:T(8,128)(2,1)S(1)}, bf16[1,160,1024]{2,1,0:T(8,128)(2,1)S(1)}, u32[]{:S(2)}, u32[]{:S(2)}) %collective-permute-start.6) | collective-permute-done | bytes 327712 | tf_op jit(solution)/shard_map/two_last/ppermute | solution.py:381
  22.8 2.9 %collective-permute-done.7.refs_0_ = bf16[1,160,1024]{2,1,0:T(8,128)(2,1)S(1)} collective-permute-done((bf16[1,160,1024]{2,1,0:T(8,128)(2,1)S(1)}, bf16[1,160,1024]{2,1,0:T(8,128)(2,1)S(1)}, u32[]{:S(2)}, u32[]{:S(2)}) %collective-permute-start.7) | collective-permute-done | bytes 327712 | tf_op jit(solution)/shard_map/zero_beyond/ppermute | solution.py:381
  25.9 4.8 %conv_one.1 = (bf16[640,1024]{1,0:T(8,128)(2,1)S(1)}, f32[80,1024]{1,0:T(8,128)S(1)}, f32[80,1024]{1,0:T(8,128)S(1)}, bf16[1,160,1024]{2,1,0:T(8,128)(2,1)S(1)}, f32[8,128]{1,0:T(8,128)S(1)}) custom-call(s32[1]{0:T(128)} %bitcast.refs_0_, s32[4]{0:T(128)S(1)} %get-tuple-element.201.refs_0_.refs_1_, bf16[3,160,1024]{2,1,0:T(8,128)(2,1)S(1)} %get-tuple-element.117.refs_2_, ...), custom_call_target="tpu_custom_call" | custom-call | flops 10000000000 | tf_op jit(solution)/shard_map/conv_one/pallas_call | solution.py:345
  30.7 1.4 %collective-permute-done.8.refs_2_ = bf16[1,160,1024]{2,1,0:T(8,128)(2,1)S(1)} collective-permute-done((bf16[1,160,1024]{2,1,0:T(8,128)(2,1)S(1)}, bf16[1,160,1024]{2,1,0:T(8,128)(2,1)S(1)}, u32[]{:S(2)}, u32[]{:S(2)}) %collective-permute-start.8) | collective-permute-done | bytes 327712 | tf_op jit(solution)/shard_map/two_near/ppermute | solution.py:381
  33.8 1.5 %grad_one_a.1 = (bf16[400,640]{1,0:T(8,128)(2,1)S(1)}, f32[8,128]{1,0:T(8,128)S(1)}) custom-call(bf16[80,1024]{1,0:T(8,128)(2,1)S(1)} %get-tuple-element.128.refs_0_.refs_1_, bf16[80,1024]{1,0:T(8,128)(2,1)S(1)} %collective-permute-done.10.refs_1_, bf16[640,1024]{1,0:T(8,128)(2,1)S(1)} %get-tuple-element.130.refs_2_, ...), custom_call_target="tpu_custom_call" | custom-call | flops 500000000 | tf_op jit(solution)/shard_map/grad_one_a/pallas_call | solution.py:345
  37.2 3.5 %collective-permute-start.16 = (bf16[400,640]{1,0:T(8,128)(2,1)S(1)}, bf16[400,640]{1,0:T(8,128)(2,1)S(1)}, u32[]{:S(2)}, u32[]{:S(2)}) collective-permute-start(bf16[400,640]{1,0:T(8,128)(2,1)S(1)} %get-tuple-element.141.refs_0_), channel_id=1, source_target_pairs={{0,8},{24,16},{1,9},{25,17},{2,10},{26,18},{3,11},{27,19},{4,12},{... | collective-permute-start | bytes 1536008 | tf_op jit(solution)/shard_map/one_a_in/ppermute | solution.py:381
  42.0 5.3 %back_one.1 = (bf16[2,160,1024]{2,1,0:T(8,128)(2,1)S(1)}, f32[2,160,1024]{2,1,0:T(8,128)S(1)}, f32[8,128]{1,0:T(8,128)S(1)}) custom-call(s32[4]{0:T(128)S(1)} %get-tuple-element.201.refs_0_.refs_1_, bf16[80,1024]{1,0:T(8,128)(2,1)S(1)} %get-tuple-element.128.refs_0_.refs_1_, bf16[80,1024]{1,0:T(8,128)(2,1)S(1)} %get-tuple-element.129.refs_2_, ...), custom_call_target="tpu_custom_call" | custom-call | flops 30000001024 | tf_op jit(solution)/shard_map/back_one/pallas_call | solution.py:345
  52.4 3.1 %collective-permute-done.15.refs_0_ = bf16[1,160,1024]{2,1,0:T(8,128)(2,1)S(1)} collective-permute-done((bf16[1,160,1024]{2,1,0:T(8,128)(2,1)S(1)}, bf16[1,160,1024]{2,1,0:T(8,128)(2,1)S(1)}, u32[]{:S(2)}, u32[]{:S(2)}) %collective-permute-start.15) | collective-permute-done | bytes 327712 | tf_op jit(solution)/shard_map/one_beyond/ppermute | solution.py:381
  58.2 2.6 %grad_two.1 = (bf16[400,640]{1,0:T(8,128)(2,1)S(1)}, bf16[336,640]{1,0:T(8,128)(2,1)S(1)}, f32[8,128]{1,0:T(8,128)S(1)}) custom-call(s32[1]{0:T(128)} %bitcast.refs_0_, bf16[80,2048]{1,0:T(8,128)(2,1)S(1)} %copy-done.1, bf16[640,1024]{1,0:T(8,128)(2,1)S(1)} %get-tuple-element.148.refs_2_.refs_0_, bf16[640,1024]{1,0:T(8,128)(2,1)S(1)} %get-tuple-element.151.refs_3_, ...), custom_call_target="tpu_custom_call" | custom-call | flops 20000000000 | tf_op jit(solution)/shard_map/grad_two/pallas_call | solution.py:345
  60.8 4.2 %collective-permute-start.24 = (bf16[400,640]{1,0:T(8,128)(2,1)S(1)}, bf16[400,640]{1,0:T(8,128)(2,1)S(1)}, u32[]{:S(2)}, u32[]{:S(2)}) collective-permute-start(bf16[400,640]{1,0:T(8,128)(2,1)S(1)} %get-tuple-element.166.refs_0_), channel_id=1, source_target_pairs={{0,8},{24,16},{1,9},{25,17},{2,10},{26,18},{3,11},{27,19},{4,12},{... | collective-permute-start | bytes 1536008 | tf_op jit(solution)/shard_map/two_a_in/ppermute | solution.py:381
  68.1 6.1 %collective-permute-start.22 = (bf16[336,640]{1,0:T(8,128)(2,1)}, bf16[336,640]{1,0:T(8,128)(2,1)}, u32[]{:S(2)}, u32[]{:S(2)}) collective-permute-start(bf16[336,640]{1,0:T(8,128)(2,1)} %get-tuple-element.164.refs_0_), channel_id=1, source_target_pairs={{0,8},{24,16},{1,9},{25,17},{2,10},{26,18},{3,11},{27,19},{4,12},{... | collective-permute-start | bytes 1290248 | tf_op jit(solution)/shard_map/two_b_in/ppermute | solution.py:381
  74.3 3.1 %conv_two.1 = (f32[80,1024]{1,0:T(8,128)S(1)}, f32[80,1024]{1,0:T(8,128)S(1)}, f32[8,128]{1,0:T(8,128)S(1)}) custom-call(bf16[640,1024]{1,0:T(8,128)(2,1)S(1)} %get-tuple-element.148.refs_2_.refs_0_, bf16[720,640]{1,0:T(8,128)(2,1)S(1)} %bitcast.8, bf16[720,640]{1,0:T(8,128)(2,1)S(1)} %collective-permute-done.3.refs_4_.refs_2_, ...), custom_call_target="tpu_custom_call" | custom-call | flops 100000000 | tf_op jit(solution)/shard_map/conv_two/pallas_call | solution.py:345
  81.0 4.5 %collective-permute-done.22.refs_1_ = bf16[336,640]{1,0:T(8,128)(2,1)} collective-permute-done((bf16[336,640]{1,0:T(8,128)(2,1)}, bf16[336,640]{1,0:T(8,128)(2,1)}, u32[]{:S(2)}, u32[]{:S(2)}) %collective-permute-start.22) | collective-permute-done | bytes 430112 | tf_op jit(solution)/shard_map/two_b_in/ppermute | solution.py:381
  91.0 1.8 %collective-permute-done.27.refs_4_ = bf16[336,640]{1,0:T(8,128)(2,1)} collective-permute-done((bf16[336,640]{1,0:T(8,128)(2,1)S(1)}, bf16[336,640]{1,0:T(8,128)(2,1)}, u32[]{:S(2)}, u32[]{:S(2)}) %collective-permute-start.27) | collective-permute-done | bytes 430112 | tf_op jit(solution)/shard_map/one_b_out/ppermute | solution.py:381
  92.8 2.4 %finish_one.1 = (f32[720,640]{1,0:T(8,128)}, f32[80]{0:T(128)S(1)}, f32[8,128]{1,0:T(8,128)S(1)}) custom-call(s32[1]{0:T(128)} %bitcast.3.refs_0_, bf16[400,640]{1,0:T(8,128)(2,1)S(1)} %get-tuple-element.163.refs_1_, bf16[400,640]{1,0:T(8,128)(2,1)S(1)} %get-tuple-element.174.refs_2_, bf16[336,640]{1,0:T(8,128)(2,1)S(1)} %get-tuple-element.175.refs_3_, ...), custom_call_target="tpu_custom_call" | custom-call | flops 10000000000 | tf_op jit(solution)/shard_map/finish_one/pallas_call | solution.py:345
  95.3 4.0 %collective-permute-done.25.refs_1_.refs_2_ = bf16[2,160,1024]{2,1,0:T(8,128)(2,1)S(1)} collective-permute-done((bf16[2,160,1024]{2,1,0:T(8,128)(2,1)S(1)}, bf16[2,160,1024]{2,1,0:T(8,128)(2,1)S(1)}, u32[]{:S(2)}, u32[]{:S(2)}) %collective-permute-start.25) | collective-permute-done | bytes 655392 | tf_op jit(solution)/shard_map/one_near/ppermute | solution.py:381
  102.1 4.4 %collective-permute-done.31.refs_3_ = bf16[1,160,1024]{2,1,0:T(8,128)(2,1)S(1)} collective-permute-done((bf16[1,160,1024]{2,1,0:T(8,128)(2,1)S(1)}, bf16[1,160,1024]{2,1,0:T(8,128)(2,1)S(1)}, u32[]{:S(2)}, u32[]{:S(2)}) %collective-permute-start.31) | collective-permute-done | bytes 327712 | tf_op jit(solution)/shard_map/one_far/ppermute | solution.py:381
  110.1 4.8 %collective-permute-done.33.refs_2_ = bf16[336,640]{1,0:T(8,128)(2,1)S(1)} collective-permute-done((bf16[336,640]{1,0:T(8,128)(2,1)S(1)}, bf16[336,640]{1,0:T(8,128)(2,1)S(1)}, u32[]{:S(2)}, u32[]{:S(2)}) %collective-permute-start.33) | collective-permute-done | bytes 430112 | tf_op jit(solution)/shard_map/two_b_out/ppermute | solution.py:381
  114.9 1.6 %finish_two.1 = (f32[720,640]{1,0:T(8,128)}, f32[80]{0:T(128)S(1)}, f32[8,128]{1,0:T(8,128)}) custom-call(s32[1]{0:T(128)} %bitcast.3.refs_0_, bf16[336,640]{1,0:T(8,128)(2,1)S(1)} %get-tuple-element.195.refs_1_, bf16[336,640]{1,0:T(8,128)(2,1)S(1)} %collective-permute-done.33.refs_2_, ...), custom_call_target="tpu_custom_call", output_to_operand_aliasing={{0}: (3, {})} | custom-call | flops 99999997952 | tf_op jit(solution)/shard_map/finish_two/pallas_call | solution.py:345
  (117 shorter events, 36.7 us)
Async XLA Ops:
  0.6 8.5 %collective-permute-start.3 = (bf16[720,640]{1,0:T(8,128)(2,1)}, bf16[720,640]{1,0:T(8,128)(2,1)S(1)}, u32[]{:S(2)}, u32[]{:S(2)}) collective-permute-start(bf16[720,640]{1,0:T(8,128)(2,1)} %bitcast.6), channel_id=1, source_target_pairs={{0,1},{1,0},{2,3},{3,2},{4,5},{5,4},{6,7},{7,6},{8,9},{9,8},{10,11... | collective-permute-start | bytes 2764808 | tf_op jit(solution)/shard_map/kernel_two/ppermute | solution.py:381
  3.3 12.6 %collective-permute-start.4 = (bf16[720,640]{1,0:T(8,128)(2,1)}, bf16[720,640]{1,0:T(8,128)(2,1)S(1)}, u32[]{:S(2)}, u32[]{:S(2)}) collective-permute-start(bf16[720,640]{1,0:T(8,128)(2,1)} %bitcast.2.refs_4_.refs_3_), channel_id=1, source_target_pairs={{0,1},{1,0},{2,3},{3,2},{4,5},{5,4},{6,7},{7,6},{8,9},{9,8},{10,11... | collective-permute-start | bytes 2764808 | tf_op jit(solution)/shard_map/kernel_one/ppermute | solution.py:381
  3.8 11.2 %collective-permute-start.5 = (bf16[80,128]{1,0:T(8,128)(2,1)S(1)}, bf16[80,128]{1,0:T(8,128)(2,1)S(1)}, u32[]{:S(2)}, u32[]{:S(2)}) collective-permute-start(bf16[80,128]{1,0:T(8,128)(2,1)S(1)} %broadcast_in_dim.4.refs_6_), channel_id=1, source_target_pairs={{0,1},{1,0},{2,3},{3,2},{4,5},{5,4},{6,7},{7,6},{8,9},{9,8},{10,11... | collective-permute-start | bytes 61448 | tf_op jit(solution)/shard_map/bias/ppermute | solution.py:381
  4.9 10.2 %collective-permute-start.1 = (bf16[1,160,1024]{2,1,0:T(8,128)(2,1)S(1)}, bf16[1,160,1024]{2,1,0:T(8,128)(2,1)S(1)}, u32[]{:S(2)}, u32[]{:S(2)}) collective-permute-start(bf16[1,160,1024]{2,1,0:T(8,128)(2,1)S(1)} %get-tuple-element.106.refs_0_), channel_id=1, source_target_pairs={{0,2},{1,5},{2,0},{3,7},{4,6},{5,1},{6,4},{7,3},{8,10},{9,13},{10,... | collective-permute-start | bytes 983048 | tf_op jit(solution)/shard_map/zero_near/ppermute | solution.py:381
  7.6 8.3 %collective-permute-start.2 = (bf16[1,160,1024]{2,1,0:T(8,128)(2,1)S(1)}, bf16[1,160,1024]{2,1,0:T(8,128)(2,1)S(1)}, u32[]{:S(2)}, u32[]{:S(2)}) collective-permute-start(bf16[1,160,1024]{2,1,0:T(8,128)(2,1)S(1)} %get-tuple-element.106.refs_0_), channel_id=1, source_target_pairs={{0,4},{1,3},{2,6},{3,1},{4,0},{5,7},{6,2},{7,5},{8,12},{9,11},{10,... | collective-permute-start | bytes 983048 | tf_op jit(solution)/shard_map/zero_across/ppermute | solution.py:381
  16.0 9.8 %collective-permute-start.7 = (bf16[1,160,1024]{2,1,0:T(8,128)(2,1)S(1)}, bf16[1,160,1024]{2,1,0:T(8,128)(2,1)S(1)}, u32[]{:S(2)}, u32[]{:S(2)}) collective-permute-start(bf16[1,160,1024]{2,1,0:T(8,128)(2,1)S(1)} %get-tuple-element.118), channel_id=1, source_target_pairs={{0,4},{1,3},{2,6},{3,1},{4,0},{5,7},{6,2},{7,5},{8,12},{9,11},{10,... | collective-permute-start | bytes 983048 | tf_op jit(solution)/shard_map/zero_beyond/ppermute | solution.py:381
  18.1 14.4 %collective-permute-start.11 = (bf16[3,160,1024]{2,1,0:T(8,128)(2,1)S(1)}, bf16[3,160,1024]{2,1,0:T(8,128)(2,1)S(1)}, u32[]{:S(2)}, u32[]{:S(2)}) collective-permute-start(bf16[3,160,1024]{2,1,0:T(8,128)(2,1)S(1)} %get-tuple-element.117.refs_2_), channel_id=1, source_target_pairs={{0,1},{1,0},{2,3},{3,2},{4,5},{5,4},{6,7},{7,6},{8,9},{9,8},{10,11... | collective-permute-start | bytes 2949128 | tf_op jit(solution)/shard_map/zero_pair/ppermute | solution.py:381
  21.7 10.4 %collective-permute-start.8 = (bf16[1,160,1024]{2,1,0:T(8,128)(2,1)S(1)}, bf16[1,160,1024]{2,1,0:T(8,128)(2,1)S(1)}, u32[]{:S(2)}, u32[]{:S(2)}) collective-permute-start(bf16[1,160,1024]{2,1,0:T(8,128)(2,1)S(1)} %get-tuple-element.123), channel_id=1, source_target_pairs={{0,4},{1,3},{2,6},{3,1},{4,0},{5,7},{6,2},{7,5},{8,12},{9,11},{10,... | collective-permute-start | bytes 983048 | tf_op jit(solution)/shard_map/two_near/ppermute | solution.py:381
  22.3 9.8 %collective-permute-start.9 = (bf16[1,160,1024]{2,1,0:T(8,128)(2,1)S(1)}, bf16[1,160,1024]{2,1,0:T(8,128)(2,1)S(1)}, u32[]{:S(2)}, u32[]{:S(2)}) collective-permute-start(bf16[1,160,1024]{2,1,0:T(8,128)(2,1)S(1)} %get-tuple-element.124), channel_id=1, source_target_pairs={{0,2},{1,5},{2,0},{3,7},{4,6},{5,1},{6,4},{7,3},{8,10},{9,13},{10,... | collective-permute-start | bytes 983048 | tf_op jit(solution)/shard_map/two_far/ppermute | solution.py:381
  35.3 12.8 %collective-permute-start.13 = (bf16[1,160,1024]{2,1,0:T(8,128)(2,1)S(1)}, bf16[1,160,1024]{2,1,0:T(8,128)(2,1)S(1)}, u32[]{:S(2)}, u32[]{:S(2)}) collective-permute-start(bf16[1,160,1024]{2,1,0:T(8,128)(2,1)S(1)} %get-tuple-element.135.refs_0_), channel_id=1, source_target_pairs={{0,2},{1,5},{2,0},{3,7},{4,6},{5,1},{6,4},{7,3},{8,10},{9,13},{10,... | collective-permute-start | bytes 983048 | tf_op jit(solution)/shard_map/one_near/ppermute | solution.py:381
  35.9 12.2 %collective-permute-start.14 = (bf16[1,160,1024]{2,1,0:T(8,128)(2,1)S(1)}, bf16[1,160,1024]{2,1,0:T(8,128)(2,1)S(1)}, u32[]{:S(2)}, u32[]{:S(2)}) collective-permute-start(bf16[1,160,1024]{2,1,0:T(8,128)(2,1)S(1)} %get-tuple-element.135.refs_0_), channel_id=1, source_target_pairs={{0,4},{1,3},{2,6},{3,1},{4,0},{5,7},{6,2},{7,5},{8,12},{9,11},{10,... | collective-permute-start | bytes 983048 | tf_op jit(solution)/shard_map/one_across/ppermute | solution.py:381
  37.2 14.1 %collective-permute-start.16 = (bf16[400,640]{1,0:T(8,128)(2,1)S(1)}, bf16[400,640]{1,0:T(8,128)(2,1)S(1)}, u32[]{:S(2)}, u32[]{:S(2)}) collective-permute-start(bf16[400,640]{1,0:T(8,128)(2,1)S(1)} %get-tuple-element.141.refs_0_), channel_id=1, source_target_pairs={{0,8},{24,16},{1,9},{25,17},{2,10},{26,18},{3,11},{27,19},{4,12},{... | collective-permute-start | bytes 1536008 | tf_op jit(solution)/shard_map/one_a_in/ppermute | solution.py:381
  49.2 15.8 %collective-permute-start.20 = (bf16[336,640]{1,0:T(8,128)(2,1)S(1)}, bf16[336,640]{1,0:T(8,128)(2,1)S(1)}, u32[]{:S(2)}, u32[]{:S(2)}) collective-permute-start(bf16[336,640]{1,0:T(8,128)(2,1)S(1)} %get-tuple-element.154.refs_0_), channel_id=1, source_target_pairs={{0,8},{24,16},{1,9},{25,17},{2,10},{26,18},{3,11},{27,19},{4,12},{... | collective-permute-start | bytes 1290248 | tf_op jit(solution)/shard_map/one_b_in/ppermute | solution.py:381
  51.5 15.1 %collective-permute-start.17 = (bf16[400,640]{1,0:T(8,128)(2,1)S(1)}, bf16[400,640]{1,0:T(8,128)(2,1)S(1)}, u32[]{:S(2)}, u32[]{:S(2)}) collective-permute-start(bf16[400,640]{1,0:T(8,128)(2,1)S(1)} %get-tuple-element.149.refs_0_), channel_id=1, source_target_pairs={{8,16},{16,8},{9,17},{17,9},{10,18},{18,10},{11,19},{19,11},{12,20... | collective-permute-start | bytes 1536008 | tf_op jit(solution)/shard_map/one_a_middle/ppermute | solution.py:381
  60.8 17.3 %collective-permute-start.24 = (bf16[400,640]{1,0:T(8,128)(2,1)S(1)}, bf16[400,640]{1,0:T(8,128)(2,1)S(1)}, u32[]{:S(2)}, u32[]{:S(2)}) collective-permute-start(bf16[400,640]{1,0:T(8,128)(2,1)S(1)} %get-tuple-element.166.refs_0_), channel_id=1, source_target_pairs={{0,8},{24,16},{1,9},{25,17},{2,10},{26,18},{3,11},{27,19},{4,12},{... | collective-permute-start | bytes 1536008 | tf_op jit(solution)/shard_map/two_a_in/ppermute | solution.py:381
  65.1 14.4 %collective-permute-start.23 = (bf16[336,640]{1,0:T(8,128)(2,1)S(1)}, bf16[336,640]{1,0:T(8,128)(2,1)S(1)}, u32[]{:S(2)}, u32[]{:S(2)}) collective-permute-start(bf16[336,640]{1,0:T(8,128)(2,1)S(1)} %get-tuple-element.165.refs_0_), channel_id=1, source_target_pairs={{8,16},{16,8},{9,17},{17,9},{10,18},{18,10},{11,19},{19,11},{12,20... | collective-permute-start | bytes 1290248 | tf_op jit(solution)/shard_map/one_b_middle/ppermute | solution.py:381
  66.7 20.7 %collective-permute-start.21 = (bf16[400,640]{1,0:T(8,128)(2,1)S(1)}, bf16[400,640]{1,0:T(8,128)(2,1)}, u32[]{:S(2)}, u32[]{:S(2)}) collective-permute-start(bf16[400,640]{1,0:T(8,128)(2,1)S(1)} %get-tuple-element.163.refs_1_), channel_id=1, source_target_pairs={{8,0},{16,24},{9,1},{17,25},{10,2},{18,26},{11,3},{19,27},{12,4},{... | collective-permute-start | bytes 1536008 | tf_op jit(solution)/shard_map/one_a_out/ppermute | solution.py:381
  68.1 17.3 %collective-permute-start.22 = (bf16[336,640]{1,0:T(8,128)(2,1)}, bf16[336,640]{1,0:T(8,128)(2,1)}, u32[]{:S(2)}, u32[]{:S(2)}) collective-permute-start(bf16[336,640]{1,0:T(8,128)(2,1)} %get-tuple-element.164.refs_0_), channel_id=1, source_target_pairs={{0,8},{24,16},{1,9},{25,17},{2,10},{26,18},{3,11},{27,19},{4,12},{... | collective-permute-start | bytes 1290248 | tf_op jit(solution)/shard_map/two_b_in/ppermute | solution.py:381
  78.8 10.7 %collective-permute-start.28 = (bf16[400,640]{1,0:T(8,128)(2,1)S(1)}, bf16[400,640]{1,0:T(8,128)(2,1)S(1)}, u32[]{:S(2)}, u32[]{:S(2)}) collective-permute-start(bf16[400,640]{1,0:T(8,128)(2,1)S(1)} %get-tuple-element.176.refs_0_), channel_id=1, source_target_pairs={{8,16},{16,8},{9,17},{17,9},{10,18},{18,10},{11,19},{19,11},{12,20... | collective-permute-start | bytes 1536008 | tf_op jit(solution)/shard_map/two_a_middle/ppermute | solution.py:381
  79.7 13.1 %collective-permute-start.27 = (bf16[336,640]{1,0:T(8,128)(2,1)S(1)}, bf16[336,640]{1,0:T(8,128)(2,1)}, u32[]{:S(2)}, u32[]{:S(2)}) collective-permute-start(bf16[336,640]{1,0:T(8,128)(2,1)S(1)} %get-tuple-element.175.refs_3_), channel_id=1, source_target_pairs={{8,0},{16,24},{9,1},{17,25},{10,2},{18,26},{11,3},{19,27},{12,4},{... | collective-permute-start | bytes 1290248 | tf_op jit(solution)/shard_map/one_b_out/ppermute | solution.py:381
  86.7 8.5 %collective-permute-start.26 = (bf16[336,640]{1,0:T(8,128)(2,1)S(1)}, bf16[336,640]{1,0:T(8,128)(2,1)S(1)}, u32[]{:S(2)}, u32[]{:S(2)}) collective-permute-start(bf16[336,640]{1,0:T(8,128)(2,1)S(1)} %get-tuple-element.173.refs_0_), channel_id=1, source_target_pairs={{8,16},{16,8},{9,17},{17,9},{10,18},{18,10},{11,19},{19,11},{12,20... | collective-permute-start | bytes 1290248 | tf_op jit(solution)/shard_map/two_b_middle/ppermute | solution.py:381
  88.7 10.7 %collective-permute-start.25 = (bf16[2,160,1024]{2,1,0:T(8,128)(2,1)S(1)}, bf16[2,160,1024]{2,1,0:T(8,128)(2,1)S(1)}, u32[]{:S(2)}, u32[]{:S(2)}) collective-permute-start(bf16[2,160,1024]{2,1,0:T(8,128)(2,1)S(1)} %get-tuple-element.172), channel_id=1, source_target_pairs={{0,4},{1,3},{2,6},{3,1},{4,0},{5,7},{6,2},{7,5},{8,12},{9,11},{10,... | collective-permute-start | bytes 1966088 | tf_op jit(solution)/shard_map/one_near/ppermute | solution.py:381
  89.7 17.1 %collective-permute-start.30 = (bf16[400,640]{1,0:T(8,128)(2,1)S(1)}, bf16[400,640]{1,0:T(8,128)(2,1)S(1)}, u32[]{:S(2)}, u32[]{:S(2)}) collective-permute-start(bf16[400,640]{1,0:T(8,128)(2,1)S(1)} %get-tuple-element.183.refs_1_), channel_id=1, source_target_pairs={{8,0},{16,24},{9,1},{17,25},{10,2},{18,26},{11,3},{19,27},{12,4},{... | collective-permute-start | bytes 1536008 | tf_op jit(solution)/shard_map/two_a_out/ppermute | solution.py:381
  100.2 14.7 %collective-permute-start.33 = (bf16[336,640]{1,0:T(8,128)(2,1)S(1)}, bf16[336,640]{1,0:T(8,128)(2,1)S(1)}, u32[]{:S(2)}, u32[]{:S(2)}) collective-permute-start(bf16[336,640]{1,0:T(8,128)(2,1)S(1)} %get-tuple-element.195.refs_1_), channel_id=1, source_target_pairs={{8,0},{16,24},{9,1},{17,25},{10,2},{18,26},{11,3},{19,27},{12,4},{... | collective-permute-start | bytes 1290248 | tf_op jit(solution)/shard_map/two_b_out/ppermute | solution.py:381
  (24 other events, 87.6 us)

commit v6 on v5

--- a/solution.py
+++ b/solution.py
@@ -15,7 +15,7 @@
 SMALL = ("place", "copy", "add", "join", "onward", "sum", "assemble")
 EXTRA = 16
 PARTS_ONE, PARTS_TWO = (5, 9), (5, 9)
-TILE = 256
+TILE = 512
 CONV_TILE = 512
 
 

time: 118 us -> 118 us (level)
  starting transfers between devices: 37.2 us -> 38.5 us
  Pallas kernels: 41 us -> 39.8 us
    ppermute x34, starting transfers between devices: 37.2 us -> 38.5 us  [swap(): return lax.ppermute(values, axis, pairs)]
    pallas_call x40, Pallas kernels: 41 us -> 39.8 us  [run(): pl.pallas_call(marked, name=name, out_shape=[SPACES[id(spec)](out.shape,...]
  transfers between devices with their start and end apart: 34 -> 34, of which waited for: 15 -> 15; matrix products, arithmetic and copies ran while one was open for 1% -> 1% of each run, Pallas kernels for 32% -> 31%
where the time goes in v6:
time: 118 us; the launch traced here: 117 us
  Pallas kernels  39.8 us (34%)
  starting transfers between devices  38.5 us (33%)
  waiting for transfers between devices  34.2 us (29%)
  local copies, waits for them, and re-layouts  3.52 us (3%)
  between operations  1.23 us (1%)
    pallas_call x40, Pallas kernels, run(): pl.pallas_call(marked, name=name, out_shape=[SPACES[id(spec)](out.shape,...  39.8 us
    ppermute x34, starting transfers between devices, swap(): return lax.ppermute(values, axis, pairs)  38.5 us
    ppermute x34, waiting for transfers between devices, swap(): return lax.ppermute(values, axis, pairs)  34.2 us
    unnamed x30, local copies, waits for them, and re-layouts  3.37 us
  transfers between devices with their start and end apart: 34, of which 15 were waited for; matrix products, arithmetic and copies ran while one was open for 1% of the time, Pallas kernels for 31%

profile of v6, /device:TPU:0, one launch (start us, length us, event | category | flops | bytes accessed | tf_op | source)
XLA Modules:
  0.0 117.3 jit_solution(11068297961657758890)
XLA Ops:
  1.2 2.0 %field.1 = (bf16[80,2048]{1,0:T(8,128)(2,1)S(1)}, bf16[80,2048]{1,0:T(8,128)(2,1)S(1)}, bf16[80,2048]{1,0:T(8,128)(2,1)S(1)}, f32[8,128]{1,0:T(8,128)S(1)}) custom-call(s32[1]{0:T(128)} %bitcast.refs_0_, s32[32]{0:T(128)} %refs_1_.2, s32[32]{0:T(128)} %refs_2_.2, bf16[80,2048]{1,0:T(8,128)(2,1)} %refs_3_.1, bf16[80,8192]{1,0:T(8,128)(2,1)} %refs_4_.1, ...), custom_call_target="tpu_custom_call" | custom-call | flops 10000000000 | tf_op jit(solution)/shard_map/field/pallas_call | solution.py:345
  4.9 2.7 %collective-permute-start.1 = (bf16[1,160,1024]{2,1,0:T(8,128)(2,1)S(1)}, bf16[1,160,1024]{2,1,0:T(8,128)(2,1)S(1)}, u32[]{:S(2)}, u32[]{:S(2)}) collective-permute-start(bf16[1,160,1024]{2,1,0:T(8,128)(2,1)S(1)} %get-tuple-element.106.refs_0_), channel_id=1, source_target_pairs={{0,2},{1,5},{2,0},{3,7},{4,6},{5,1},{6,4},{7,3},{8,10},{9,13},{10,... | collective-permute-start | bytes 983048 | tf_op jit(solution)/shard_map/zero_near/ppermute | solution.py:381
  9.1 4.7 %back_two.1 = (bf16[1,160,1024]{2,1,0:T(8,128)(2,1)S(1)}, bf16[1,160,1024]{2,1,0:T(8,128)(2,1)S(1)}, f32[2,160,1024]{2,1,0:T(8,128)S(1)}, f32[8,128]{1,0:T(8,128)S(1)}) custom-call(s32[4]{0:T(128)S(1)} %get-tuple-element.201.refs_0_.refs_1_, bf16[80,2048]{1,0:T(8,128)(2,1)S(1)} %get-tuple-element.103.refs_1_, ...), custom_call_target="tpu_custom_call" | custom-call | flops 10000000000 | tf_op jit(solution)/shard_map/back_two/pallas_call | solution.py:345
  16.0 2.3 %collective-permute-start.7 = (bf16[1,160,1024]{2,1,0:T(8,128)(2,1)S(1)}, bf16[1,160,1024]{2,1,0:T(8,128)(2,1)S(1)}, u32[]{:S(2)}, u32[]{:S(2)}) collective-permute-start(bf16[1,160,1024]{2,1,0:T(8,128)(2,1)S(1)} %get-tuple-element.118), channel_id=1, source_target_pairs={{0,4},{1,3},{2,6},{3,1},{4,0},{5,7},{6,2},{7,5},{8,12},{9,11},{10,... | collective-permute-start | bytes 983048 | tf_op jit(solution)/shard_map/zero_beyond/ppermute | solution.py:381
  18.3 2.7 %collective-permute-done.6.refs_1_ = bf16[1,160,1024]{2,1,0:T(8,128)(2,1)S(1)} collective-permute-done((bf16[1,160,1024]{2,1,0:T(8,128)(2,1)S(1)}, bf16[1,160,1024]{2,1,0:T(8,128)(2,1)S(1)}, u32[]{:S(2)}, u32[]{:S(2)}) %collective-permute-start.6) | collective-permute-done | bytes 327712 | tf_op jit(solution)/shard_map/two_last/ppermute | solution.py:381
  22.8 1.8 %collective-permute-done.7.refs_0_ = bf16[1,160,1024]{2,1,0:T(8,128)(2,1)S(1)} collective-permute-done((bf16[1,160,1024]{2,1,0:T(8,128)(2,1)S(1)}, bf16[1,160,1024]{2,1,0:T(8,128)(2,1)S(1)}, u32[]{:S(2)}, u32[]{:S(2)}) %collective-permute-start.7) | collective-permute-done | bytes 327712 | tf_op jit(solution)/shard_map/zero_beyond/ppermute | solution.py:381
  24.7 4.8 %conv_one.1 = (bf16[640,1024]{1,0:T(8,128)(2,1)S(1)}, f32[80,1024]{1,0:T(8,128)S(1)}, f32[80,1024]{1,0:T(8,128)S(1)}, bf16[1,160,1024]{2,1,0:T(8,128)(2,1)S(1)}, f32[8,128]{1,0:T(8,128)S(1)}) custom-call(s32[1]{0:T(128)} %bitcast.refs_0_, s32[4]{0:T(128)S(1)} %get-tuple-element.201.refs_0_.refs_1_, bf16[3,160,1024]{2,1,0:T(8,128)(2,1)S(1)} %get-tuple-element.117.refs_2_, ...), custom_call_target="tpu_custom_call" | custom-call | flops 10000000000 | tf_op jit(solution)/shard_map/conv_one/pallas_call | solution.py:345
  29.5 2.0 %collective-permute-done.8.refs_2_ = bf16[1,160,1024]{2,1,0:T(8,128)(2,1)S(1)} collective-permute-done((bf16[1,160,1024]{2,1,0:T(8,128)(2,1)S(1)}, bf16[1,160,1024]{2,1,0:T(8,128)(2,1)S(1)}, u32[]{:S(2)}, u32[]{:S(2)}) %collective-permute-start.8) | collective-permute-done | bytes 327712 | tf_op jit(solution)/shard_map/two_near/ppermute | solution.py:381
  35.5 1.7 %collective-permute-start.14 = (bf16[1,160,1024]{2,1,0:T(8,128)(2,1)S(1)}, bf16[1,160,1024]{2,1,0:T(8,128)(2,1)S(1)}, u32[]{:S(2)}, u32[]{:S(2)}) collective-permute-start(bf16[1,160,1024]{2,1,0:T(8,128)(2,1)S(1)} %get-tuple-element.135.refs_0_), channel_id=1, source_target_pairs={{0,4},{1,3},{2,6},{3,1},{4,0},{5,7},{6,2},{7,5},{8,12},{9,11},{10,... | collective-permute-start | bytes 983048 | tf_op jit(solution)/shard_map/one_across/ppermute | solution.py:381
  37.2 3.5 %collective-permute-start.16 = (bf16[400,640]{1,0:T(8,128)(2,1)S(1)}, bf16[400,640]{1,0:T(8,128)(2,1)S(1)}, u32[]{:S(2)}, u32[]{:S(2)}) collective-permute-start(bf16[400,640]{1,0:T(8,128)(2,1)S(1)} %get-tuple-element.141.refs_0_), channel_id=1, source_target_pairs={{0,8},{24,16},{1,9},{25,17},{2,10},{26,18},{3,11},{27,19},{4,12},{... | collective-permute-start | bytes 1536008 | tf_op jit(solution)/shard_map/one_a_in/ppermute | solution.py:381
  42.0 4.7 %back_one.1 = (bf16[2,160,1024]{2,1,0:T(8,128)(2,1)S(1)}, f32[2,160,1024]{2,1,0:T(8,128)S(1)}, f32[8,128]{1,0:T(8,128)S(1)}) custom-call(s32[4]{0:T(128)S(1)} %get-tuple-element.201.refs_0_.refs_1_, bf16[80,1024]{1,0:T(8,128)(2,1)S(1)} %get-tuple-element.128.refs_0_.refs_1_, bf16[80,1024]{1,0:T(8,128)(2,1)S(1)} %get-tuple-element.129.refs_2_, ...), custom_call_target="tpu_custom_call" | custom-call | flops 30000001024 | tf_op jit(solution)/shard_map/back_one/pallas_call | solution.py:345
  48.1 1.8 %collective-permute-start.20 = (bf16[336,640]{1,0:T(8,128)(2,1)S(1)}, bf16[336,640]{1,0:T(8,128)(2,1)S(1)}, u32[]{:S(2)}, u32[]{:S(2)}) collective-permute-start(bf16[336,640]{1,0:T(8,128)(2,1)S(1)} %get-tuple-element.154.refs_0_), channel_id=1, source_target_pairs={{0,8},{24,16},{1,9},{25,17},{2,10},{26,18},{3,11},{27,19},{4,12},{... | collective-permute-start | bytes 1290248 | tf_op jit(solution)/shard_map/one_b_in/ppermute | solution.py:381
  49.9 2.1 %collective-permute-done.16.refs_1_ = bf16[400,640]{1,0:T(8,128)(2,1)S(1)} collective-permute-done((bf16[400,640]{1,0:T(8,128)(2,1)S(1)}, bf16[400,640]{1,0:T(8,128)(2,1)S(1)}, u32[]{:S(2)}, u32[]{:S(2)}) %collective-permute-start.16) | collective-permute-done | bytes 512032 | tf_op jit(solution)/shard_map/one_a_in/ppermute | solution.py:381
  53.1 1.7 %collective-permute-done.15.refs_0_ = bf16[1,160,1024]{2,1,0:T(8,128)(2,1)S(1)} collective-permute-done((bf16[1,160,1024]{2,1,0:T(8,128)(2,1)S(1)}, bf16[1,160,1024]{2,1,0:T(8,128)(2,1)S(1)}, u32[]{:S(2)}, u32[]{:S(2)}) %collective-permute-start.15) | collective-permute-done | bytes 327712 | tf_op jit(solution)/shard_map/one_beyond/ppermute | solution.py:381
  57.6 2.6 %grad_two.1 = (bf16[400,640]{1,0:T(8,128)(2,1)S(1)}, bf16[336,640]{1,0:T(8,128)(2,1)S(1)}, f32[8,128]{1,0:T(8,128)S(1)}) custom-call(s32[1]{0:T(128)} %bitcast.refs_0_, bf16[80,2048]{1,0:T(8,128)(2,1)S(1)} %copy-done.1, bf16[640,1024]{1,0:T(8,128)(2,1)S(1)} %get-tuple-element.148.refs_2_.refs_0_, bf16[640,1024]{1,0:T(8,128)(2,1)S(1)} %get-tuple-element.151.refs_3_, ...), custom_call_target="tpu_custom_call" | custom-call | flops 20000000000 | tf_op jit(solution)/shard_map/grad_two/pallas_call | solution.py:345
  60.2 5.5 %collective-permute-start.24 = (bf16[400,640]{1,0:T(8,128)(2,1)S(1)}, bf16[400,640]{1,0:T(8,128)(2,1)S(1)}, u32[]{:S(2)}, u32[]{:S(2)}) collective-permute-start(bf16[400,640]{1,0:T(8,128)(2,1)S(1)} %get-tuple-element.166.refs_0_), channel_id=1, source_target_pairs={{0,8},{24,16},{1,9},{25,17},{2,10},{26,18},{3,11},{27,19},{4,12},{... | collective-permute-start | bytes 1536008 | tf_op jit(solution)/shard_map/two_a_in/ppermute | solution.py:381
  68.9 6.1 %collective-permute-start.22 = (bf16[336,640]{1,0:T(8,128)(2,1)}, bf16[336,640]{1,0:T(8,128)(2,1)}, u32[]{:S(2)}, u32[]{:S(2)}) collective-permute-start(bf16[336,640]{1,0:T(8,128)(2,1)} %get-tuple-element.164.refs_0_), channel_id=1, source_target_pairs={{0,8},{24,16},{1,9},{25,17},{2,10},{26,18},{3,11},{27,19},{4,12},{... | collective-permute-start | bytes 1290248 | tf_op jit(solution)/shard_map/two_b_in/ppermute | solution.py:381
  75.0 3.1 %conv_two.1 = (f32[80,1024]{1,0:T(8,128)S(1)}, f32[80,1024]{1,0:T(8,128)S(1)}, f32[8,128]{1,0:T(8,128)S(1)}) custom-call(bf16[640,1024]{1,0:T(8,128)(2,1)S(1)} %get-tuple-element.148.refs_2_.refs_0_, bf16[720,640]{1,0:T(8,128)(2,1)S(1)} %bitcast.8, bf16[720,640]{1,0:T(8,128)(2,1)S(1)} %collective-permute-done.3.refs_4_.refs_2_, ...), custom_call_target="tpu_custom_call" | custom-call | flops 100000000 | tf_op jit(solution)/shard_map/conv_two/pallas_call | solution.py:345
  81.7 4.5 %collective-permute-done.22.refs_1_ = bf16[336,640]{1,0:T(8,128)(2,1)} collective-permute-done((bf16[336,640]{1,0:T(8,128)(2,1)}, bf16[336,640]{1,0:T(8,128)(2,1)}, u32[]{:S(2)}, u32[]{:S(2)}) %collective-permute-start.22) | collective-permute-done | bytes 430112 | tf_op jit(solution)/shard_map/two_b_in/ppermute | solution.py:381
  91.0 2.5 %collective-permute-done.27.refs_4_ = bf16[336,640]{1,0:T(8,128)(2,1)} collective-permute-done((bf16[336,640]{1,0:T(8,128)(2,1)S(1)}, bf16[336,640]{1,0:T(8,128)(2,1)}, u32[]{:S(2)}, u32[]{:S(2)}) %collective-permute-start.27) | collective-permute-done | bytes 430112 | tf_op jit(solution)/shard_map/one_b_out/ppermute | solution.py:381
  93.5 2.4 %finish_one.1 = (f32[720,640]{1,0:T(8,128)}, f32[80]{0:T(128)S(1)}, f32[8,128]{1,0:T(8,128)S(1)}) custom-call(s32[1]{0:T(128)} %bitcast.3.refs_0_, bf16[400,640]{1,0:T(8,128)(2,1)S(1)} %get-tuple-element.163.refs_1_, bf16[400,640]{1,0:T(8,128)(2,1)S(1)} %get-tuple-element.174.refs_2_, bf16[336,640]{1,0:T(8,128)(2,1)S(1)} %get-tuple-element.175.refs_3_, ...), custom_call_target="tpu_custom_call" | custom-call | flops 10000000000 | tf_op jit(solution)/shard_map/finish_one/pallas_call | solution.py:345
  96.0 4.0 %collective-permute-done.25.refs_1_.refs_2_ = bf16[2,160,1024]{2,1,0:T(8,128)(2,1)S(1)} collective-permute-done((bf16[2,160,1024]{2,1,0:T(8,128)(2,1)S(1)}, bf16[2,160,1024]{2,1,0:T(8,128)(2,1)S(1)}, u32[]{:S(2)}, u32[]{:S(2)}) %collective-permute-start.25) | collective-permute-done | bytes 655392 | tf_op jit(solution)/shard_map/one_near/ppermute | solution.py:381
  102.2 5.1 %collective-permute-done.31.refs_3_ = bf16[1,160,1024]{2,1,0:T(8,128)(2,1)S(1)} collective-permute-done((bf16[1,160,1024]{2,1,0:T(8,128)(2,1)S(1)}, bf16[1,160,1024]{2,1,0:T(8,128)(2,1)S(1)}, u32[]{:S(2)}, u32[]{:S(2)}) %collective-permute-start.31) | collective-permute-done | bytes 327712 | tf_op jit(solution)/shard_map/one_far/ppermute | solution.py:381
  110.8 4.3 %collective-permute-done.33.refs_2_ = bf16[336,640]{1,0:T(8,128)(2,1)S(1)} collective-permute-done((bf16[336,640]{1,0:T(8,128)(2,1)S(1)}, bf16[336,640]{1,0:T(8,128)(2,1)S(1)}, u32[]{:S(2)}, u32[]{:S(2)}) %collective-permute-start.33) | collective-permute-done | bytes 430112 | tf_op jit(solution)/shard_map/two_b_out/ppermute | solution.py:381
  (117 shorter events, 37.3 us)
Async XLA Ops:
  0.6 8.5 %collective-permute-start.3 = (bf16[720,640]{1,0:T(8,128)(2,1)}, bf16[720,640]{1,0:T(8,128)(2,1)S(1)}, u32[]{:S(2)}, u32[]{:S(2)}) collective-permute-start(bf16[720,640]{1,0:T(8,128)(2,1)} %bitcast.6), channel_id=1, source_target_pairs={{0,1},{1,0},{2,3},{3,2},{4,5},{5,4},{6,7},{7,6},{8,9},{9,8},{10,11... | collective-permute-start | bytes 2764808 | tf_op jit(solution)/shard_map/kernel_two/ppermute | solution.py:381
  3.3 12.6 %collective-permute-start.4 = (bf16[720,640]{1,0:T(8,128)(2,1)}, bf16[720,640]{1,0:T(8,128)(2,1)S(1)}, u32[]{:S(2)}, u32[]{:S(2)}) collective-permute-start(bf16[720,640]{1,0:T(8,128)(2,1)} %bitcast.2.refs_4_.refs_3_), channel_id=1, source_target_pairs={{0,1},{1,0},{2,3},{3,2},{4,5},{5,4},{6,7},{7,6},{8,9},{9,8},{10,11... | collective-permute-start | bytes 2764808 | tf_op jit(solution)/shard_map/kernel_one/ppermute | solution.py:381
  3.8 10.6 %collective-permute-start.5 = (bf16[80,128]{1,0:T(8,128)(2,1)S(1)}, bf16[80,128]{1,0:T(8,128)(2,1)S(1)}, u32[]{:S(2)}, u32[]{:S(2)}) collective-permute-start(bf16[80,128]{1,0:T(8,128)(2,1)S(1)} %broadcast_in_dim.4.refs_6_), channel_id=1, source_target_pairs={{0,1},{1,0},{2,3},{3,2},{4,5},{5,4},{6,7},{7,6},{8,9},{9,8},{10,11... | collective-permute-start | bytes 61448 | tf_op jit(solution)/shard_map/bias/ppermute | solution.py:381
  4.9 10.2 %collective-permute-start.1 = (bf16[1,160,1024]{2,1,0:T(8,128)(2,1)S(1)}, bf16[1,160,1024]{2,1,0:T(8,128)(2,1)S(1)}, u32[]{:S(2)}, u32[]{:S(2)}) collective-permute-start(bf16[1,160,1024]{2,1,0:T(8,128)(2,1)S(1)} %get-tuple-element.106.refs_0_), channel_id=1, source_target_pairs={{0,2},{1,5},{2,0},{3,7},{4,6},{5,1},{6,4},{7,3},{8,10},{9,13},{10,... | collective-permute-start | bytes 983048 | tf_op jit(solution)/shard_map/zero_near/ppermute | solution.py:381
  16.0 8.6 %collective-permute-start.7 = (bf16[1,160,1024]{2,1,0:T(8,128)(2,1)S(1)}, bf16[1,160,1024]{2,1,0:T(8,128)(2,1)S(1)}, u32[]{:S(2)}, u32[]{:S(2)}) collective-permute-start(bf16[1,160,1024]{2,1,0:T(8,128)(2,1)S(1)} %get-tuple-element.118), channel_id=1, source_target_pairs={{0,4},{1,3},{2,6},{3,1},{4,0},{5,7},{6,2},{7,5},{8,12},{9,11},{10,... | collective-permute-start | bytes 983048 | tf_op jit(solution)/shard_map/zero_beyond/ppermute | solution.py:381
  18.3 13.6 %collective-permute-start.11 = (bf16[3,160,1024]{2,1,0:T(8,128)(2,1)S(1)}, bf16[3,160,1024]{2,1,0:T(8,128)(2,1)S(1)}, u32[]{:S(2)}, u32[]{:S(2)}) collective-permute-start(bf16[3,160,1024]{2,1,0:T(8,128)(2,1)S(1)} %get-tuple-element.117.refs_2_), channel_id=1, source_target_pairs={{0,1},{1,0},{2,3},{3,2},{4,5},{5,4},{6,7},{7,6},{8,9},{9,8},{10,11... | collective-permute-start | bytes 2949128 | tf_op jit(solution)/shard_map/zero_pair/ppermute | solution.py:381
  21.1 10.4 %collective-permute-start.8 = (bf16[1,160,1024]{2,1,0:T(8,128)(2,1)S(1)}, bf16[1,160,1024]{2,1,0:T(8,128)(2,1)S(1)}, u32[]{:S(2)}, u32[]{:S(2)}) collective-permute-start(bf16[1,160,1024]{2,1,0:T(8,128)(2,1)S(1)} %get-tuple-element.123), channel_id=1, source_target_pairs={{0,4},{1,3},{2,6},{3,1},{4,0},{5,7},{6,2},{7,5},{8,12},{9,11},{10,... | collective-permute-start | bytes 983048 | tf_op jit(solution)/shard_map/two_near/ppermute | solution.py:381
  21.7 9.8 %collective-permute-start.9 = (bf16[1,160,1024]{2,1,0:T(8,128)(2,1)S(1)}, bf16[1,160,1024]{2,1,0:T(8,128)(2,1)S(1)}, u32[]{:S(2)}, u32[]{:S(2)}) collective-permute-start(bf16[1,160,1024]{2,1,0:T(8,128)(2,1)S(1)} %get-tuple-element.124), channel_id=1, source_target_pairs={{0,2},{1,5},{2,0},{3,7},{4,6},{5,1},{6,4},{7,3},{8,10},{9,13},{10,... | collective-permute-start | bytes 983048 | tf_op jit(solution)/shard_map/two_far/ppermute | solution.py:381
  34.8 12.8 %collective-permute-start.13 = (bf16[1,160,1024]{2,1,0:T(8,128)(2,1)S(1)}, bf16[1,160,1024]{2,1,0:T(8,128)(2,1)S(1)}, u32[]{:S(2)}, u32[]{:S(2)}) collective-permute-start(bf16[1,160,1024]{2,1,0:T(8,128)(2,1)S(1)} %get-tuple-element.135.refs_0_), channel_id=1, source_target_pairs={{0,2},{1,5},{2,0},{3,7},{4,6},{5,1},{6,4},{7,3},{8,10},{9,13},{10,... | collective-permute-start | bytes 983048 | tf_op jit(solution)/shard_map/one_near/ppermute | solution.py:381
  35.5 12.1 %collective-permute-start.14 = (bf16[1,160,1024]{2,1,0:T(8,128)(2,1)S(1)}, bf16[1,160,1024]{2,1,0:T(8,128)(2,1)S(1)}, u32[]{:S(2)}, u32[]{:S(2)}) collective-permute-start(bf16[1,160,1024]{2,1,0:T(8,128)(2,1)S(1)} %get-tuple-element.135.refs_0_), channel_id=1, source_target_pairs={{0,4},{1,3},{2,6},{3,1},{4,0},{5,7},{6,2},{7,5},{8,12},{9,11},{10,... | collective-permute-start | bytes 983048 | tf_op jit(solution)/shard_map/one_across/ppermute | solution.py:381
  37.2 14.9 %collective-permute-start.16 = (bf16[400,640]{1,0:T(8,128)(2,1)S(1)}, bf16[400,640]{1,0:T(8,128)(2,1)S(1)}, u32[]{:S(2)}, u32[]{:S(2)}) collective-permute-start(bf16[400,640]{1,0:T(8,128)(2,1)S(1)} %get-tuple-element.141.refs_0_), channel_id=1, source_target_pairs={{0,8},{24,16},{1,9},{25,17},{2,10},{26,18},{3,11},{27,19},{4,12},{... | collective-permute-start | bytes 1536008 | tf_op jit(solution)/shard_map/one_a_in/ppermute | solution.py:381
  48.1 8.4 %collective-permute-start.18 = (bf16[3,160,1024]{2,1,0:T(8,128)(2,1)S(1)}, bf16[3,160,1024]{2,1,0:T(8,128)(2,1)S(1)}, u32[]{:S(2)}, u32[]{:S(2)}) collective-permute-start(bf16[3,160,1024]{2,1,0:T(8,128)(2,1)S(1)} %get-tuple-element.139.refs_1_), channel_id=1, source_target_pairs={{0,1},{1,0},{2,3},{3,2},{4,5},{5,4},{6,7},{7,6},{8,9},{9,8},{10,11... | collective-permute-start | bytes 2949128 | tf_op jit(solution)/shard_map/one_pair/ppermute | solution.py:381
  48.1 17.6 %collective-permute-start.20 = (bf16[336,640]{1,0:T(8,128)(2,1)S(1)}, bf16[336,640]{1,0:T(8,128)(2,1)S(1)}, u32[]{:S(2)}, u32[]{:S(2)}) collective-permute-start(bf16[336,640]{1,0:T(8,128)(2,1)S(1)} %get-tuple-element.154.refs_0_), channel_id=1, source_target_pairs={{0,8},{24,16},{1,9},{25,17},{2,10},{26,18},{3,11},{27,19},{4,12},{... | collective-permute-start | bytes 1290248 | tf_op jit(solution)/shard_map/one_b_in/ppermute | solution.py:381
  52.2 15.1 %collective-permute-start.17 = (bf16[400,640]{1,0:T(8,128)(2,1)S(1)}, bf16[400,640]{1,0:T(8,128)(2,1)S(1)}, u32[]{:S(2)}, u32[]{:S(2)}) collective-permute-start(bf16[400,640]{1,0:T(8,128)(2,1)S(1)} %get-tuple-element.149.refs_0_), channel_id=1, source_target_pairs={{8,16},{16,8},{9,17},{17,9},{10,18},{18,10},{11,19},{19,11},{12,20... | collective-permute-start | bytes 1536008 | tf_op jit(solution)/shard_map/one_a_middle/ppermute | solution.py:381
  60.2 18.7 %collective-permute-start.24 = (bf16[400,640]{1,0:T(8,128)(2,1)S(1)}, bf16[400,640]{1,0:T(8,128)(2,1)S(1)}, u32[]{:S(2)}, u32[]{:S(2)}) collective-permute-start(bf16[400,640]{1,0:T(8,128)(2,1)S(1)} %get-tuple-element.166.refs_0_), channel_id=1, source_target_pairs={{0,8},{24,16},{1,9},{25,17},{2,10},{26,18},{3,11},{27,19},{4,12},{... | collective-permute-start | bytes 1536008 | tf_op jit(solution)/shard_map/two_a_in/ppermute | solution.py:381
  65.8 14.4 %collective-permute-start.23 = (bf16[336,640]{1,0:T(8,128)(2,1)S(1)}, bf16[336,640]{1,0:T(8,128)(2,1)S(1)}, u32[]{:S(2)}, u32[]{:S(2)}) collective-permute-start(bf16[336,640]{1,0:T(8,128)(2,1)S(1)} %get-tuple-element.165.refs_0_), channel_id=1, source_target_pairs={{8,16},{16,8},{9,17},{17,9},{10,18},{18,10},{11,19},{19,11},{12,20... | collective-permute-start | bytes 1290248 | tf_op jit(solution)/shard_map/one_b_middle/ppermute | solution.py:381
  67.5 20.7 %collective-permute-start.21 = (bf16[400,640]{1,0:T(8,128)(2,1)S(1)}, bf16[400,640]{1,0:T(8,128)(2,1)}, u32[]{:S(2)}, u32[]{:S(2)}) collective-permute-start(bf16[400,640]{1,0:T(8,128)(2,1)S(1)} %get-tuple-element.163.refs_1_), channel_id=1, source_target_pairs={{8,0},{16,24},{9,1},{17,25},{10,2},{18,26},{11,3},{19,27},{12,4},{... | collective-permute-start | bytes 1536008 | tf_op jit(solution)/shard_map/one_a_out/ppermute | solution.py:381
  68.9 17.3 %collective-permute-start.22 = (bf16[336,640]{1,0:T(8,128)(2,1)}, bf16[336,640]{1,0:T(8,128)(2,1)}, u32[]{:S(2)}, u32[]{:S(2)}) collective-permute-start(bf16[336,640]{1,0:T(8,128)(2,1)} %get-tuple-element.164.refs_0_), channel_id=1, source_target_pairs={{0,8},{24,16},{1,9},{25,17},{2,10},{26,18},{3,11},{27,19},{4,12},{... | collective-permute-start | bytes 1290248 | tf_op jit(solution)/shard_map/two_b_in/ppermute | solution.py:381
  79.6 9.9 %collective-permute-start.28 = (bf16[400,640]{1,0:T(8,128)(2,1)S(1)}, bf16[400,640]{1,0:T(8,128)(2,1)S(1)}, u32[]{:S(2)}, u32[]{:S(2)}) collective-permute-start(bf16[400,640]{1,0:T(8,128)(2,1)S(1)} %get-tuple-element.176.refs_0_), channel_id=1, source_target_pairs={{8,16},{16,8},{9,17},{17,9},{10,18},{18,10},{11,19},{19,11},{12,20... | collective-permute-start | bytes 1536008 | tf_op jit(solution)/shard_map/two_a_middle/ppermute | solution.py:381
  80.4 13.1 %collective-permute-start.27 = (bf16[336,640]{1,0:T(8,128)(2,1)S(1)}, bf16[336,640]{1,0:T(8,128)(2,1)}, u32[]{:S(2)}, u32[]{:S(2)}) collective-permute-start(bf16[336,640]{1,0:T(8,128)(2,1)S(1)} %get-tuple-element.175.refs_3_), channel_id=1, source_target_pairs={{8,0},{16,24},{9,1},{17,25},{10,2},{18,26},{11,3},{19,27},{12,4},{... | collective-permute-start | bytes 1290248 | tf_op jit(solution)/shard_map/one_b_out/ppermute | solution.py:381
  87.4 8.5 %collective-permute-start.26 = (bf16[336,640]{1,0:T(8,128)(2,1)S(1)}, bf16[336,640]{1,0:T(8,128)(2,1)S(1)}, u32[]{:S(2)}, u32[]{:S(2)}) collective-permute-start(bf16[336,640]{1,0:T(8,128)(2,1)S(1)} %get-tuple-element.173.refs_0_), channel_id=1, source_target_pairs={{8,16},{16,8},{9,17},{17,9},{10,18},{18,10},{11,19},{19,11},{12,20... | collective-permute-start | bytes 1290248 | tf_op jit(solution)/shard_map/two_b_middle/ppermute | solution.py:381
  89.4 10.7 %collective-permute-start.25 = (bf16[2,160,1024]{2,1,0:T(8,128)(2,1)S(1)}, bf16[2,160,1024]{2,1,0:T(8,128)(2,1)S(1)}, u32[]{:S(2)}, u32[]{:S(2)}) collective-permute-start(bf16[2,160,1024]{2,1,0:T(8,128)(2,1)S(1)} %get-tuple-element.172), channel_id=1, source_target_pairs={{0,4},{1,3},{2,6},{3,1},{4,0},{5,7},{6,2},{7,5},{8,12},{9,11},{10,... | collective-permute-start | bytes 1966088 | tf_op jit(solution)/shard_map/one_near/ppermute | solution.py:381
  89.7 17.8 %collective-permute-start.30 = (bf16[400,640]{1,0:T(8,128)(2,1)S(1)}, bf16[400,640]{1,0:T(8,128)(2,1)S(1)}, u32[]{:S(2)}, u32[]{:S(2)}) collective-permute-start(bf16[400,640]{1,0:T(8,128)(2,1)S(1)} %get-tuple-element.183.refs_1_), channel_id=1, source_target_pairs={{8,0},{16,24},{9,1},{17,25},{10,2},{18,26},{11,3},{19,27},{12,4},{... | collective-permute-start | bytes 1536008 | tf_op jit(solution)/shard_map/two_a_out/ppermute | solution.py:381
  100.2 14.9 %collective-permute-start.33 = (bf16[336,640]{1,0:T(8,128)(2,1)S(1)}, bf16[336,640]{1,0:T(8,128)(2,1)S(1)}, u32[]{:S(2)}, u32[]{:S(2)}) collective-permute-start(bf16[336,640]{1,0:T(8,128)(2,1)S(1)} %get-tuple-element.195.refs_1_), channel_id=1, source_target_pairs={{8,0},{16,24},{9,1},{17,25},{10,2},{18,26},{11,3},{19,27},{12,4},{... | collective-permute-start | bytes 1290248 | tf_op jit(solution)/shard_map/two_b_out/ppermute | solution.py:381
  (24 other events, 87.9 us)
